TPU v7x, 32 devices: a whole 2x2x4 slice. The times are simulated.
32 devices in a mesh: tm: 8 (over z, x), heads: 4 (over y, core).
Axes of the slice: x: 2, y: 2, z: 4, core: 2. Of those that a mesh axis runs over, the one named last changes fastest.
Arguments:
- slab_tokens: bfloat16 [4096, 3584], P('tm', 'heads'), may hold values from -14 to 14
- memory: bfloat16 [4096, 3584], P('tm', 'heads'), may hold values from -14 to 14
- query_weight: bfloat16 [3584, 3584], P(None, 'heads'), may hold values from -0.09375 to 0.09375
- key_weight: bfloat16 [3584, 512], P(None, 'heads'), may hold values from -0.09375 to 0.09375
- value_weight: bfloat16 [3584, 512], P(None, 'heads'), may hold values from -0.09375 to 0.09375
- query_down: bfloat16 [16, 3584], replicated, may hold values from -0.09375 to 0.09375
- query_up: bfloat16 [16, 3584], P(None, 'heads'), may hold values from -1.5 to 1.5
- value_down: bfloat16 [16, 3584], replicated, may hold values from -0.09375 to 0.09375
- value_up: bfloat16 [16, 512], P(None, 'heads'), may hold values from -1.5 to 1.5
- tag_weight: bfloat16 [3584, 8], P('heads'), may hold values from -0.75 to 0.75
- retrieval: int32 [32, 8], P('tm'), may hold values from 0 to 31, as said below
- boundary: int32 [32], P('tm'), may hold values from 0 to 127
- grad_tags: float32 [4096, 8], P('tm'), may hold values from -0.375 to 0.375
Outputs:
- tag_logits: float32 [4096, 8], P('tm')
- query_down_grad: float32 [16, 3584], P(None, 'heads')
- query_up_grad: float32 [16, 3584], P(None, 'heads')
- value_down_grad: float32 [16, 3584], P(None, 'heads')
- value_up_grad: float32 [16, 512], P(None, 'heads')
Inputs may be any that keep to these rules, and one draw needn't show every extreme that they name: `retrieval`: each row names 8 different memory blocks; the rows of one index of tm name at most 1 different blocks held by any one index of tm.
All inputs are finite; a program needn't handle non-finite values.
Results may differ from a plain program's by a relative error of at most 0.035.
The roundings to bfloat16 on the way count: a program that leaves them out, or rounds other values in their place, can miss the bound.
Values may be sent and summed in bfloat16 or wider, within the bound.
No kernel may reach another device: no remote copies, remote signals or barrier semaphores. Data moves between devices by JAX's collectives and lax.ppermute only.
A program may use at most 128 MiB of HBM per device.

v0:
```python
import jax
import jax.numpy as jnp
from jax import lax
from jax.sharding import PartitionSpec as P

HD = 128
RANK = 16
TOP = 8
BLK = 128
CAP = 1


HIGHEST = lax.Precision.HIGHEST


def attend(query, all_keys, all_values, split_row, out_grad):
    span_count, row_count, query_width = query.shape
    key_count, kv_width = (all_keys.shape[1], all_keys.shape[2])
    kv_heads = kv_width // HD
    group_size = query_width // kv_width
    score_scale = HD ** (-0.5)
    query_heads = query.reshape(span_count, row_count, kv_heads, group_size, HD)
    key_heads = all_keys.reshape(span_count, key_count, kv_heads, HD)
    value_heads = all_values.reshape(span_count, key_count, kv_heads, HD)
    grad_heads = out_grad.reshape(span_count, row_count, kv_heads, group_size, HD)
    scores = (
        jnp.einsum("crngd,cknd->cngrk", query_heads, key_heads, preferred_element_type=jnp.float32)
        * score_scale
    )
    row_ids = jnp.arange(row_count, dtype=jnp.int32)[:, None]
    col_ids = jnp.arange(BLK, dtype=jnp.int32)[None, :]
    edge_at = split_row[:, None, None]
    local_seen = (col_ids <= row_ids) & ((col_ids >= edge_at) | (row_ids < edge_at))
    visible = jnp.concatenate(
        [jnp.ones((span_count, row_count, key_count - BLK), jnp.bool_), local_seen], axis=2
    )
    scores = jnp.where(visible[:, None, None], scores, -jnp.inf)
    row_max = jnp.max(scores, axis=-1, keepdims=True)
    weights = jnp.exp(scores - row_max)
    probs = weights / jnp.sum(weights, axis=-1, keepdims=True)
    probs_low = probs.astype(jnp.bfloat16)
    attended = jnp.einsum(
        "cngrk,cknd->crngd", probs_low, value_heads, preferred_element_type=jnp.float32
    ).astype(jnp.bfloat16)
    prob_grad = jnp.einsum(
        "crngd,cknd->cngrk", grad_heads, value_heads, preferred_element_type=jnp.float32
    )
    row_dot = jnp.sum(grad_heads.astype(jnp.float32) * attended.astype(jnp.float32), axis=-1)
    row_dot = jnp.transpose(row_dot, (0, 2, 3, 1))[..., None]
    score_grad = (probs * (prob_grad - row_dot) * score_scale).astype(jnp.bfloat16)
    query_grad = jnp.einsum(
        "cngrk,cknd->crngd", score_grad, key_heads, preferred_element_type=jnp.float32
    ).astype(jnp.bfloat16)
    value_grad = jnp.einsum(
        "cngrk,crngd->cknd", probs_low, grad_heads, preferred_element_type=jnp.float32
    )
    return (
        attended.reshape(span_count, row_count, query_width),
        query_grad.reshape(span_count, row_count, query_width),
        value_grad.reshape(span_count, key_count, kv_width),
    )


def choose_slots(needed, places):
    slot_ids = jnp.arange(CAP, dtype=jnp.int32)
    return needed[:, None, :] * (places[:, None, :] == slot_ids[None, :, None]).astype(jnp.int32)


def local(
    slab_tokens,
    memory,
    query_weight,
    key_weight,
    value_weight,
    query_down,
    query_up,
    value_down,
    value_up,
    tag_weight,
    retrieval,
    boundary,
    grad_tags,
):
    tok_rows = slab_tokens.shape[0]
    mem_rows = memory.shape[0]
    query_width = query_weight.shape[1]
    kv_width = key_weight.shape[1]
    span_count = tok_rows // BLK
    block_count = mem_rows // BLK
    pair_weight = jnp.concatenate([key_weight, value_weight], 1)
    adapter_pair = jnp.concatenate([query_down, value_down], 0)
    contract_last = (((1,), (1,)), ((), ()))
    contract_first = (((0,), (0,)), ((), ()))
    token_piece = lax.all_gather(slab_tokens, "heads", axis=1, tiled=True)
    memory_piece = lax.all_gather(memory, "heads", axis=1, tiled=True)
    query_acc = jnp.dot(token_piece, query_weight, preferred_element_type=jnp.float32)
    pair_acc = jnp.dot(token_piece, pair_weight, preferred_element_type=jnp.float32)
    low_acc = lax.dot_general(
        token_piece, adapter_pair, contract_last, preferred_element_type=jnp.float32
    )
    memory_acc = jnp.dot(memory_piece, pair_weight, preferred_element_type=jnp.float32)
    memory_low_acc = lax.dot_general(
        memory_piece, adapter_pair[RANK:], contract_last, preferred_element_type=jnp.float32
    )
    query_acc, pair_acc, low_acc, memory_acc, memory_low_acc = (
        query_acc,
        pair_acc,
        low_acc,
        memory_acc,
        memory_low_acc,
    )
    low_tokens = low_acc.astype(jnp.bfloat16)
    low_query = low_tokens[:, :RANK]
    low_value = low_tokens[:, RANK:]
    queries = (query_acc + jnp.dot(low_query, query_up, preferred_element_type=jnp.float32)).astype(
        jnp.bfloat16
    )
    keys_local = pair_acc[:, :kv_width].astype(jnp.bfloat16)
    values_local = (
        pair_acc[:, kv_width:] + jnp.dot(low_value, value_up, preferred_element_type=jnp.float32)
    ).astype(jnp.bfloat16)
    memory_low = memory_low_acc.astype(jnp.bfloat16)
    memory_pair = (
        jnp.concatenate(
            [
                memory_acc[:, :kv_width],
                memory_acc[:, kv_width:]
                + jnp.dot(memory_low, value_up, preferred_element_type=jnp.float32),
            ],
            1,
        )
        .astype(jnp.bfloat16)
        .reshape(block_count, BLK, 2 * kv_width)
    )
    peer_count = lax.axis_size("tm")
    every_block = jnp.arange(peer_count * block_count, dtype=jnp.int32)
    wanted = (
        jnp.any(retrieval.reshape(-1, 1) == every_block[None, :], axis=0)
        .astype(jnp.int32)
        .reshape(peer_count, block_count)
    )
    places = jnp.cumsum(wanted, axis=1) - wanted
    requested = choose_slots(wanted, places)
    asked_for = lax.all_to_all(requested, "tm", split_axis=0, concat_axis=0, tiled=True)
    rows_needed = retrieval // block_count * CAP + jnp.take(places.reshape(-1), retrieval)
    asked_low = asked_for.astype(jnp.bfloat16)
    outgoing = jnp.einsum(
        "rcm,mbw->rcbw", asked_low, memory_pair, preferred_element_type=jnp.float32
    ).astype(jnp.bfloat16)
    fetched = lax.all_to_all(outgoing, "tm", split_axis=0, concat_axis=0, tiled=True)
    slot_rows = fetched.reshape(peer_count * CAP, BLK, 2 * kv_width)
    picked = jnp.take(slot_rows, rows_needed.reshape(-1), axis=0).reshape(
        span_count, TOP * BLK, 2 * kv_width
    )
    all_keys = jnp.concatenate(
        [picked[..., :kv_width], keys_local.reshape(span_count, BLK, kv_width)], 1
    )
    all_values = jnp.concatenate(
        [picked[..., kv_width:], values_local.reshape(span_count, BLK, kv_width)], 1
    )
    attended_grad = lax.dot_general(
        grad_tags, tag_weight.astype(jnp.float32), contract_last, precision=HIGHEST
    ).astype(jnp.bfloat16)
    attended, query_grad, value_grad = attend(
        queries.reshape(span_count, BLK, query_width),
        all_keys,
        all_values,
        boundary,
        attended_grad.reshape(span_count, BLK, query_width),
    )
    attended = attended.reshape(tok_rows, query_width)
    query_grad = query_grad.reshape(tok_rows, query_width)
    logits_out = lax.psum(
        jnp.dot(attended, tag_weight, preferred_element_type=jnp.float32), "heads"
    )
    local_grad = value_grad[:, TOP * BLK :].reshape(tok_rows, kv_width)
    slot_grads = value_grad[:, : TOP * BLK].reshape(span_count * TOP, BLK * kv_width)
    slot_hits = (
        rows_needed.reshape(-1, 1) == jnp.arange(peer_count * CAP, dtype=jnp.int32)[None, :]
    ).astype(jnp.float32)
    grad_buffer = lax.dot_general(slot_hits, slot_grads, contract_first, precision=HIGHEST).reshape(
        peer_count * CAP, BLK, kv_width
    )
    up_wide = value_up.astype(jnp.float32)
    returned = lax.all_to_all(
        grad_buffer.reshape(peer_count, CAP, BLK, kv_width),
        "tm",
        split_axis=0,
        concat_axis=0,
        tiled=True,
    )
    owned_grad = jnp.einsum(
        "rcm,rcbw->mbw", asked_for.astype(jnp.float32), returned, precision=HIGHEST
    ).reshape(mem_rows, kv_width)
    memory_cot = lax.dot_general(up_wide, owned_grad, contract_last, precision=HIGHEST)
    up_memory = lax.dot_general(
        memory_low.astype(jnp.float32), owned_grad, contract_first, precision=HIGHEST
    )
    query_cot = lax.dot_general(
        query_up, query_grad, contract_last, preferred_element_type=jnp.float32
    )
    value_cot = lax.dot_general(up_wide, local_grad, contract_last, precision=HIGHEST)
    query_cot, value_cot, memory_cot = lax.psum((query_cot, value_cot, memory_cot), "heads")
    query_down_grad = jnp.dot(
        query_cot.astype(jnp.bfloat16), slab_tokens, preferred_element_type=jnp.float32
    )
    value_down_grad = jnp.dot(
        value_cot.astype(jnp.bfloat16), slab_tokens, preferred_element_type=jnp.float32
    ) + jnp.dot(memory_cot.astype(jnp.bfloat16), memory, preferred_element_type=jnp.float32)
    query_up_grad = lax.dot_general(
        low_query, query_grad, contract_first, preferred_element_type=jnp.float32
    )
    value_up_grad = (
        lax.dot_general(
            low_value.astype(jnp.float32), local_grad, contract_first, precision=HIGHEST
        )
        + up_memory
    )
    query_down_grad, query_up_grad, value_down_grad, value_up_grad = lax.psum(
        (query_down_grad, query_up_grad, value_down_grad, value_up_grad), "tm"
    )
    return (logits_out, query_down_grad, query_up_grad, value_down_grad, value_up_grad)


def solution(mesh):
    in_specs = (
        P("tm", "heads"),
        P("tm", "heads"),
        P(None, "heads"),
        P(None, "heads"),
        P(None, "heads"),
        P(),
        P(None, "heads"),
        P(),
        P(None, "heads"),
        P("heads", None),
        P("tm", None),
        P("tm"),
        P("tm", None),
    )
    out_specs = (
        P("tm", None),
        P(None, "heads"),
        P(None, "heads"),
        P(None, "heads"),
        P(None, "heads"),
    )
    return jax.shard_map(local, mesh=mesh, in_specs=in_specs, out_specs=out_specs, check_vma=False)
```

profile of v0, /device:TPU:0, one launch (start us, length us, event | category | flops | bytes accessed | tf_op | source)
XLA Modules:
  0.0 273.4 jit_solution(1586620854201250273)
XLA Ops:
  7.3 0.7 all-gather.3.cloned.1.call-update
  8.0 0.7 all-gather.5.cloned.1.call-update
  8.7 0.8 eq.42
  10.1 0.7 copy.132
  10.7 7.3 %all-to-all-start = ((s32[8,1,4]{2,1,0:T(1,128)}), s32[8,1,4]{2,1,0:T(1,128)S(1)}, u32[]{:S(2)}, u32[]{:S(2)}) async-start(s32[8,1,4]{2,1,0:T(1,128)} %copy.132), calls=%async_computation | async-start | bytes 8192 | tf_op jit(solution)/shard_map/all_to_all | solution.py:144
  18.1 0.7 add_select_fusion
  18.9 0.7 gather_fusion
  19.9 0.9 convolution_convert_fusion
  20.8 2.0 reshape.313
  22.8 1.0 reshape.314
  24.1 2.2 constant_dynamic-update-slice_fusion.1
  26.3 2.3 constant_dynamic-update-slice_fusion
  28.6 1.4 copy.153
  30.0 1.7 copy.149
  32.0 11.9 %all-gather.3.cloned.1.call-done = bf16[512,3584]{1,0:T(8,128)(2,1)} async-done(((bf16[512,896]{1,0:T(8,128)(2,1)}), bf16[512,3584]{1,0:T(8,128)(2,1)}) %all-gather.3.cloned.1.call-update) | async-done | bytes 3670032 | tf_op jit(solution)/shard_map/all_gather | solution.py:95
  43.8 3.8 %convolution_bitcast_fusion.1 = f32[512,256]{0,1:T(8,128)S(1)} fusion(bf16[3584,256]{1,0:T(8,128)(2,1)} %constant_dynamic-update-slice_fusion, bf16[512,3584]{1,0:T(8,128)(2,1)} %all-gather.3.cloned.1.call-done), kind=kOutput, calls=%fused_computation.35 | convolution fusion | flops 939524096 | bytes 6029312 | tf_op jit(solution)/shard_map/dot_general | solution.py:101
  47.9 3.1 %convolution_convert_fusion.3 = bf16[512,16]{0,1:T(8,128)(2,1)S(1)} fusion(bf16[512,3584]{1,0:T(8,128)(2,1)} %all-gather.3.cloned.1.call-done, bf16[16,3584]{1,0:T(8,128)(2,1)S(1)} %copy-done.10), kind=kOutput, calls=%fused_computation.48 | convolution fusion | flops 58728448 | bytes 3801088 | tf_op jit(solution)/shard_map/dot_general | solution.py:102
  51.0 0.2 fusion.31
  51.4 0.4 fusion.27
  51.8 0.9 copy.137
  52.7 5.5 %all-to-all-start.1 = ((bf16[8,1,128,256]{3,2,1,0:T(8,128)(2,1)}), bf16[8,1,128,256]{3,2,1,0:T(8,128)(2,1)S(1)}, u32[]{:S(2)}, u32[]{:S(2)}) async-start(bf16[8,1,128,256]{3,2,1,0:T(8,128)(2,1)} %copy.137), calls=%async_computation.1 | async-start | bytes 1048576 | tf_op jit(solution)/shard_map/all_to_all | solution.py:150
  58.2 18.7 %all-gather.5.cloned.1.call-done = bf16[512,3584]{1,0:T(8,128)(2,1)} async-done(((bf16[512,896]{1,0:T(8,128)(2,1)}), bf16[512,3584]{1,0:T(8,128)(2,1)}) %all-gather.5.cloned.1.call-update) | async-done | bytes 3670032 | tf_op jit(solution)/shard_map/all_gather | solution.py:94
  76.9 3.3 %fusion.33 = bf16[512,32]{0,1:T(8,128)(2,1)S(1)} fusion(bf16[512,3584]{1,0:T(8,128)(2,1)} %all-gather.5.cloned.1.call-done, bf16[16,3584]{1,0:T(8,128)(2,1)S(1)} %copy-done.10, bf16[16,3584]{1,0:T(8,128)(2,1)S(1)} %copy-done.13), kind=kOutput, calls=%fused_computation.44 | convolution fusion | flops 117915648 | bytes 3932160 | tf_op jit(solution)/shard_map/dot_general | solution.py:98
  80.3 7.6 %fusion.88 = f32[512,896]{1,0:T(8,128)S(1)} fusion(bf16[512,3584]{1,0:T(8,128)(2,1)S(1)} %copy-done.5, bf16[3584,896]{1,0:T(8,128)(2,1)} %param.15), kind=kOutput, calls=%fused_computation.124 | convolution fusion | flops 3288334336 | bytes 11927552 | tf_op jit(solution)/shard_map/dot_general | solution.py:96
  87.9 0.4 add_convert_fusion
  88.4 2.0 reshape.312
  90.4 3.8 %convolution_bitcast_fusion = f32[512,256]{0,1:T(8,128)S(1)} fusion(bf16[3584,256]{1,0:T(8,128)(2,1)} %constant_dynamic-update-slice_fusion, bf16[512,3584]{1,0:T(8,128)(2,1)} %all-gather.5.cloned.1.call-done), kind=kOutput, calls=%fused_computation.34 | convolution fusion | flops 939524096 | bytes 6029312 | tf_op jit(solution)/shard_map/dot_general | solution.py:97
  94.2 0.2 fusion.32
  94.5 0.8 copy.175
  95.3 0.7 gather_fusion.1
  96.0 1.1 bitcast_select_fusion.1
  97.0 1.3 fusion.87
  98.4 7.0 %fusion.3 = (f32[4,7,128]{2,1,0:T(8,128)S(1)}, f32[4,1152,128,7]{2,1,3,0:T(8,128)}) fusion(pred[4,128,1152]{1,2,0:T(8,128)(4,1)S(1)} %concatenate.30, bf16[4,128,7,128]{3,2,1,0:T(8,128)(2,1)S(1)} %copy-done.7, bf16[4,128,128]{2,1,0:T(8,128)(2,1)S(1)} %bitcast.237, bf16[4,1024,128]{2,1,0:T(8,128)(2,1)S(1)} %get-tuple-element.15), kind=kOutput, calls=%fused_computation.9 | convolution fusion | flops 1071706624 | bytes 19216384 | tf_op jit(solution)/shard_map/crngd,cknd->cngrk/dot_general | solution.py:27
  105.3 8.8 %fusion.5 = f32[4,7,128]{2,1,0:T(8,128)S(1)} fusion(f32[4,1152,128,7]{2,1,3,0:T(8,128)} %get-tuple-element.20, f32[4,7,128]{2,1,0:T(8,128)S(1)} %get-tuple-element.19, pred[4,128,1152]{1,2,0:T(8,128)(4,1)S(1)} %concatenate.30), kind=kLoop, calls=%fused_computation.11 | loop fusion | flops 12382720 | bytes 17133568 | tf_op jit(solution)/shard_map/reduce_sum | solution.py:40
  114.1 8.6 %fusion.12 = f32[4,1152,128]{1,2,0:T(8,128)S(1)} fusion(bf16[4,128,7,128]{1,3,2,0:T(8,128)(2,1)} %copy.153, f32[4,7,128]{2,1,0:T(8,128)S(1)} %fusion.5, f32[4,7,128]{2,1,0:T(8,128)S(1)} %get-tuple-element.19, f32[4,1152,128,7]{2,1,3,0:T(8,128)} %get-tuple-element.20, pred[4,128,1152]{1,2,0:T(8,128)(4,1)S(1)} %concatenate.30), kind=kOutput, calls=%fused_computation.18 | convolution fusion | flops 1073479680 | bytes 20410368 | tf_op jit(solution)/shard_map/cngrk,crngd->cknd/dot_general | solution.py:54
  122.8 2.3 copy-done.6
  125.1 0.3 copy-done.9
  125.4 9.3 %multiply_reduce_fusion = (f32[4,128,7]{1,2,0:T(8,128)S(1)}, bf16[4,128,1,7,128]{1,4,3,0,2:T(8,128)(2,1)}) fusion(f32[4,128,1,7,128]{1,4,3,0,2:T(8,128)S(1)} %copy-done.6, f32[4,7,128]{2,1,0:T(8,128)S(1)} %fusion.5, f32[4,7,128]{2,1,0:T(8,128)S(1)} %get-tuple-element.19, f32[4,1152,128,7]{2,1,3,0:T(8,128)} %get-tuple-element.20, ...), kind=kOutput, calls=%fused_computation.24 | convolution fusion | flops 1077670400 | bytes 21080064 | tf_op jit(solution)/shard_map/cngrk,cknd->crngd/dot_general | solution.py:42
  134.6 11.1 %fusion.23 = bf16[4,128,1,7,128]{1,4,3,0,2:T(8,128)(2,1)} fusion(bf16[4,128,7,128]{1,3,2,0:T(8,128)(2,1)} %copy.153, f32[4,7,128]{2,1,0:T(8,128)S(1)} %bitcast.240, f32[4,7,128]{2,1,0:T(8,128)S(1)} %fusion.5, f32[4,7,128]{2,1,0:T(8,128)S(1)} %get-tuple-element.19, f32[4,1152,128,7]{2,1,3,0:T(8,128)} %get-tuple-element.20, ...), kind=kOutput, calls=%fused_computation.29 | convolution fusion | flops 2148007936 | bytes 21342208 | tf_op jit(solution)/shard_map/cngrk,cknd->crngd/dot_general | solution.py:51
  145.8 2.0 copy.152
  147.8 0.2 convolution_bitcast_fusion.2
  148.0 1.8 copy.157
  149.9 1.8 reshape.279
  151.7 0.8 fusion.28
  152.5 0.9 copy.159
  153.5 5.7 %all-to-all-start.2 = ((f32[8,1,128,128]{3,2,1,0:T(8,128)}), f32[8,1,128,128]{3,2,1,0:T(8,128)}, u32[]{:S(2)}, u32[]{:S(2)}) async-start(f32[8,1,128,128]{3,2,1,0:T(8,128)} %copy.159), calls=%async_computation.2 | async-start | bytes 1048576 | tf_op jit(solution)/shard_map/all_to_all | solution.py:185
  159.2 0.3 all-reduce.6.cloned.1.call-start
  159.5 0.2 convolution_bitcast_fusion.4
  159.7 2.0 copy.145
  161.9 0.2 fusion.37
  162.2 1.0 fusion.34
  163.2 11.0 %all-to-all-done.2 = f32[8,1,128,128]{3,2,1,0:T(8,128)} async-done(((f32[8,1,128,128]{3,2,1,0:T(8,128)}), f32[8,1,128,128]{3,2,1,0:T(8,128)}, u32[]{:S(2)}, u32[]{:S(2)}) %all-to-all-start.2) | async-done | bytes 524320 | tf_op jit(solution)/shard_map/all_to_all | solution.py:185
  174.2 1.8 fusion.43
  176.1 0.2 convolution_bitcast_fusion.3
  176.3 0.8 convolution_add_fusion.3
  177.1 12.3 %all-reduce.7 = (f32[512,8]{0,1:T(8,128)}, bf16[16,512]{1,0:T(8,128)(2,1)S(1)}, bf16[16,512]{1,0:T(8,128)(2,1)S(1)}, bf16[16,512]{1,0:T(8,128)(2,1)S(1)}) all-reduce(f32[512,8]{0,1:T(8,128)S(1)} %fusion.37, f32[16,512]{1,0:T(8,128)S(1)} %convolution_bitcast_fusion.2, ...), channel_id=1, replica_groups=mesh['tm'=8,'heads'=4] {'heads'}, use_global_device_ids=true, to_apply=%region_4.5 | all-reduce | flops 28672 | bytes 180224 | tf_op jit(solution)/shard_map/psum | solution.py:173
  189.5 0.9 fusion.90
  190.3 0.2 fusion.89
  190.6 0.9 convolution_add_fusion.2
  191.5 69.7 %all-reduce.6.cloned.1.call-done = (f32[16,896]{1,0:T(8,128)}, f32[16,896]{1,0:T(8,128)}, f32[16,896]{1,0:T(8,128)}, f32[16,128]{1,0:T(8,128)}) async-done(((f32[16,896]{1,0:T(8,128)}, f32[16,896]{1,0:T(8,128)}, f32[16,896]{1,0:T(8,128)}, f32[16,128]{1,0:T(8,128)}), (f32[16,896]{1,0:T(8,128)}, f32[16,896]{1,0:T(8,128)}, f32[16,896]{1,0:T(8,128)}, f32[16,128]{1,0:T(8,128)})) %all-reduce.6.cloned.1.call-update) | async-done | bytes 180240 | tf_op jit(solution)/shard_map/psum | solution.py:219
  261.2 1.4 copy.229
  262.6 1.4 copy.230
  264.1 1.4 copy.231
  265.5 1.3 copy.232
  (80 shorter events, 2.7 us)
Async XLA Ops:
  7.2 80.8 %copy-start = (bf16[16,896]{1,0:T(8,128)(2,1)S(1)}, bf16[16,896]{1,0:T(8,128)(2,1)}, u32[]{:S(2)}) copy-start(bf16[16,896]{1,0:T(8,128)(2,1)} %param.19) | copy-start | bytes 86020
  7.2 12.5 %copy-start.15 = (s32[4,8]{1,0:T(4,128)S(1)}, s32[4,8]{1,0:T(4,128)}, u32[]{:S(2)}) copy-start(s32[4,8]{1,0:T(4,128)} %param.23) | copy-start | bytes 388
  7.2 12.7 %copy-start.17 = (bf16[896,8]{0,1:T(8,128)(2,1)S(1)}, bf16[896,8]{0,1:T(8,128)(2,1)}, u32[]{:S(2)}) copy-start(bf16[896,8]{0,1:T(8,128)(2,1)} %param.22) | copy-start | bytes 43012
  7.2 12.6 %copy-start.16 = (f32[512,8]{0,1:T(8,128)S(1)}, f32[512,8]{0,1:T(8,128)}, u32[]{:S(2)}) copy-start(f32[512,8]{0,1:T(8,128)} %param.25) | copy-start | bytes 49156
  7.2 36.6 %all-gather.3.cloned.1.call-start = ((), (), s32[]{:S(2)}) async-start(), calls=%async_computation.3 | async-start | bytes 4587520 | tf_op jit(solution)/shard_map/all_gather | solution.py:95
  8.0 69.0 %all-gather.5.cloned.1.call-start = ((), (), s32[]{:S(2)}) async-start(), calls=%async_computation.4 | async-start | bytes 4587520 | tf_op jit(solution)/shard_map/all_gather | solution.py:94
  10.7 21.2 %all-to-all-start = ((s32[8,1,4]{2,1,0:T(1,128)}), s32[8,1,4]{2,1,0:T(1,128)S(1)}, u32[]{:S(2)}, u32[]{:S(2)}) async-start(s32[8,1,4]{2,1,0:T(1,128)} %copy.132), calls=%async_computation | async-start | bytes 8192 | tf_op jit(solution)/shard_map/all_to_all | solution.py:144
  18.9 5.0 %copy-start.18 = (s32[4]{0:T(128)S(1)}, s32[4]{0:T(128)}, u32[]{:S(2)}) copy-start(s32[4]{0:T(128)} %param.24) | copy-start | bytes 52
  23.7 4.9 %copy-start.3 = (bf16[4,128,7,128]{3,2,1,0:T(8,128)(2,1)S(1)}, bf16[4,128,7,128]{3,2,1,0:T(8,128)(2,1)}, u32[]{:S(2)}) copy-start(bf16[4,128,7,128]{3,2,1,0:T(8,128)(2,1)} %reshape.313) | copy-start | bytes 2752516
  32.0 15.8 %copy-start.10 = (bf16[16,3584]{1,0:T(8,128)(2,1)S(1)}, bf16[16,3584]{1,0:T(8,128)(2,1)}, u32[]{:S(2)}) copy-start(bf16[16,3584]{1,0:T(8,128)(2,1)} %param.20) | copy-start | bytes 344068
  47.6 3.4 %copy-start.14 = (bf16[16,128]{1,0:T(8,128)(2,1)S(1)}, bf16[16,128]{1,0:T(8,128)(2,1)}, u32[]{:S(2)}) copy-start(bf16[16,128]{1,0:T(8,128)(2,1)} %param.21) | copy-start | bytes 12292
  47.8 29.1 %copy-start.13 = (bf16[16,3584]{1,0:T(8,128)(2,1)S(1)}, bf16[16,3584]{1,0:T(8,128)(2,1)}, u32[]{:S(2)}) copy-start(bf16[16,3584]{1,0:T(8,128)(2,1)} %param.18) | copy-start | bytes 344068
  52.7 42.6 %all-to-all-start.1 = ((bf16[8,1,128,256]{3,2,1,0:T(8,128)(2,1)}), bf16[8,1,128,256]{3,2,1,0:T(8,128)(2,1)S(1)}, u32[]{:S(2)}, u32[]{:S(2)}) async-start(bf16[8,1,128,256]{3,2,1,0:T(8,128)(2,1)} %copy.137), calls=%async_computation.1 | async-start | bytes 1048576 | tf_op jit(solution)/shard_map/all_to_all | solution.py:150
  76.9 3.4 %copy-start.5 = (bf16[512,3584]{1,0:T(8,128)(2,1)S(1)}, bf16[512,3584]{1,0:T(8,128)(2,1)}, u32[]{:S(2)}) copy-start(bf16[512,3584]{1,0:T(8,128)(2,1)} %all-gather.5.cloned.1.call-done) | copy-start | bytes 11010052
  96.0 2.4 copy-start.7
  96.0 2.4 copy-start.11
  98.4 7.0 %copy-start.8 = (bf16[4,1024,128]{2,1,0:T(8,128)(2,1)}, bf16[4,1024,128]{2,1,0:T(8,128)(2,1)S(1)}, u32[]{:S(2)}) copy-start(bf16[4,1024,128]{2,1,0:T(8,128)(2,1)S(1)} %get-tuple-element.15) | copy-start | bytes 3145732
  122.7 11.9 %copy-start.1 = (f32[4,1152,128]{1,2,0:T(8,128)}, f32[4,1152,128]{1,2,0:T(8,128)S(1)}, u32[]{:S(2)}) copy-start(f32[4,1152,128]{1,2,0:T(8,128)S(1)} %fusion.12) | copy-start | bytes 7077892
  122.8 2.4 copy-start.6
  122.8 2.6 copy-start.9
  125.4 9.3 %copy-start.12 = (bf16[512,128]{1,0:T(8,128)(2,1)S(1)}, bf16[512,128]{1,0:T(8,128)(2,1)}, u32[]{:S(2)}) copy-start(bf16[512,128]{1,0:T(8,128)(2,1)} %copy.175) | copy-start | bytes 393220
  145.8 2.3 slice-start.1
  149.9 3.5 %slice-start = ((f32[4,1152,128]{1,2,0:T(8,128)}), f32[4,128,128]{1,2,0:T(8,128)S(1)}, s32[]{:S(2)}) async-start(f32[4,1152,128]{1,2,0:T(8,128)} %copy-done.1), calls=%async_computation.6 | async-start | bytes 524288 | tf_op jit(solution)/shard_map/slice | solution.py:176
  153.5 35.9 %copy-start.2 = (bf16[512,896]{1,0:T(8,128)(2,1)S(1)}, bf16[512,896]{1,0:T(8,128)(2,1)}, u32[]{:S(2)}) copy-start(bf16[512,896]{1,0:T(8,128)(2,1)} %param.13) | copy-start | bytes 2752516
  153.5 20.7 %all-to-all-start.2 = ((f32[8,1,128,128]{3,2,1,0:T(8,128)}), f32[8,1,128,128]{3,2,1,0:T(8,128)}, u32[]{:S(2)}, u32[]{:S(2)}) async-start(f32[8,1,128,128]{3,2,1,0:T(8,128)} %copy.159), calls=%async_computation.2 | async-start | bytes 1048576 | tf_op jit(solution)/shard_map/all_to_all | solution.py:185
  159.2 102.0 %all-reduce.6.cloned.1.call-start = ((), (), s32[]{:S(2)}) async-start(), calls=%async_computation.5 | async-start | bytes 360448 | tf_op jit(solution)/shard_map/psum | solution.py:219
  159.7 30.8 %copy-start.4 = (bf16[512,896]{1,0:T(8,128)(2,1)S(1)}, bf16[512,896]{1,0:T(8,128)(2,1)}, u32[]{:S(2)}) copy-start(bf16[512,896]{1,0:T(8,128)(2,1)} %param.14) | copy-start | bytes 2752516
Sparse Core Ops, SparseCore 0:
  9.6 34.1 all-gather.2
  45.4 31.4 all-gather.4
  191.6 69.5 all-reduce.5
where the time goes:
time: 274 us; the launch traced here: 273 us
  waiting for transfers between devices  113 us (41%)
  matrix products  67.4 us (25%)
  local copies, waits for them, and re-layouts  37 us (14%)
  starting transfers between devices  18.8 us (7%)
  between operations  14.2 us (5%)
  blocking collectives  12.3 us (4%)
  other arithmetic  11 us (4%)
    psum x1, waiting for transfers between devices, local(): lax.psum((query_down_grad, query_up_grad, value_down_grad, value_up_grad)...  69.7 us
    all_gather x1, waiting for transfers between devices, local(): token_piece = lax.all_gather(slab_tokens, 'heads', axis=1, tiled=True)  18.7 us
    psum x1, blocking collectives, local(): lax.psum(jnp.dot(attended, tag_weight, preferred_element_type=jnp.float32...  12.3 us
    all_gather x1, waiting for transfers between devices, local(): memory_piece = lax.all_gather(memory, 'heads', axis=1, tiled=True)  11.9 us
    dot_general x1, matrix products, attend(): jnp.einsum('cngrk,cknd->crngd', score_grad, key_heads, preferred_element_...  11.1 us
    all_to_all x1, waiting for transfers between devices, local(): lax.all_to_all(grad_buffer.reshape(peer_count, CAP, BLK, kv_width), 'tm',...  11 us
    unnamed x45, local copies, waits for them, and re-layouts  10.6 us
    dot_general x1, matrix products, attend(): jnp.einsum('cngrk,cknd->crngd', probs_low, value_heads, preferred_element...  9.25 us
  transfers between devices with their start and end apart: 6, of which 4 were waited for; matrix products, arithmetic and copies ran while one was open for 17% of the time, Pallas kernels for 0%

commit v1 on v0

--- a/solution.py
+++ b/solution.py
@@ -1,6 +1,8 @@
 import jax
 import jax.numpy as jnp
 from jax import lax
+from jax.experimental import pallas as pl
+from jax.experimental.pallas import tpu as pltpu
 from jax.sharding import PartitionSpec as P
 
 HD = 128
@@ -66,7 +68,7 @@
     return needed[:, None, :] * (places[:, None, :] == slot_ids[None, :, None]).astype(jnp.int32)
 
 
-def local(
+def general(
     slab_tokens,
     memory,
     query_weight,
@@ -222,6 +224,306 @@
     return (logits_out, query_down_grad, query_up_grad, value_down_grad, value_up_grad)
 
 
+LOG2E = 1.4426950408889634
+NT = (((1,), (1,)), ((), ()))
+PACK = 2 * BLK + RANK
+VMEM_BYTES = 56 * 1024 * 1024
+
+
+def dot_nt(a, b, precision=None):
+    return lax.dot_general(a, b, NT, precision=precision, preferred_element_type=jnp.float32)
+
+
+def dot_nn(a, b, precision=None):
+    return jnp.dot(a, b, precision=precision, preferred_element_type=jnp.float32)
+
+
+def memory_kernel(pieces, readers, place_ref, asked_ref, *refs):
+    tokens = refs[: 4 * pieces]
+    wk_ref, wv_ref, down_ref, up_ref, out_ref, pair_ref = refs[4 * pieces :]
+    width = tokens[0].shape[1]
+    rows = tokens[0].shape[0]
+    for part in range(pieces):
+        acc = None
+        low = None
+        for j in range(4):
+            start = pl.multiple_of(lax.bitwise_xor(place_ref[0], j) * width, width)
+            x = tokens[4 * part + j][...]
+            w = jnp.concatenate([wk_ref[pl.ds(start, width), :], wv_ref[pl.ds(start, width), :]], 1)
+            term = dot_nn(x, w)
+            low_term = dot_nt(x, down_ref[:, pl.ds(start, width)])
+            acc = term if acc is None else acc + term
+            low = low_term if low is None else low + low_term
+        low_b = low.astype(jnp.bfloat16)
+        values = (acc[:, HD:] + dot_nn(low_b, up_ref[...])).astype(jnp.bfloat16)
+        keys = acc[:, :HD].astype(jnp.bfloat16)
+        low_t = jnp.transpose(low).astype(jnp.bfloat16)
+        for b in range(rows // BLK):
+            m = part * (rows // BLK) + b
+            pair_ref[m, 0:BLK, :] = keys[b * BLK : (b + 1) * BLK]
+            pair_ref[m, BLK : 2 * BLK, :] = values[b * BLK : (b + 1) * BLK]
+            pair_ref[m, 2 * BLK : PACK, :] = low_t[:, b * BLK : (b + 1) * BLK]
+    for r in range(readers):
+        out_ref[r] = pair_ref[asked_ref[r]]
+
+
+def span_kernel(spans, owners, heads, place_ref, bound_ref, x0, x1, x2, x3, wq_hbm, wk_hbm, wv_hbm, qd_hbm, vd_hbm,
+                qup_ref, vup_ref, tag_ref, grad_ref, grad_t_ref, got_ref, mcot_in, qg_in, vg_in,
+                cot_ref, mcot_ref, qg_ref, vg_ref,
+                wq_s, wkv_s, wv_s, qd_s, vd_s, q_s, k_own, v_own, low_s, k_all, v_all, p_s, att_s, dq_s, dv_s, sems):
+    width = x0.shape[1]
+    tokens = (x0, x1, x2, x3)
+    copies = []
+    for j in range(4):
+        start = pl.multiple_of(lax.bitwise_xor(place_ref[0], j) * width, width)
+        here = pl.ds(start, width)
+        group = [
+            pltpu.make_async_copy(wq_hbm.at[here, :], wq_s.at[j], sems.at[j, 0]),
+            pltpu.make_async_copy(wk_hbm.at[here, :], wkv_s.at[j], sems.at[j, 1]),
+            pltpu.make_async_copy(wv_hbm.at[here, :], wv_s.at[j], sems.at[j, 2]),
+            pltpu.make_async_copy(qd_hbm.at[:, here], qd_s.at[j], sems.at[j, 3]),
+            pltpu.make_async_copy(vd_hbm.at[:, here], vd_s.at[j], sems.at[j, 4]),
+        ]
+        for c in group:
+            c.start()
+        copies.append(group)
+    for b in range(owners):
+        k_all[b * BLK : (b + 1) * BLK, :] = got_ref[b, 0:BLK, :]
+        v_all[b * BLK : (b + 1) * BLK, :] = got_ref[b, BLK : 2 * BLK, :]
+    q_acc = None
+    for j in range(4):
+        for c in copies[j]:
+            c.wait()
+        x = tokens[j][...]
+        q_term = dot_nn(x, wq_s[j])
+        kv_term = dot_nn(x, jnp.concatenate([wkv_s[j], wv_s[j]], 1))
+        low_term = dot_nt(x, jnp.concatenate([qd_s[j], vd_s[j]], 0))
+        if q_acc is None:
+            q_acc, kv_acc, low_acc = q_term, kv_term, low_term
+        else:
+            q_acc, kv_acc, low_acc = q_acc + q_term, kv_acc + kv_term, low_acc + low_term
+    low = low_acc.astype(jnp.bfloat16)
+    q_s[...] = (q_acc + dot_nn(low[:, :RANK], qup_ref[...])).astype(jnp.bfloat16)
+    k_own[...] = kv_acc[:, :HD].astype(jnp.bfloat16)
+    v_own[...] = (kv_acc[:, HD:] + dot_nn(low[:, RANK:], vup_ref[...])).astype(jnp.bfloat16)
+    low_s[...] = jnp.transpose(low_acc).astype(jnp.bfloat16)
+    dv_s[...] = jnp.zeros_like(dv_s)
+    qg_ref[...] = qg_in[...]
+    vg_ref[...] = vg_in[...]
+    seen = owners * BLK
+    scale = HD ** (-0.5)
+    up_wide = vup_ref[...].astype(jnp.float32)
+
+    def span_step(c, carry):
+        first = pl.multiple_of(c * BLK, BLK)
+        rows = pl.ds(first, BLK)
+        k_all[seen:, :] = k_own[rows, :]
+        v_all[seen:, :] = v_own[rows, :]
+        edge = bound_ref[c]
+        row_ids = lax.broadcasted_iota(jnp.int32, (BLK, BLK), 0)
+        col_ids = lax.broadcasted_iota(jnp.int32, (BLK, BLK), 1)
+        visible = (col_ids <= row_ids) & ((col_ids >= edge) | (row_ids < edge))
+        keys = k_all[...]
+        values = v_all[...]
+        for h in range(heads):
+            cols = slice(h * HD, (h + 1) * HD)
+            g = grad_ref[rows, cols]
+            s = dot_nt(q_s[rows, cols], keys)
+            s = jnp.concatenate([s[:, :seen], jnp.where(visible, s[:, seen:], -jnp.inf)], 1)
+            top = jnp.max(s, axis=1, keepdims=True)
+            w = jnp.exp2((s - top) * (scale * LOG2E))
+            probs = w * (1.0 / jnp.sum(w, axis=1, keepdims=True))
+            probs_low = probs.astype(jnp.bfloat16)
+            att = dot_nn(probs_low, values).astype(jnp.bfloat16)
+            dp = dot_nt(g, values)
+            dot = jnp.sum(g.astype(jnp.float32) * att.astype(jnp.float32), axis=1, keepdims=True)
+            ds = (probs * ((dp - dot) * scale)).astype(jnp.bfloat16)
+            dq_s[:, cols] = dot_nn(ds, keys).astype(jnp.bfloat16)
+            att_s[:, cols] = att
+            p_s[h * BLK : (h + 1) * BLK, :] = probs_low
+        g_t = jnp.concatenate([grad_t_ref[h * HD : (h + 1) * HD, rows] for h in range(heads)], 1)
+        dv = dot_nn(g_t, p_s[...])
+        dv_s[...] += dv[:, :seen]
+        dv_own = dv[:, seen:]
+        low_v = low_s[RANK:, rows].astype(jnp.float32)
+        dq = dq_s[...]
+        cot_ref[0:RANK, rows] = dot_nt(qup_ref[...], dq)
+        cot_ref[RANK : 2 * RANK, rows] = dot_nn(up_wide, dv_own, HIGHEST)
+        cot_ref[2 * RANK :, rows] = dot_nt(tag_ref[...], att_s[...])
+        qg_ref[...] += dot_nn(low_s[0:RANK, rows], dq)
+        vg_ref[...] += dot_nt(low_v, dv_own, HIGHEST)
+        return carry
+
+    lax.fori_loop(0, spans, span_step, 0)
+    dv = dv_s[...]
+    mcot = dot_nn(up_wide, dv, HIGHEST)
+    low_m = jnp.concatenate([got_ref[b, 2 * BLK : PACK, :] for b in range(owners)], 1).astype(jnp.float32)
+    vg_ref[...] += dot_nt(low_m, dv, HIGHEST)
+    for b in range(owners):
+        mcot_ref[b] = mcot_in[b] + mcot[:, b * BLK : (b + 1) * BLK]
+
+
+def swap(x, bit):
+    return lax.ppermute(x, "heads", [(i, i ^ bit) for i in range(4)])
+
+
+def gather_parts(x):
+    far = swap(x, 2)
+    near = swap(x, 1)
+    return x, near, far, swap(far, 1)
+
+
+def heads_sum(x):
+    x = x + swap(x, 1)
+    return x + swap(x, 2)
+
+
+def smem():
+    return pl.BlockSpec(memory_space=pltpu.SMEM)
+
+
+def vmem():
+    return pl.BlockSpec(memory_space=pltpu.VMEM)
+
+
+def fast(
+    slab_tokens,
+    memory,
+    query_weight,
+    key_weight,
+    value_weight,
+    query_down,
+    query_up,
+    value_down,
+    value_up,
+    tag_weight,
+    retrieval,
+    boundary,
+    grad_tags,
+):
+    tok_rows, width = slab_tokens.shape
+    mem_rows = memory.shape[0]
+    query_width = query_weight.shape[1]
+    heads = query_width // HD
+    spans = tok_rows // BLK
+    blocks = mem_rows // BLK
+    peers = lax.axis_size("tm")
+    f32 = jnp.float32
+    bf16 = jnp.bfloat16
+    mem_cuts, tok_cuts = 2, 2
+
+    mem_parts = [gather_parts(m) for m in jnp.split(memory, mem_cuts, 0)]
+    tok_parts = [gather_parts(x) for x in jnp.split(slab_tokens, tok_cuts, 0)]
+
+    named = retrieval[0]
+    owner_ids = jnp.arange(peers, dtype=jnp.int32)
+    wanted = jnp.sum(
+        jnp.where(named[None, :] // blocks == owner_ids[:, None], named[None, :] % blocks, 0), axis=1
+    ).astype(jnp.int32)
+    asked = lax.all_to_all(wanted, "tm", split_axis=0, concat_axis=0, tiled=True)
+    place = lax.axis_index("heads").astype(jnp.int32).reshape(1)
+
+    tag_t = tag_weight.T
+    wide_tag = tag_t.astype(f32)
+    grad_t = lax.dot_general(
+        wide_tag, grad_tags, (((0,), (1,)), ((), ())), precision=HIGHEST
+    ).astype(bf16)
+    grad = lax.dot_general(grad_tags, wide_tag, (((1,), (0,)), ((), ())), precision=HIGHEST).astype(bf16)
+
+    outgoing = pl.pallas_call(
+        lambda *refs: memory_kernel(mem_cuts, peers, *refs),
+        out_shape=jax.ShapeDtypeStruct((peers, PACK, HD), bf16),
+        in_specs=[smem(), smem()] + [vmem()] * (4 * mem_cuts + 4),
+        out_specs=vmem(),
+        scratch_shapes=[pltpu.VMEM((blocks, PACK, HD), bf16)],
+        compiler_params=pltpu.CompilerParams(vmem_limit_bytes=VMEM_BYTES),
+        name="memory_pairs",
+    )(place, asked, *[p for part in mem_parts for p in part], key_weight, value_weight, value_down, value_up)
+    got = lax.all_to_all(outgoing, "tm", split_axis=0, concat_axis=0, tiled=True)
+
+    rows = tok_rows // tok_cuts
+    cut_spans = spans // tok_cuts
+    seen = peers * BLK
+    mcot = jnp.zeros((peers, RANK, BLK), f32)
+    query_up_grad = jnp.zeros((RANK, query_width), f32)
+    value_up_grad = jnp.zeros((RANK, HD), f32)
+    cots = []
+    anywhere = pl.BlockSpec(memory_space=pl.ANY)
+    call = pl.pallas_call(
+        lambda *refs: span_kernel(cut_spans, peers, heads, *refs),
+        out_shape=(
+            jax.ShapeDtypeStruct((2 * RANK + tag_t.shape[0], rows), f32),
+            jax.ShapeDtypeStruct((peers, RANK, BLK), f32),
+            jax.ShapeDtypeStruct((RANK, query_width), f32),
+            jax.ShapeDtypeStruct((RANK, HD), f32),
+        ),
+        in_specs=[smem(), smem()] + [vmem()] * 4 + [anywhere] * 5 + [vmem()] * 9,
+        out_specs=(vmem(),) * 4,
+        scratch_shapes=[
+            pltpu.VMEM((4, width, query_width), bf16),
+            pltpu.VMEM((4, width, HD), bf16),
+            pltpu.VMEM((4, width, HD), bf16),
+            pltpu.VMEM((4, RANK, width), bf16),
+            pltpu.VMEM((4, RANK, width), bf16),
+            pltpu.VMEM((rows, query_width), bf16),
+            pltpu.VMEM((rows, HD), bf16),
+            pltpu.VMEM((rows, HD), bf16),
+            pltpu.VMEM((2 * RANK, rows), bf16),
+            pltpu.VMEM((seen + BLK, HD), bf16),
+            pltpu.VMEM((seen + BLK, HD), bf16),
+            pltpu.VMEM((heads * BLK, seen + BLK), bf16),
+            pltpu.VMEM((BLK, query_width), bf16),
+            pltpu.VMEM((BLK, query_width), bf16),
+            pltpu.VMEM((HD, seen), f32),
+            pltpu.SemaphoreType.DMA((4, 5)),
+        ],
+        compiler_params=pltpu.CompilerParams(vmem_limit_bytes=VMEM_BYTES),
+        name="span_attention",
+    )
+    for t in range(tok_cuts):
+        cut = slice(t * rows, (t + 1) * rows)
+        cot, mcot, query_up_grad, value_up_grad = call(
+            place, boundary[t * cut_spans : (t + 1) * cut_spans], *tok_parts[t],
+            query_weight, key_weight, value_weight, query_down, value_down,
+            query_up, value_up, tag_t, grad[cut], grad_t[:, cut], got, mcot, query_up_grad, value_up_grad,
+        )
+        cots.append(cot)
+    cot = heads_sum(jnp.concatenate(cots, 1))
+    logits = cot[2 * RANK :].T
+    back = lax.all_to_all(mcot, "tm", split_axis=0, concat_axis=0, tiled=True)
+    block_ids = jnp.arange(blocks, dtype=jnp.int32)
+    hits = (asked[:, None] == block_ids[None, :])[:, :, None, None]
+    owned = jnp.sum(jnp.where(hits, back[:, None], 0.0), axis=0)
+    owned = heads_sum(owned)
+    owned = jnp.transpose(owned, (1, 0, 2)).reshape(RANK, mem_rows)
+    query_down_grad = jnp.dot(cot[:RANK].astype(bf16), slab_tokens, preferred_element_type=f32)
+    value_down_grad = jnp.dot(
+        cot[RANK : 2 * RANK].astype(bf16), slab_tokens, preferred_element_type=f32
+    ) + jnp.dot(owned.astype(bf16), memory, preferred_element_type=f32)
+
+    tiles = []
+    for grad_piece in (query_up_grad, value_up_grad, query_down_grad, value_down_grad):
+        for n in range(grad_piece.shape[1] // HD):
+            tiles.append(grad_piece[:, n * HD : (n + 1) * HD])
+    real = len(tiles)
+    each = -(-real // peers)
+    tiles += [jnp.zeros((RANK, HD), f32)] * (each * peers - real)
+    packed = jnp.concatenate(tiles, 0).reshape(peers, each * RANK, HD)
+    shares = lax.all_to_all(packed, "tm", split_axis=0, concat_axis=0, tiled=True)
+    share = jnp.sum(shares, axis=0)
+    everyone = jnp.broadcast_to(share[None], shares.shape)
+    whole = lax.all_to_all(everyone, "tm", split_axis=0, concat_axis=0, tiled=True)
+    whole = whole.reshape(peers * each, RANK, HD)
+    outs = []
+    at = 0
+    for grad_piece in (query_up_grad, value_up_grad, query_down_grad, value_down_grad):
+        count = grad_piece.shape[1] // HD
+        outs.append(jnp.concatenate([whole[at + n] for n in range(count)], 1))
+        at += count
+    query_up_grad, value_up_grad, query_down_grad, value_down_grad = outs
+    return (logits, query_down_grad, query_up_grad, value_down_grad, value_up_grad)
+
+
 def solution(mesh):
     in_specs = (
         P("tm", "heads"),
@@ -245,4 +547,6 @@
         P(None, "heads"),
         P(None, "heads"),
     )
+    fits = mesh.shape["heads"] == 4 and mesh.shape["tm"] * CAP == TOP
+    local = fast if fits else general
     return jax.shard_map(local, mesh=mesh, in_specs=in_specs, out_specs=out_specs, check_vma=False)

time: 274 us -> 155 us (0.57)
  waiting for transfers between devices: 113 us -> 34.2 us
  matrix products: 67.4 us -> 2.58 us
  Pallas kernels: 0 us -> 51.2 us
  local copies, waits for them, and re-layouts: 37 us -> 21.7 us
  between operations: 14.2 us -> 0.95 us
  starting transfers between devices: 18.8 us -> 28.3 us
  other arithmetic: 11 us -> 1.78 us
    psum x1 -> x0, waiting for transfers between devices: 69.7 us -> none  [local(): lax.psum((query_down_grad, query_up_grad, value_down_grad, value_up_grad)...]
    dot_general x26 -> x5, matrix products: 67.4 us -> 2.58 us  [the longest x1 0.94 us: fast(): lax.dot_general(grad_tags, wide_tag, (((1,), (0,)), ((), ())), precision=...]
    pallas_call x0 -> x3, Pallas kernels: none -> 51.2 us  [the longest x2 45.2 us: fast(): call(place, boundary[t * cut_spans:(t + 1) * cut_spans], *tok_parts[t], q...]
    all_gather x2 -> x0, waiting for transfers between devices: 30.6 us -> none  [the longest x1 18.7 us: local(): token_piece = lax.all_gather(slab_tokens, 'heads', axis=1, tiled=True)]
    ppermute x0 -> x16, waiting for transfers between devices: none -> 20.1 us  [swap(): return lax.ppermute(x, 'heads', [(i, i ^ bit) for i in range(4)])]
    all_to_all x0 -> x1, blocking collectives: none -> 13.6 us  [fast(): lax.all_to_all(packed, 'tm', split_axis=0, concat_axis=0, tiled=True)]
    psum x1 -> x0, blocking collectives: 12.3 us -> none  [local(): lax.psum(jnp.dot(attended, tag_weight, preferred_element_type=jnp.float32...]
    ppermute x0 -> x16, starting transfers between devices: none -> 9.09 us  [swap(): return lax.ppermute(x, 'heads', [(i, i ^ bit) for i in range(4)])]
  transfers between devices with their start and end apart: 6 -> 20, of which waited for: 4 -> 8; matrix products, arithmetic and copies ran while one was open for 17% -> 11% of each run, Pallas kernels for 0% -> 19%
where the time goes in v1:
time: 155 us; the launch traced here: 154 us
  Pallas kernels  51.2 us (33%)
  waiting for transfers between devices  34.2 us (22%)
  starting transfers between devices  28.3 us (18%)
  local copies, waits for them, and re-layouts  21.7 us (14%)
  blocking collectives  13.6 us (9%)
  matrix products  2.58 us (2%)
  other arithmetic  1.78 us (1%)
    pallas_call x2, Pallas kernels, fast(): call(place, boundary[t * cut_spans:(t + 1) * cut_spans], *tok_parts[t], q...  45.2 us
    ppermute x16, waiting for transfers between devices, swap(): return lax.ppermute(x, 'heads', [(i, i ^ bit) for i in range(4)])  20.1 us
    all_to_all x1, blocking collectives, fast(): lax.all_to_all(packed, 'tm', split_axis=0, concat_axis=0, tiled=True)  13.6 us
    unnamed x63, local copies, waits for them, and re-layouts  10.8 us
    ppermute x16, starting transfers between devices, swap(): return lax.ppermute(x, 'heads', [(i, i ^ bit) for i in range(4)])  9.09 us
    all_to_all x1, waiting for transfers between devices, fast(): lax.all_to_all(everyone, 'tm', split_axis=0, concat_axis=0, tiled=True)  7.11 us
    all_to_all x1, waiting for transfers between devices, fast(): lax.all_to_all(outgoing, 'tm', split_axis=0, concat_axis=0, tiled=True)  7 us
    all_to_all x1, starting transfers between devices, fast(): lax.all_to_all(wanted, 'tm', split_axis=0, concat_axis=0, tiled=True)  6.03 us
  transfers between devices with their start and end apart: 20, of which 8 were waited for; matrix products, arithmetic and copies ran while one was open for 11% of the time, Pallas kernels for 19%

profile of v1, /device:TPU:0, one launch (start us, length us, event | category | flops | bytes accessed | tf_op | source)
XLA Modules:
  0.0 154.2 jit_solution(7276541887652570889)
XLA Ops:
  0.7 1.3 fusion.13
  2.0 3.0 %collective-permute-start.4 = (bf16[256,896]{1,0:T(8,128)(2,1)S(1)}, bf16[256,896]{1,0:T(8,128)(2,1)}, u32[]{:S(2)}, u32[]{:S(2)}) collective-permute-start(bf16[256,896]{1,0:T(8,128)(2,1)S(1)} %get-tuple-element.32.refs_2_), channel_id=1, source_target_pairs={{0,2},{1,3},{2,0},{3,1},{4,6},{5,7},{6,4},{7,5},{8,10},{9,11},{10,... | collective-permute-start | bytes 1376264 | tf_op jit(solution)/shard_map/ppermute | solution.py:367
  5.0 0.2 collective-permute-start.7
  5.2 0.4 collective-permute-start.6
  5.6 0.7 fusion.8
  6.2 0.1 select_reduce_fusion.1
  6.4 0.7 copy.20
  7.0 6.0 %all-to-all-start = ((s32[8,1,1]{2,1,0:T(1,128)}), s32[8,1,1]{2,1,0:T(1,128)S(1)}, u32[]{:S(2)}, u32[]{:S(2)}) async-start(s32[8,1,1]{2,1,0:T(1,128)} %copy.20), calls=%async_computation | async-start | bytes 8192 | tf_op jit(solution)/shard_map/all_to_all | solution.py:423
  13.1 3.4 %collective-permute-done.4.refs_4_ = bf16[256,896]{1,0:T(8,128)(2,1)} collective-permute-done((bf16[256,896]{1,0:T(8,128)(2,1)S(1)}, bf16[256,896]{1,0:T(8,128)(2,1)}, u32[]{:S(2)}, u32[]{:S(2)}) %collective-permute-start.4) | collective-permute-done | bytes 458784 | tf_op jit(solution)/shard_map/ppermute | solution.py:367
  16.5 9.0 %collective-permute-done.7.refs_8_ = bf16[256,896]{1,0:T(8,128)(2,1)} collective-permute-done((bf16[256,896]{1,0:T(8,128)(2,1)S(1)}, bf16[256,896]{1,0:T(8,128)(2,1)}, u32[]{:S(2)}, u32[]{:S(2)}) %collective-permute-start.7) | collective-permute-done | bytes 458784 | tf_op jit(solution)/shard_map/ppermute | solution.py:367
  25.5 0.9 fusion.12
  26.4 1.7 %collective-permute-start.1 = (bf16[256,896]{1,0:T(8,128)(2,1)}, bf16[256,896]{1,0:T(8,128)(2,1)}, u32[]{:S(2)}, u32[]{:S(2)}) collective-permute-start(bf16[256,896]{1,0:T(8,128)(2,1)} %get-tuple-element.30.refs_2_), channel_id=1, source_target_pairs={{0,2},{1,3},{2,0},{3,1},{4,6},{5,7},{6,4},{7,5},{8,10},{9,11},{10,... | collective-permute-start | bytes 1376264 | tf_op jit(solution)/shard_map/ppermute | solution.py:367
  28.1 0.9 convolution_convert_fusion
  29.0 0.8 reduce.refs_1_
  29.8 0.2 collective-permute-start
  30.0 0.3 collective-permute-start.10
  30.4 6.0 %memory_pairs.1 = bf16[8,272,128]{2,1,0:T(8,128)(2,1)} custom-call(s32[1]{0:T(128)} %bitcast.refs_0_, s32[8]{0:T(128)} %reduce.refs_1_, bf16[256,896]{1,0:T(8,128)(2,1)} %copy-done.5, bf16[256,896]{1,0:T(8,128)(2,1)} %collective-permute-done.3.refs_3_, bf16[256,896]{1,0:T(8,128)(2,1)} %collective-permute-done.4.refs_4_, ...), custom_call_target="tpu_custom_call" | custom-call | tf_op jit(solution)/shard_map/memory_pairs/pallas_call | solution.py:433
  36.4 6.0 %all-to-all-start.1 = ((bf16[8,272,128]{2,1,0:T(8,128)(2,1)}), bf16[8,272,128]{2,1,0:T(8,128)(2,1)S(1)}, u32[]{:S(2)}, u32[]{:S(2)}) async-start(bf16[8,272,128]{2,1,0:T(8,128)(2,1)} %memory_pairs.1), calls=%async_computation.1 | async-start | bytes 1114112 | tf_op jit(solution)/shard_map/all_to_all | solution.py:442
  42.3 0.9 convolution_convert_fusion.1
  43.3 1.0 fusion.10
  44.3 0.2 collective-permute-start.2
  44.5 4.9 %collective-permute-done.10.refs_4_ = bf16[256,896]{1,0:T(8,128)(2,1)} collective-permute-done((bf16[256,896]{1,0:T(8,128)(2,1)S(1)}, bf16[256,896]{1,0:T(8,128)(2,1)}, u32[]{:S(2)}, u32[]{:S(2)}) %collective-permute-start.10) | collective-permute-done | bytes 458784 | tf_op jit(solution)/shard_map/ppermute | solution.py:367
  49.4 1.0 fusion.11
  50.5 0.7 fusion.14
  51.2 7.0 %all-to-all-done.1.refs_16_ = bf16[8,272,128]{2,1,0:T(8,128)(2,1)S(1)} async-done(((bf16[8,272,128]{2,1,0:T(8,128)(2,1)}), bf16[8,272,128]{2,1,0:T(8,128)(2,1)S(1)}, u32[]{:S(2)}, u32[]{:S(2)}) %all-to-all-start.1) | async-done | bytes 557088 | tf_op jit(solution)/shard_map/all_to_all | solution.py:442
  58.2 0.7 broadcast_in_dim.57.refs_17_
  58.8 0.6 broadcast_in_dim.58.refs_18_
  59.5 0.6 broadcast_in_dim.59.refs_19_
  60.1 22.7 %span_attention.2 = (f32[40,256]{1,0:T(8,128)}, f32[8,16,128]{2,1,0:T(8,128)}, f32[16,896]{1,0:T(8,128)}, f32[16,128]{1,0:T(8,128)}) custom-call(s32[1]{0:T(128)} %bitcast.refs_0_, s32[2]{0:T(128)} %get-tuple-element.55.refs_1_, bf16[256,896]{1,0:T(8,128)(2,1)} %get-tuple-element.30.refs_2_, bf16[256,896]{1,0:T(8,128)(2,1)} %collective-permute-done.refs_3_, ...), custom_call_target="tpu_custom_call" | custom-call | tf_op jit(solution)/shard_map/span_attention/pallas_call | solution.py:485
  82.8 0.8 copy-done.8
  83.6 22.6 %span_attention.3 = (f32[40,256]{1,0:T(8,128)}, f32[8,16,128]{2,1,0:T(8,128)}, f32[16,896]{1,0:T(8,128)}, f32[16,128]{1,0:T(8,128)}) custom-call(s32[1]{0:T(128)} %bitcast.refs_0_, s32[2]{0:T(128)} %get-tuple-element.54.refs_1_, bf16[256,896]{1,0:T(8,128)(2,1)} %copy-done.6, bf16[256,896]{1,0:T(8,128)(2,1)} %collective-permute-done.9.refs_3_, ...), custom_call_target="tpu_custom_call" | custom-call | tf_op jit(solution)/shard_map/span_attention/pallas_call | solution.py:485
  106.1 3.8 %all-to-all-start.2 = ((f32[8,16,128]{2,1,0:T(8,128)}), f32[8,16,128]{2,1,0:T(8,128)S(1)}, u32[]{:S(2)}, u32[]{:S(2)}) async-start(f32[8,16,128]{2,1,0:T(8,128)} %get-tuple-element.20), calls=%async_computation.2 | async-start | bytes 131072 | tf_op jit(solution)/shard_map/all_to_all | solution.py:493
  109.9 0.8 constant_dynamic-update-slice_fusion
  110.7 0.7 constant_dynamic-update-slice_fusion.24
  111.4 0.7 constant_dynamic-update-slice_fusion.23
  112.1 0.7 constant_dynamic-update-slice_fusion.22
  112.8 0.7 constant_dynamic-update-slice_fusion.21
  113.5 0.7 constant_dynamic-update-slice_fusion.20
  114.2 0.7 constant_dynamic-update-slice_fusion.19
  114.9 0.7 constant_dynamic-update-slice_fusion.18
  115.6 1.6 %collective-permute-start.13 = (f32[40,512]{1,0:T(8,128)S(1)}, f32[40,512]{1,0:T(8,128)S(1)}, u32[]{:S(2)}, u32[]{:S(2)}) collective-permute-start(f32[40,512]{1,0:T(8,128)S(1)} %add.23), channel_id=1, source_target_pairs={{0,2},{1,3},{2,0},{3,1},{4,6},{5,7},{6,4},{7,5},{8,10},{9,11},{10,... | collective-permute-start | bytes 245768 | tf_op jit(solution)/shard_map/ppermute | solution.py:367
  117.2 0.1 select_reduce_fusion
  117.3 0.3 collective-permute-start.14
  117.6 0.7 constant_dynamic-update-slice_fusion.17
  118.3 0.3 collective-permute-done.14
  118.6 1.1 collective-permute-start.15
  119.7 0.8 collective-permute-done.13
  120.6 0.2 fusion.5
  120.9 1.7 %collective-permute-done.15 = f32[4,16,128]{2,1,0:T(8,128)S(1)} collective-permute-done((f32[4,16,128]{2,1,0:T(8,128)S(1)}, f32[4,16,128]{2,1,0:T(8,128)S(1)}, u32[]{:S(2)}, u32[]{:S(2)}) %collective-permute-start.15) | collective-permute-done | bytes 32800 | tf_op jit(solution)/shard_map/ppermute | solution.py:367
  122.5 0.2 fusion.1
  122.8 0.3 convolution_add_fusion
  123.1 13.6 %all_to_all.31 = f32[8,48,128]{2,1,0:T(8,128)S(1)} all-to-all(f32[8,48,128]{2,1,0:T(8,128)S(1)} %bitcast.122), channel_id=1, replica_groups=mesh['tm'=8,'heads'=4] {'tm'}, dimensions={0} | all-to-all | bytes 393216 | tf_op jit(solution)/shard_map/all_to_all | solution.py:512
  136.7 0.7 broadcast_in_dim.63
  137.4 3.4 %all-to-all-start.4 = ((f32[8,48,128]{2,1,0:T(8,128)}), f32[8,48,128]{2,1,0:T(8,128)S(1)}, u32[]{:S(2)}, u32[]{:S(2)}) async-start(f32[8,48,128]{2,1,0:T(8,128)} %broadcast_in_dim.63), calls=%async_computation.4 | async-start | bytes 393216 | tf_op jit(solution)/shard_map/all_to_all | solution.py:515
  140.8 0.6 slice_bitcast_fusion
  141.4 7.1 %all-to-all-done.4 = f32[8,48,128]{2,1,0:T(8,128)S(1)} async-done(((f32[8,48,128]{2,1,0:T(8,128)}), f32[8,48,128]{2,1,0:T(8,128)S(1)}, u32[]{:S(2)}, u32[]{:S(2)}) %all-to-all-start.4) | async-done | bytes 196640 | tf_op jit(solution)/shard_map/all_to_all | solution.py:515
  148.5 0.6 slice_bitcast_fusion.1
  149.2 0.7 constant_dynamic-update-slice_fusion.44
  149.9 0.7 constant_dynamic-update-slice_fusion.43
  150.6 0.7 constant_dynamic-update-slice_fusion.42
  151.4 0.7 constant_dynamic-update-slice_fusion.41
  152.1 0.7 constant_dynamic-update-slice_fusion.40
  152.8 0.7 constant_dynamic-update-slice_fusion.39
  153.6 0.6 copy-done.14
  (73 shorter events, 0.4 us)
Async XLA Ops:
  0.6 27.5 %copy-start = (f32[512,8]{0,1:T(8,128)S(1)}, f32[512,8]{0,1:T(8,128)}, u32[]{:S(2)}) copy-start(f32[512,8]{0,1:T(8,128)} %param.25) | copy-start | bytes 49156
  0.6 24.9 %copy-start.1 = (bf16[512,896]{1,0:T(8,128)(2,1)S(1)}, bf16[512,896]{1,0:T(8,128)(2,1)}, u32[]{:S(2)}) copy-start(bf16[512,896]{1,0:T(8,128)(2,1)} %param.13) | copy-start | bytes 2752516
  0.7 27.4 %copy-start.10 = (bf16[896,8]{0,1:T(8,128)(2,1)S(1)}, bf16[896,8]{0,1:T(8,128)(2,1)}, u32[]{:S(2)}) copy-start(bf16[896,8]{0,1:T(8,128)(2,1)} %param.22) | copy-start | bytes 43012
  2.0 28.4 %copy-start.4 = (bf16[256,896]{1,0:T(8,128)(2,1)}, bf16[256,896]{1,0:T(8,128)(2,1)S(1)}, u32[]{:S(2)}) copy-start(bf16[256,896]{1,0:T(8,128)(2,1)S(1)} %get-tuple-element.31.refs_6_) | copy-start | bytes 1376260
  2.0 28.4 %copy-start.5 = (bf16[256,896]{1,0:T(8,128)(2,1)}, bf16[256,896]{1,0:T(8,128)(2,1)S(1)}, u32[]{:S(2)}) copy-start(bf16[256,896]{1,0:T(8,128)(2,1)S(1)} %get-tuple-element.32.refs_2_) | copy-start | bytes 1376260
  2.0 14.5 %collective-permute-start.4 = (bf16[256,896]{1,0:T(8,128)(2,1)S(1)}, bf16[256,896]{1,0:T(8,128)(2,1)}, u32[]{:S(2)}, u32[]{:S(2)}) collective-permute-start(bf16[256,896]{1,0:T(8,128)(2,1)S(1)} %get-tuple-element.32.refs_2_), channel_id=1, source_target_pairs={{0,2},{1,3},{2,0},{3,1},{4,6},{5,7},{6,4},{7,5},{8,10},{9,11},{10,... | collective-permute-start | bytes 1376264 | tf_op jit(solution)/shard_map/ppermute | solution.py:367
  5.0 24.8 %collective-permute-start.3 = (bf16[256,896]{1,0:T(8,128)(2,1)S(1)}, bf16[256,896]{1,0:T(8,128)(2,1)}, u32[]{:S(2)}, u32[]{:S(2)}) collective-permute-start(bf16[256,896]{1,0:T(8,128)(2,1)S(1)} %get-tuple-element.32.refs_2_), channel_id=1, source_target_pairs={{0,1},{1,0},{2,3},{3,2},{4,5},{5,4},{6,7},{7,6},{8,9},{9,8},{10,11... | collective-permute-start | bytes 1376264 | tf_op jit(solution)/shard_map/ppermute | solution.py:367
  5.0 20.5 %collective-permute-start.7 = (bf16[256,896]{1,0:T(8,128)(2,1)S(1)}, bf16[256,896]{1,0:T(8,128)(2,1)}, u32[]{:S(2)}, u32[]{:S(2)}) collective-permute-start(bf16[256,896]{1,0:T(8,128)(2,1)S(1)} %get-tuple-element.31.refs_6_), channel_id=1, source_target_pairs={{0,2},{1,3},{2,0},{3,1},{4,6},{5,7},{6,4},{7,5},{8,10},{9,11},{10,... | collective-permute-start | bytes 1376264 | tf_op jit(solution)/shard_map/ppermute | solution.py:367
  5.2 24.8 %collective-permute-start.6 = (bf16[256,896]{1,0:T(8,128)(2,1)S(1)}, bf16[256,896]{1,0:T(8,128)(2,1)}, u32[]{:S(2)}, u32[]{:S(2)}) collective-permute-start(bf16[256,896]{1,0:T(8,128)(2,1)S(1)} %get-tuple-element.31.refs_6_), channel_id=1, source_target_pairs={{0,1},{1,0},{2,3},{3,2},{4,5},{5,4},{6,7},{7,6},{8,9},{9,8},{10,11... | collective-permute-start | bytes 1376264 | tf_op jit(solution)/shard_map/ppermute | solution.py:367
  7.0 22.0 %all-to-all-start = ((s32[8,1,1]{2,1,0:T(1,128)}), s32[8,1,1]{2,1,0:T(1,128)S(1)}, u32[]{:S(2)}, u32[]{:S(2)}) async-start(s32[8,1,1]{2,1,0:T(1,128)} %copy.20), calls=%async_computation | async-start | bytes 8192 | tf_op jit(solution)/shard_map/all_to_all | solution.py:423
  16.5 13.8 %collective-permute-start.5 = (bf16[256,896]{1,0:T(8,128)(2,1)}, bf16[256,896]{1,0:T(8,128)(2,1)}, u32[]{:S(2)}, u32[]{:S(2)}) collective-permute-start(bf16[256,896]{1,0:T(8,128)(2,1)} %collective-permute-done.4.refs_4_), channel_id=1, source_target_pairs={{0,1},{1,0},{2,3},{3,2},{4,5},{5,4},{6,7},{7,6},{8,9},{9,8},{10,11... | collective-permute-start | bytes 1376264 | tf_op jit(solution)/shard_map/ppermute | solution.py:367
  25.5 4.9 %collective-permute-start.8 = (bf16[256,896]{1,0:T(8,128)(2,1)}, bf16[256,896]{1,0:T(8,128)(2,1)}, u32[]{:S(2)}, u32[]{:S(2)}) collective-permute-start(bf16[256,896]{1,0:T(8,128)(2,1)} %collective-permute-done.7.refs_8_), channel_id=1, source_target_pairs={{0,1},{1,0},{2,3},{3,2},{4,5},{5,4},{6,7},{7,6},{8,9},{9,8},{10,11... | collective-permute-start | bytes 1376264 | tf_op jit(solution)/shard_map/ppermute | solution.py:367
  26.4 10.0 %copy-start.6 = (bf16[256,896]{1,0:T(8,128)(2,1)}, bf16[256,896]{1,0:T(8,128)(2,1)S(1)}, u32[]{:S(2)}) copy-start(bf16[256,896]{1,0:T(8,128)(2,1)S(1)} %get-tuple-element.29.refs_2_) | copy-start | bytes 1376260
  26.4 18.0 %collective-permute-start.1 = (bf16[256,896]{1,0:T(8,128)(2,1)}, bf16[256,896]{1,0:T(8,128)(2,1)}, u32[]{:S(2)}, u32[]{:S(2)}) collective-permute-start(bf16[256,896]{1,0:T(8,128)(2,1)} %get-tuple-element.30.refs_2_), channel_id=1, source_target_pairs={{0,2},{1,3},{2,0},{3,1},{4,6},{5,7},{6,4},{7,5},{8,10},{9,11},{10,... | collective-permute-start | bytes 1376264 | tf_op jit(solution)/shard_map/ppermute | solution.py:367
  29.8 21.4 %collective-permute-start = (bf16[256,896]{1,0:T(8,128)(2,1)}, bf16[256,896]{1,0:T(8,128)(2,1)}, u32[]{:S(2)}, u32[]{:S(2)}) collective-permute-start(bf16[256,896]{1,0:T(8,128)(2,1)} %get-tuple-element.30.refs_2_), channel_id=1, source_target_pairs={{0,1},{1,0},{2,3},{3,2},{4,5},{5,4},{6,7},{7,6},{8,9},{9,8},{10,11... | collective-permute-start | bytes 1376264 | tf_op jit(solution)/shard_map/ppermute | solution.py:367
  30.0 19.4 %collective-permute-start.10 = (bf16[256,896]{1,0:T(8,128)(2,1)S(1)}, bf16[256,896]{1,0:T(8,128)(2,1)}, u32[]{:S(2)}, u32[]{:S(2)}) collective-permute-start(bf16[256,896]{1,0:T(8,128)(2,1)S(1)} %get-tuple-element.29.refs_2_), channel_id=1, source_target_pairs={{0,2},{1,3},{2,0},{3,1},{4,6},{5,7},{6,4},{7,5},{8,10},{9,11},{10,... | collective-permute-start | bytes 1376264 | tf_op jit(solution)/shard_map/ppermute | solution.py:367
  30.3 52.5 %collective-permute-start.9 = (bf16[256,896]{1,0:T(8,128)(2,1)S(1)}, bf16[256,896]{1,0:T(8,128)(2,1)}, u32[]{:S(2)}, u32[]{:S(2)}) collective-permute-start(bf16[256,896]{1,0:T(8,128)(2,1)S(1)} %get-tuple-element.29.refs_2_), channel_id=1, source_target_pairs={{0,1},{1,0},{2,3},{3,2},{4,5},{5,4},{6,7},{7,6},{8,9},{9,8},{10,11... | collective-permute-start | bytes 1376264 | tf_op jit(solution)/shard_map/ppermute | solution.py:367
  36.4 21.8 %all-to-all-start.1 = ((bf16[8,272,128]{2,1,0:T(8,128)(2,1)}), bf16[8,272,128]{2,1,0:T(8,128)(2,1)S(1)}, u32[]{:S(2)}, u32[]{:S(2)}) async-start(bf16[8,272,128]{2,1,0:T(8,128)(2,1)} %memory_pairs.1), calls=%async_computation.1 | async-start | bytes 1114112 | tf_op jit(solution)/shard_map/all_to_all | solution.py:442
  43.3 7.2 %copy-start.13 = (s32[4]{0:T(128)S(1)}, s32[4]{0:T(128)}, u32[]{:S(2)}) copy-start(s32[4]{0:T(128)} %param.24) | copy-start | bytes 52
  43.3 7.8 %copy-start.12 = (s32[8]{0:T(128)S(1)}, s32[8]{0:T(128)}, u32[]{:S(2)}) copy-start(s32[8]{0:T(128)} %reduce.refs_1_) | copy-start | bytes 100
  44.3 6.9 %collective-permute-start.2 = (bf16[256,896]{1,0:T(8,128)(2,1)}, bf16[256,896]{1,0:T(8,128)(2,1)S(1)}, u32[]{:S(2)}, u32[]{:S(2)}) collective-permute-start(bf16[256,896]{1,0:T(8,128)(2,1)} %collective-permute-done.1.refs_4_), channel_id=1, source_target_pairs={{0,1},{1,0},{2,3},{3,2},{4,5},{5,4},{6,7},{7,6},{8,9},{9,8},{10,11... | collective-permute-start | bytes 1376264 | tf_op jit(solution)/shard_map/ppermute | solution.py:367
  49.4 33.3 %collective-permute-start.11 = (bf16[256,896]{1,0:T(8,128)(2,1)}, bf16[256,896]{1,0:T(8,128)(2,1)S(1)}, u32[]{:S(2)}, u32[]{:S(2)}) collective-permute-start(bf16[256,896]{1,0:T(8,128)(2,1)} %collective-permute-done.10.refs_4_), channel_id=1, source_target_pairs={{0,1},{1,0},{2,3},{3,2},{4,5},{5,4},{6,7},{7,6},{8,9},{9,8},{10,11... | collective-permute-start | bytes 1376264 | tf_op jit(solution)/shard_map/ppermute | solution.py:367
  51.2 8.9 %copy-start.9 = (bf16[256,896]{1,0:T(8,128)(2,1)}, bf16[256,896]{1,0:T(8,128)(2,1)S(1)}, u32[]{:S(2)}) copy-start(bf16[256,896]{1,0:T(8,128)(2,1)S(1)} %collective-permute-done.2.refs_5_) | copy-start | bytes 1376260
  58.2 1.9 %copy-start.2 = (bf16[8,272,128]{2,1,0:T(8,128)(2,1)}, bf16[8,272,128]{2,1,0:T(8,128)(2,1)S(1)}, u32[]{:S(2)}) copy-start(bf16[8,272,128]{2,1,0:T(8,128)(2,1)S(1)} %all-to-all-done.1.refs_16_) | copy-start | bytes 1671172
  82.8 0.8 copy-start.8
  83.6 26.4 %copy-start.11 = (f32[40,256]{1,0:T(8,128)S(1)}, f32[40,256]{1,0:T(8,128)}, u32[]{:S(2)}) copy-start(f32[40,256]{1,0:T(8,128)} %get-tuple-element.13) | copy-start | bytes 122884
  106.1 16.4 %copy-start.3 = (bf16[512,896]{1,0:T(8,128)(2,1)S(1)}, bf16[512,896]{1,0:T(8,128)(2,1)}, u32[]{:S(2)}) copy-start(bf16[512,896]{1,0:T(8,128)(2,1)} %param.14) | copy-start | bytes 2752516
  106.1 11.1 %all-to-all-start.2 = ((f32[8,16,128]{2,1,0:T(8,128)}), f32[8,16,128]{2,1,0:T(8,128)S(1)}, u32[]{:S(2)}, u32[]{:S(2)}) async-start(f32[8,16,128]{2,1,0:T(8,128)} %get-tuple-element.20), calls=%async_computation.2 | async-start | bytes 131072 | tf_op jit(solution)/shard_map/all_to_all | solution.py:493
  110.7 4.9 %collective-permute-start.12 = (f32[40,512]{1,0:T(8,128)S(1)}, f32[40,512]{1,0:T(8,128)S(1)}, u32[]{:S(2)}, u32[]{:S(2)}) collective-permute-start(f32[40,512]{1,0:T(8,128)S(1)} %constant_dynamic-update-slice_fusion), channel_id=1, source_target_pairs={{0,1},{1,0},{2,3},{3,2},{4,5},{5,4},{6,7},{7,6},{8,9},{9,8},{10,11... | collective-permute-start | bytes 245768 | tf_op jit(solution)/shard_map/ppermute | solution.py:367
  115.6 4.9 %collective-permute-start.13 = (f32[40,512]{1,0:T(8,128)S(1)}, f32[40,512]{1,0:T(8,128)S(1)}, u32[]{:S(2)}, u32[]{:S(2)}) collective-permute-start(f32[40,512]{1,0:T(8,128)S(1)} %add.23), channel_id=1, source_target_pairs={{0,2},{1,3},{2,0},{3,1},{4,6},{5,7},{6,4},{7,5},{8,10},{9,11},{10,... | collective-permute-start | bytes 245768 | tf_op jit(solution)/shard_map/ppermute | solution.py:367
  117.3 1.3 collective-permute-start.14
  118.6 3.9 %collective-permute-start.15 = (f32[4,16,128]{2,1,0:T(8,128)S(1)}, f32[4,16,128]{2,1,0:T(8,128)S(1)}, u32[]{:S(2)}, u32[]{:S(2)}) collective-permute-start(f32[4,16,128]{2,1,0:T(8,128)S(1)} %add.25), channel_id=1, source_target_pairs={{0,2},{1,3},{2,0},{3,1},{4,6},{5,7},{6,4},{7,5},{8,10},{9,11},{10,... | collective-permute-start | bytes 98312 | tf_op jit(solution)/shard_map/ppermute | solution.py:367
  137.4 11.1 %all-to-all-start.4 = ((f32[8,48,128]{2,1,0:T(8,128)}), f32[8,48,128]{2,1,0:T(8,128)S(1)}, u32[]{:S(2)}, u32[]{:S(2)}) async-start(f32[8,48,128]{2,1,0:T(8,128)} %broadcast_in_dim.63), calls=%async_computation.4 | async-start | bytes 393216 | tf_op jit(solution)/shard_map/all_to_all | solution.py:515
  148.5 0.7 copy-start.7
  153.6 0.6 copy-start.14
  153.6 0.6 copy-start.15
  153.6 0.7 copy-start.16

commit v2 on v0

--- a/solution.py
+++ b/solution.py
@@ -1,6 +1,8 @@
 import jax
 import jax.numpy as jnp
 from jax import lax
+from jax.experimental import pallas as pl
+from jax.experimental.pallas import tpu as pltpu
 from jax.sharding import PartitionSpec as P
 
 HD = 128
@@ -66,7 +68,7 @@
     return needed[:, None, :] * (places[:, None, :] == slot_ids[None, :, None]).astype(jnp.int32)
 
 
-def local(
+def general(
     slab_tokens,
     memory,
     query_weight,
@@ -222,6 +224,459 @@
     return (logits_out, query_down_grad, query_up_grad, value_down_grad, value_up_grad)
 
 
+LOG2E = 1.4426950408889634
+NT = (((1,), (1,)), ((), ()))
+PACK = 2 * BLK + RANK
+STRIP = 16
+VMEM_BYTES = 48 * 1024 * 1024
+
+
+def dot_nt(a, b, precision=None):
+    return lax.dot_general(a, b, NT, precision=precision, preferred_element_type=jnp.float32)
+
+
+def dot_nn(a, b, precision=None):
+    return jnp.dot(a, b, precision=precision, preferred_element_type=jnp.float32)
+
+
+def piece_rows(place_ref, j, width):
+    return pl.ds(pl.multiple_of(lax.bitwise_xor(place_ref[0], j) * width, width), width)
+
+
+def memory_kernel(peers, last, place_ref, me_ref, asked_ref, x0, x1, x2, x3, wk_ref, wv_ref, down_ref, up_ref, *refs):
+    tokens = (x0, x1, x2, x3)
+    rows, width = x0.shape
+    blocks = rows // BLK
+    acc = None
+    low = None
+    for j in range(4):
+        here = piece_rows(place_ref, j, width)
+        x = tokens[j][...]
+        term = dot_nn(x, jnp.concatenate([wk_ref[here, :], wv_ref[here, :]], 1))
+        low_term = dot_nt(x, down_ref[:, here])
+        acc = term if acc is None else acc + term
+        low = low_term if low is None else low + low_term
+    values = (acc[:, HD:] + dot_nn(low.astype(jnp.bfloat16), up_ref[...])).astype(jnp.bfloat16)
+    keys = acc[:, :HD].astype(jnp.bfloat16)
+    low_t = jnp.transpose(low).astype(jnp.bfloat16)
+    if last:
+        before, outs, pair_ref = refs[0], refs[1 : 1 + peers], refs[1 + peers]
+        offset = before.shape[0]
+        pair_ref[:offset] = before[...]
+    else:
+        pair_ref = refs[0]
+        offset = 0
+    for b in range(blocks):
+        at = slice(b * BLK, (b + 1) * BLK)
+        pair_ref[offset + b, 0:BLK, :] = keys[at]
+        pair_ref[offset + b, BLK : 2 * BLK, :] = values[at]
+        pair_ref[offset + b, 2 * BLK : PACK, :] = low_t[:, at]
+    if last:
+        for d in range(peers):
+            outs[d][...] = pair_ref[asked_ref[lax.bitwise_xor(me_ref[0], d)]]
+
+
+def project_kernel(place_ref, x0, x1, x2, x3, wq_hbm, wk_hbm, wv_hbm, qd_hbm, vd_hbm, qup_ref, vup_ref,
+                   q_ref, k_ref, v_ref, low_ref, wq_s, wk_s, wv_s, qd_s, vd_s, sems):
+    tokens = (x0, x1, x2, x3)
+    width = x0.shape[1]
+    copies = []
+    for j in range(4):
+        here = piece_rows(place_ref, j, width)
+        group = [
+            pltpu.make_async_copy(wq_hbm.at[here, :], wq_s.at[j], sems.at[j, 0]),
+            pltpu.make_async_copy(wk_hbm.at[here, :], wk_s.at[j], sems.at[j, 1]),
+            pltpu.make_async_copy(wv_hbm.at[here, :], wv_s.at[j], sems.at[j, 2]),
+            pltpu.make_async_copy(qd_hbm.at[:, here], qd_s.at[j], sems.at[j, 3]),
+            pltpu.make_async_copy(vd_hbm.at[:, here], vd_s.at[j], sems.at[j, 4]),
+        ]
+        for c in group:
+            c.start()
+        copies.append(group)
+    q_acc = kv_acc = low_acc = None
+    for j in range(4):
+        for c in copies[j]:
+            c.wait()
+        x = tokens[j][...]
+        q_term = dot_nn(x, wq_s[j])
+        kv_term = dot_nn(x, jnp.concatenate([wk_s[j], wv_s[j]], 1))
+        low_term = dot_nt(x, jnp.concatenate([qd_s[j], vd_s[j]], 0))
+        if q_acc is None:
+            q_acc, kv_acc, low_acc = q_term, kv_term, low_term
+        else:
+            q_acc, kv_acc, low_acc = q_acc + q_term, kv_acc + kv_term, low_acc + low_term
+    low = low_acc.astype(jnp.bfloat16)
+    q_ref[...] = (q_acc + dot_nn(low[:, :RANK], qup_ref[...])).astype(jnp.bfloat16)
+    k_ref[...] = kv_acc[:, :HD].astype(jnp.bfloat16)
+    v_ref[...] = (kv_acc[:, HD:] + dot_nn(low[:, RANK:], vup_ref[...])).astype(jnp.bfloat16)
+    low_ref[...] = jnp.transpose(low_acc).astype(jnp.bfloat16)
+
+
+def attention_kernel(cuts, peers, heads, bound_ref, *refs):
+    parts = refs[: 4 * cuts]
+    got = refs[4 * cuts : 4 * cuts + peers]
+    qup_ref, vup_ref, tag_ref, grad_ref, grad_t_ref = refs[4 * cuts + peers : 4 * cuts + peers + 5]
+    outs = refs[4 * cuts + peers + 5 :]
+    cot_ref, up_ref = outs[0], outs[1]
+    mcot_refs = outs[2 : 2 + peers]
+    (q_s, k_own, v_own, low_s, k_all, v_all, kt_all, vt_all, bias_s, s_s, e_s, dp_s, p_s, ds_s, att_s, dq_s, dv_s) = outs[2 + peers :]
+    seen = peers * BLK
+    for t in range(cuts):
+        q_c, k_c, v_c, low_c = parts[4 * t : 4 * t + 4]
+        rows = q_c.shape[0]
+        at = slice(t * rows, (t + 1) * rows)
+        q_s[at, :] = q_c[...]
+        k_own[at, :] = k_c[...]
+        v_own[at, :] = v_c[...]
+        low_s[:, at] = low_c[...]
+    for b in range(peers):
+        at = slice(b * BLK, (b + 1) * BLK)
+        k = got[b][0:BLK, :]
+        v = got[b][BLK : 2 * BLK, :]
+        k_all[at, :] = k
+        v_all[at, :] = v
+        kt_all[:, at] = jnp.transpose(k)
+        vt_all[:, at] = jnp.transpose(v)
+    dv_s[...] = jnp.zeros_like(dv_s)
+    up_ref[...] = jnp.zeros_like(up_ref)
+    scale = HD ** (-0.5)
+    up_wide = vup_ref[...].astype(jnp.float32)
+    query_width = heads * HD
+
+    def span_step(c, carry):
+        rows = pl.ds(pl.multiple_of(c * BLK, BLK), BLK)
+        k = k_own[rows, :]
+        v = v_own[rows, :]
+        k_all[seen:, :] = k
+        v_all[seen:, :] = v
+        kt_all[:, seen:] = jnp.transpose(k)
+        vt_all[:, seen:] = jnp.transpose(v)
+        edge = bound_ref[c]
+        row_ids = lax.broadcasted_iota(jnp.int32, (BLK, BLK), 0)
+        col_ids = lax.broadcasted_iota(jnp.int32, (BLK, BLK), 1)
+        visible = (col_ids <= row_ids) & ((col_ids >= edge) | (row_ids < edge))
+        bias_s[...] = jnp.where(visible, 0.0, -jnp.inf)
+
+        def head_cols(h):
+            return slice(h * HD, (h + 1) * HD)
+
+        def scores(h):
+            s_s[h % 2] = dot_nn(q_s[rows, head_cols(h)], kt_all[...])
+
+        def prob_grads(h):
+            dp_s[h % 3] = dot_nn(grad_ref[rows, head_cols(h)], vt_all[...])
+
+        def softmax(h):
+            for r in range(0, BLK, STRIP):
+                at = slice(r, r + STRIP)
+                s = s_s[h % 2, at, :]
+                s = jnp.concatenate([s[:, :seen], s[:, seen:] + bias_s[at, :]], 1) * (scale * LOG2E)
+                w = jnp.exp2(s - jnp.max(s, axis=1, keepdims=True))
+                probs = w * (1.0 / jnp.sum(w, axis=1, keepdims=True))
+                e_s[h % 2, at, :] = probs
+                p_s[h * BLK + r : h * BLK + r + STRIP, :] = probs.astype(jnp.bfloat16)
+
+        def attend_head(h):
+            att_s[:, head_cols(h)] = dot_nn(p_s[h * BLK : (h + 1) * BLK, :], v_all[...]).astype(jnp.bfloat16)
+
+        def score_grads(h):
+            for r in range(0, BLK, STRIP):
+                at = slice(r, r + STRIP)
+                g = grad_ref[pl.ds(pl.multiple_of(c * BLK + r, STRIP), STRIP), head_cols(h)]
+                dot = jnp.sum(
+                    g.astype(jnp.float32) * att_s[at, head_cols(h)].astype(jnp.float32), axis=1, keepdims=True
+                )
+                ds_s[h % 2, at, :] = (e_s[h % 2, at, :] * ((dp_s[h % 3, at, :] - dot) * scale)).astype(jnp.bfloat16)
+            dq_s[:, head_cols(h)] = dot_nn(ds_s[h % 2], k_all[...]).astype(jnp.bfloat16)
+
+        scores(0)
+        prob_grads(0)
+        for h in range(heads + 1):
+            if h < heads:
+                softmax(h)
+            if h + 1 < heads:
+                scores(h + 1)
+                prob_grads(h + 1)
+            if h > 0:
+                score_grads(h - 1)
+            if h < heads:
+                attend_head(h)
+        g_t = jnp.concatenate([grad_t_ref[h * HD : (h + 1) * HD, rows] for h in range(heads)], 1)
+        dv = dot_nn(g_t, p_s[...])
+        dv_s[...] += dv[:, :seen]
+        dv_own = dv[:, seen:]
+        dq = dq_s[...]
+        cot_ref[0:RANK, rows] = dot_nt(qup_ref[...], dq)
+        cot_ref[RANK : 2 * RANK, rows] = dot_nn(up_wide, dv_own, HIGHEST)
+        cot_ref[2 * RANK :, rows] = dot_nt(tag_ref[...], att_s[...])
+        up_ref[:, :query_width] += dot_nn(low_s[0:RANK, rows], dq)
+        up_ref[:, query_width:] += dot_nt(low_s[RANK:, rows].astype(jnp.float32), dv_own, HIGHEST)
+        return carry
+
+    lax.fori_loop(0, q_s.shape[0] // BLK, span_step, 0)
+    dv = dv_s[...]
+    mcot = dot_nn(up_wide, dv, HIGHEST)
+    low_m = jnp.concatenate([got[b][2 * BLK : PACK, :] for b in range(peers)], 1).astype(jnp.float32)
+    up_ref[:, query_width:] += dot_nt(low_m, dv, HIGHEST)
+    for b in range(peers):
+        mcot_refs[b][...] = mcot[:, b * BLK : (b + 1) * BLK]
+
+
+def own_kernel(peers, me_ref, asked_ref, *refs):
+    pieces, out_ref, sum_s = refs[:peers], refs[peers], refs[peers + 1]
+    sum_s[...] = jnp.zeros_like(sum_s)
+    for d in range(peers):
+        block = asked_ref[lax.bitwise_xor(me_ref[0], d)]
+        sum_s[block] = sum_s[block] + pieces[d][...]
+    out_ref[...] = jnp.concatenate([sum_s[m] for m in range(sum_s.shape[0])], 1)
+
+
+def down_kernel(peers, me_ref, *refs):
+    cots, owns = refs[0:4], refs[4:8]
+    slab_ref, memory_ref, logit_ref = refs[8:11]
+    outs, part_s = refs[11 : 11 + peers], refs[11 + peers]
+    cot = (cots[0][...] + cots[1][...]) + (cots[2][...] + cots[3][...])
+    own = (owns[0][...] + owns[1][...]) + (owns[2][...] + owns[3][...])
+    logit_ref[...] = cot[2 * RANK :]
+    both = dot_nn(cot[: 2 * RANK].astype(jnp.bfloat16), slab_ref[...])
+    value = both[RANK:] + dot_nn(own.astype(jnp.bfloat16), memory_ref[...])
+    tiles = []
+    for whole in (both[:RANK], value):
+        for n in range(whole.shape[1] // HD):
+            tiles.append(whole[:, n * HD : (n + 1) * HD])
+    each = part_s.shape[1]
+    for n in range(each * peers):
+        part_s[n // each, n % each] = tiles[n] if n < len(tiles) else jnp.zeros((RANK, HD), jnp.float32)
+    for d in range(peers):
+        outs[d][...] = part_s[lax.bitwise_xor(me_ref[0], d)]
+
+
+def share_kernel(peers, *refs):
+    total = refs[0][...]
+    for d in range(1, peers):
+        total = total + refs[d][...]
+    refs[peers][...] = total
+
+
+def finish_kernel(peers, me_ref, *refs):
+    shares, up_ref = refs[:peers], refs[peers]
+    query_down_ref, query_up_ref, value_down_ref, value_up_ref, all_s = refs[peers + 1 :]
+    for d in range(peers):
+        all_s[lax.bitwise_xor(me_ref[0], d)] = shares[d][...]
+    each = all_s.shape[1]
+    n = 0
+    for out_ref in (query_down_ref, value_down_ref):
+        for m in range(out_ref.shape[1] // HD):
+            out_ref[:, m * HD : (m + 1) * HD] = all_s[n // each, n % each]
+            n += 1
+    query_width = query_up_ref.shape[1]
+    query_up_ref[...] = up_ref[:, :query_width]
+    value_up_ref[...] = up_ref[:, query_width:]
+
+
+def swap(x, bit, axis="heads"):
+    return lax.ppermute(x, axis, [(i, i ^ bit) for i in range(lax.axis_size(axis))])
+
+
+def gather_parts(x):
+    far = swap(x, 2)
+    near = swap(x, 1)
+    return x, near, far, swap(far, 1)
+
+
+def smem():
+    return pl.BlockSpec(memory_space=pltpu.SMEM)
+
+
+def vmem():
+    return pl.BlockSpec(memory_space=pltpu.VMEM)
+
+
+def shaped(*shape, dtype=jnp.float32):
+    return jax.ShapeDtypeStruct(shape, dtype)
+
+
+def run(body, name, out_shape, in_specs, scratch=(), flops=0, moved=0):
+    many = isinstance(out_shape, (tuple, list))
+    return pl.pallas_call(
+        body,
+        out_shape=out_shape,
+        in_specs=in_specs,
+        out_specs=tuple(vmem() for _ in out_shape) if many else vmem(),
+        scratch_shapes=list(scratch),
+        compiler_params=pltpu.CompilerParams(vmem_limit_bytes=VMEM_BYTES),
+        cost_estimate=pl.CostEstimate(flops=flops, bytes_accessed=moved, transcendentals=0),
+        name=name,
+    )
+
+
+def fast(
+    slab_tokens,
+    memory,
+    query_weight,
+    key_weight,
+    value_weight,
+    query_down,
+    query_up,
+    value_down,
+    value_up,
+    tag_weight,
+    retrieval,
+    boundary,
+    grad_tags,
+):
+    tok_rows, width = slab_tokens.shape
+    mem_rows = memory.shape[0]
+    query_width = query_weight.shape[1]
+    heads = query_width // HD
+    spans = tok_rows // BLK
+    blocks = mem_rows // BLK
+    peers = lax.axis_size("tm")
+    f32 = jnp.float32
+    bf16 = jnp.bfloat16
+    mem_cuts, tok_cuts = 2, 2
+
+    mem_parts = [gather_parts(m) for m in jnp.split(memory, mem_cuts, 0)]
+    tok_parts = [gather_parts(x) for x in jnp.split(slab_tokens, tok_cuts, 0)]
+
+    named = retrieval[0]
+    owner_ids = jnp.arange(peers, dtype=jnp.int32)
+    wanted = jnp.sum(
+        jnp.where(named[None, :] // blocks == owner_ids[:, None], named[None, :] % blocks, 0), axis=1
+    ).astype(jnp.int32)
+    asked = lax.all_to_all(wanted, "tm", split_axis=0, concat_axis=0, tiled=True)
+    place = lax.axis_index("heads").astype(jnp.int32).reshape(1)
+    me = lax.axis_index("tm").astype(jnp.int32).reshape(1)
+
+    tag_t = tag_weight.T
+    tags = tag_t.shape[0]
+    wide_tag = tag_t.astype(f32)
+    grad_t = lax.dot_general(
+        wide_tag, grad_tags, (((0,), (1,)), ((), ())), precision=HIGHEST
+    ).astype(bf16)
+    grad = lax.dot_general(grad_tags, wide_tag, (((1,), (0,)), ((), ())), precision=HIGHEST).astype(bf16)
+
+    cut_rows = mem_rows // mem_cuts
+    cut_blocks = blocks // mem_cuts
+    before = []
+    for t in range(mem_cuts):
+        last = t == mem_cuts - 1
+        args = [place, me, asked, *mem_parts[t], key_weight, value_weight, value_down, value_up]
+        if last:
+            args.append(jnp.concatenate(before, 0) if len(before) > 1 else before[0])
+            out_shape = [shaped(PACK, HD, dtype=bf16)] * peers
+            scratch = [pltpu.VMEM((blocks, PACK, HD), bf16)]
+        else:
+            out_shape = shaped(cut_blocks, PACK, HD, dtype=bf16)
+            scratch = []
+        result = run(
+            lambda *refs, last=last: memory_kernel(peers, last, *refs),
+            "memory_pairs",
+            out_shape,
+            [smem()] * 3 + [vmem()] * (len(args) - 3),
+            scratch,
+            flops=2 * cut_rows * 4 * width * 3 * HD,
+            moved=8 * cut_rows * width + 16 * width * HD,
+        )(*args)
+        before.append(result)
+    outgoing = before[-1]
+    got = [outgoing[0]] + [swap(outgoing[d], d, "tm") for d in range(1, peers)]
+
+    rows = tok_rows // tok_cuts
+    anywhere = pl.BlockSpec(memory_space=pl.ANY)
+    parts = []
+    for t in range(tok_cuts):
+        parts += run(
+            project_kernel,
+            "project_span_rows",
+            (
+                shaped(rows, query_width, dtype=bf16),
+                shaped(rows, HD, dtype=bf16),
+                shaped(rows, HD, dtype=bf16),
+                shaped(2 * RANK, rows, dtype=bf16),
+            ),
+            [smem()] + [vmem()] * 4 + [anywhere] * 5 + [vmem()] * 2,
+            [
+                pltpu.VMEM((4, width, query_width), bf16),
+                pltpu.VMEM((4, width, HD), bf16),
+                pltpu.VMEM((4, width, HD), bf16),
+                pltpu.VMEM((4, RANK, width), bf16),
+                pltpu.VMEM((4, RANK, width), bf16),
+                pltpu.SemaphoreType.DMA((4, 5)),
+            ],
+            flops=2 * rows * 4 * width * (query_width + 3 * HD),
+            moved=8 * width * (rows + query_width + 3 * HD),
+        )(place, *tok_parts[t], query_weight, key_weight, value_weight, query_down, value_down, query_up, value_up)
+
+    seen = peers * BLK
+    total = seen + BLK
+    cot, ups, *mcot = run(
+        lambda *refs: attention_kernel(tok_cuts, peers, heads, *refs),
+        "span_attention",
+        [shaped(2 * RANK + tags, tok_rows), shaped(RANK, query_width + HD)] + [shaped(RANK, BLK)] * peers,
+        [smem()] + [vmem()] * (4 * tok_cuts + peers + 5),
+        [
+            pltpu.VMEM((tok_rows, query_width), bf16),
+            pltpu.VMEM((tok_rows, HD), bf16),
+            pltpu.VMEM((tok_rows, HD), bf16),
+            pltpu.VMEM((2 * RANK, tok_rows), bf16),
+            pltpu.VMEM((total, HD), bf16),
+            pltpu.VMEM((total, HD), bf16),
+            pltpu.VMEM((HD, total), bf16),
+            pltpu.VMEM((HD, total), bf16),
+            pltpu.VMEM((BLK, BLK), f32),
+            pltpu.VMEM((2, BLK, total), f32),
+            pltpu.VMEM((2, BLK, total), f32),
+            pltpu.VMEM((3, BLK, total), f32),
+            pltpu.VMEM((heads * BLK, total), bf16),
+            pltpu.VMEM((2, BLK, total), bf16),
+            pltpu.VMEM((BLK, query_width), bf16),
+            pltpu.VMEM((BLK, query_width), bf16),
+            pltpu.VMEM((HD, seen), f32),
+        ],
+        flops=20 * tok_rows * query_width * total,
+        moved=4 * tok_rows * query_width,
+    )(boundary, *parts, *got, query_up, value_up, tag_t, grad, grad_t)
+
+    back = [mcot[0]] + [swap(mcot[d], d, "tm") for d in range(1, peers)]
+    cots = [cot] + [swap(cot, d) for d in range(1, 4)]
+    bit = 1
+    while bit < peers:
+        ups = ups + swap(ups, bit, "tm")
+        bit *= 2
+    own = run(
+        lambda *refs: own_kernel(peers, *refs),
+        "owned_cotangent",
+        shaped(RANK, mem_rows),
+        [smem()] * 2 + [vmem()] * peers,
+        [pltpu.VMEM((blocks, RANK, BLK), f32)],
+    )(me, asked, *back)
+    owns = [own] + [swap(own, d) for d in range(1, 4)]
+    each = -(-2 * (width // HD) // peers)
+    logits, *pieces = run(
+        lambda *refs: down_kernel(peers, *refs),
+        "down_gradients",
+        [shaped(tags, tok_rows)] + [shaped(each, RANK, HD)] * peers,
+        [smem()] + [vmem()] * 10,
+        [pltpu.VMEM((peers, each, RANK, HD), f32)],
+        flops=6 * RANK * tok_rows * width,
+        moved=4 * tok_rows * width,
+    )(me, *cots, *owns, slab_tokens, memory)
+    pieces = [pieces[0]] + [swap(pieces[d], d, "tm") for d in range(1, peers)]
+    share = run(
+        lambda *refs: share_kernel(peers, *refs), "share_sum", shaped(each, RANK, HD), [vmem()] * peers
+    )(*pieces)
+    shares = [share] + [swap(share, d, "tm") for d in range(1, peers)]
+    query_down_grad, query_up_grad, value_down_grad, value_up_grad = run(
+        lambda *refs: finish_kernel(peers, *refs),
+        "finish_outputs",
+        (shaped(RANK, width), shaped(RANK, query_width), shaped(RANK, width), shaped(RANK, HD)),
+        [smem()] + [vmem()] * (peers + 1),
+        [pltpu.VMEM((peers, each, RANK, HD), f32)],
+    )(me, *shares, ups)
+    return (logits.T, query_down_grad, query_up_grad, value_down_grad, value_up_grad)
+
+
 def solution(mesh):
     in_specs = (
         P("tm", "heads"),
@@ -245,4 +700,6 @@
         P(None, "heads"),
         P(None, "heads"),
     )
+    fits = mesh.shape["heads"] == 4 and mesh.shape["tm"] * CAP == TOP
+    local = fast if fits else general
     return jax.shard_map(local, mesh=mesh, in_specs=in_specs, out_specs=out_specs, check_vma=False)

time: 274 us -> 165 us (0.60)
  waiting for transfers between devices: 113 us -> 41.2 us
  matrix products: 67.4 us -> 3.79 us
  starting transfers between devices: 18.8 us -> 65.1 us
  Pallas kernels: 0 us -> 45.5 us
  local copies, waits for them, and re-layouts: 37 us -> 6.65 us
  between operations: 14.2 us -> 0.97 us
  blocking collectives: 12.3 us -> 0 us
  other arithmetic: 11 us -> 1.07 us
    psum x1 -> x0, waiting for transfers between devices: 69.7 us -> none  [local(): lax.psum((query_down_grad, query_up_grad, value_down_grad, value_up_grad)...]
    dot_general x26 -> x2, matrix products: 67.4 us -> 3.79 us  [the longest x1 1.92 us: fast(): lax.dot_general(wide_tag, grad_tags, (((0,), (1,)), ((), ())), precision=...]
    ppermute x0 -> x49, starting transfers between devices: none -> 59.3 us  [swap(): lax.ppermute(x, axis, [(i, i ^ bit) for i in range(lax.axis_size(axis))])]
    pallas_call x0 -> x9, Pallas kernels: none -> 45.5 us  [the longest x1 21.8 us: fast(): run(lambda *refs: attention_kernel(tok_cuts, peers, heads, *refs), 'span_...]
    ppermute x0 -> x49, waiting for transfers between devices: none -> 41.2 us  [swap(): lax.ppermute(x, axis, [(i, i ^ bit) for i in range(lax.axis_size(axis))])]
    all_gather x2 -> x0, waiting for transfers between devices: 30.6 us -> none  [the longest x1 18.7 us: local(): token_piece = lax.all_gather(slab_tokens, 'heads', axis=1, tiled=True)]
    all_to_all x3 -> x1, starting transfers between devices: 18.4 us -> 5.81 us  [fast(): lax.all_to_all(wanted, 'tm', split_axis=0, concat_axis=0, tiled=True)]
    psum x1 -> x0, blocking collectives: 12.3 us -> none  [local(): lax.psum(jnp.dot(attended, tag_weight, preferred_element_type=jnp.float32...]
  transfers between devices with their start and end apart: 6 -> 50, of which waited for: 4 -> 14; matrix products, arithmetic and copies ran while one was open for 17% -> 4% of each run, Pallas kernels for 0% -> 14%
where the time goes in v2:
time: 165 us; the launch traced here: 164 us
  starting transfers between devices  65.1 us (39%)
  Pallas kernels  45.5 us (28%)
  waiting for transfers between devices  41.2 us (25%)
  local copies, waits for them, and re-layouts  6.65 us (4%)
  matrix products  3.79 us (2%)
    ppermute x49, starting transfers between devices, swap(): lax.ppermute(x, axis, [(i, i ^ bit) for i in range(lax.axis_size(axis))])  59.3 us
    ppermute x49, waiting for transfers between devices, swap(): lax.ppermute(x, axis, [(i, i ^ bit) for i in range(lax.axis_size(axis))])  41.2 us
    pallas_call x1, Pallas kernels, fast(): run(lambda *refs: attention_kernel(tok_cuts, peers, heads, *refs), 'span_...  21.8 us
    pallas_call x2, Pallas kernels, fast(): run(project_kernel, 'project_span_rows', (shaped(rows, query_width, dtype...  16.4 us
    all_to_all x1, starting transfers between devices, fast(): lax.all_to_all(wanted, 'tm', split_axis=0, concat_axis=0, tiled=True)  5.81 us
    pallas_call x2, Pallas kernels, fast(): run(lambda *refs, last=last: memory_kernel(peers, last, *refs), 'memory_p...  5.09 us
    unnamed x34, local copies, waits for them, and re-layouts  3.64 us
  transfers between devices with their start and end apart: 50, of which 14 were waited for; matrix products, arithmetic and copies ran while one was open for 4% of the time, Pallas kernels for 14%

profile of v2, /device:TPU:0, one launch (start us, length us, event | category | flops | bytes accessed | tf_op | source)
XLA Modules:
  0.0 164.3 jit_solution(2910812446424109533)
XLA Ops:
  0.7 1.3 fusion.2
  2.0 3.0 %collective-permute-start.10 = (bf16[256,896]{1,0:T(8,128)(2,1)S(1)}, bf16[256,896]{1,0:T(8,128)(2,1)}, u32[]{:S(2)}, u32[]{:S(2)}) collective-permute-start(bf16[256,896]{1,0:T(8,128)(2,1)S(1)} %get-tuple-element.85.refs_3_), channel_id=1, source_target_pairs={{0,2},{1,3},{2,0},{3,1},{4,6},{5,7},{6,4},{7,5},{8,10},{9,11},{10,... | collective-permute-start | bytes 1376264 | tf_op jit(solution)/shard_map/ppermute | solution.py:478
  5.0 0.8 copy-done.5
  6.5 1.0 fusion.3
  7.5 1.7 %collective-permute-start.4 = (bf16[256,896]{1,0:T(8,128)(2,1)}, bf16[256,896]{1,0:T(8,128)(2,1)}, u32[]{:S(2)}, u32[]{:S(2)}) collective-permute-start(bf16[256,896]{1,0:T(8,128)(2,1)} %get-tuple-element.87.x0), channel_id=1, source_target_pairs={{0,2},{1,3},{2,0},{3,1},{4,6},{5,7},{6,4},{7,5},{8,10},{9,11},{10,... | collective-permute-start | bytes 1376264 | tf_op jit(solution)/shard_map/ppermute | solution.py:478
  9.1 0.7 fusion.1
  9.8 6.6 %collective-permute-done.10.refs_5_ = bf16[256,896]{1,0:T(8,128)(2,1)} collective-permute-done((bf16[256,896]{1,0:T(8,128)(2,1)S(1)}, bf16[256,896]{1,0:T(8,128)(2,1)}, u32[]{:S(2)}, u32[]{:S(2)}) %collective-permute-start.10) | collective-permute-done | bytes 458784 | tf_op jit(solution)/shard_map/ppermute | solution.py:478
  16.5 2.1 %collective-permute-start.1 = (bf16[256,896]{1,0:T(8,128)(2,1)}, bf16[256,896]{1,0:T(8,128)(2,1)}, u32[]{:S(2)}, u32[]{:S(2)}) collective-permute-start(bf16[256,896]{1,0:T(8,128)(2,1)} %get-tuple-element.88.x0), channel_id=1, source_target_pairs={{0,2},{1,3},{2,0},{3,1},{4,6},{5,7},{6,4},{7,5},{8,10},{9,11},{10,... | collective-permute-start | bytes 1376264 | tf_op jit(solution)/shard_map/ppermute | solution.py:478
  18.5 0.8 copy-done.10
  19.4 0.7 copy.20
  20.1 5.8 %all-to-all-start = ((s32[8,1,1]{2,1,0:T(1,128)}), s32[8,1,1]{2,1,0:T(1,128)S(1)}, u32[]{:S(2)}, u32[]{:S(2)}) async-start(s32[8,1,1]{2,1,0:T(1,128)} %copy.20), calls=%async_computation | async-start | bytes 8192 | tf_op jit(solution)/shard_map/all_to_all | solution.py:547
  26.3 0.5 collective-permute-start.8
  26.8 9.3 %collective-permute-done.4.x2 = bf16[256,896]{1,0:T(8,128)(2,1)} collective-permute-done((bf16[256,896]{1,0:T(8,128)(2,1)}, bf16[256,896]{1,0:T(8,128)(2,1)}, u32[]{:S(2)}, u32[]{:S(2)}) %collective-permute-start.4) | collective-permute-done | bytes 458784 | tf_op jit(solution)/shard_map/ppermute | solution.py:478
  36.1 1.9 %convolution_convert_fusion.refs_21_ = bf16[896,512]{1,0:T(8,128)(2,1)} fusion(bf16[896,8]{0,1:T(8,128)(2,1)S(1)} %copy-done.15, f32[512,8]{0,1:T(8,128)S(1)} %copy-done), kind=kOutput, calls=%fused_computation | convolution fusion | flops 44498944 | bytes 948224 | tf_op jit(solution)/shard_map/dot_general | solution.py:554
  38.1 7.1 %collective-permute-done.1.x2 = bf16[256,896]{1,0:T(8,128)(2,1)} collective-permute-done((bf16[256,896]{1,0:T(8,128)(2,1)}, bf16[256,896]{1,0:T(8,128)(2,1)}, u32[]{:S(2)}, u32[]{:S(2)}) %collective-permute-start.1) | collective-permute-done | bytes 458784 | tf_op jit(solution)/shard_map/ppermute | solution.py:478
  45.1 0.5 collective-permute-start.2
  45.6 1.9 %convolution_convert_fusion.1.refs_20_ = bf16[512,896]{1,0:T(8,128)(2,1)} fusion(f32[512,8]{0,1:T(8,128)S(1)} %copy-done, bf16[896,8]{0,1:T(8,128)(2,1)S(1)} %copy-done.15), kind=kOutput, calls=%fused_computation.1 | convolution fusion | flops 44498944 | bytes 948224 | tf_op jit(solution)/shard_map/dot_general | solution.py:557
  47.8 1.0 copy-done.6
  48.8 1.0 copy-done.11
  49.8 2.4 %memory_pairs.2.refs_11_ = bf16[2,272,128]{2,1,0:T(8,128)(2,1)S(1)} custom-call(s32[1]{0:T(128)} %bitcast.1.place_ref.refs_0_, s32[1]{0:T(128)} %bitcast.refs_1_.refs_0_, s32[8]{0:T(128)S(1)} %reduce.refs_2_.refs_1_, bf16[256,896]{1,0:T(8,128)(2,1)S(1)} %copy-done.6, bf16[256,896]{1,0:T(8,128)(2,1)S(1)} %copy-done.11, ...), custom_call_target="tpu_custom_call" | custom-call | flops 704643072 | bytes 3670016 | tf_op jit(solution)/shard_map/memory_pairs/pallas_call | solution.py:572
  52.3 2.7 %memory_pairs.3 = (bf16[272,128]{1,0:T(8,128)(2,1)S(1)}, bf16[272,128]{1,0:T(8,128)(2,1)S(1)}, bf16[272,128]{1,0:T(8,128)(2,1)S(1)}, bf16[272,128]{1,0:T(8,128)(...) custom-call(s32[1]{0:T(128)} %bitcast.1.place_ref.refs_0_, ...), custom_call_target="tpu_custom_call" | custom-call | flops 704643072 | bytes 3670016 | tf_op jit(solution)/shard_map/memory_pairs/pallas_call | solution.py:572
  55.0 1.8 %collective-permute-start.12 = (bf16[272,128]{1,0:T(8,128)(2,1)S(1)}, bf16[272,128]{1,0:T(8,128)(2,1)S(1)}, u32[]{:S(2)}, u32[]{:S(2)}) collective-permute-start(bf16[272,128]{1,0:T(8,128)(2,1)S(1)} %get-tuple-element.53), channel_id=1, source_target_pairs={{0,4},{4,0},{8,12},{12,8},{16,20},{20,16},{24,28},{28,24},{1,5},{5... | collective-permute-start | bytes 208904 | tf_op jit(solution)/shard_map/ppermute | solution.py:478
  56.8 1.6 collective-permute-start.13
  58.5 8.2 %project_span_rows.3 = (bf16[256,896]{1,0:T(8,128)(2,1)S(1)}, bf16[256,128]{1,0:T(8,128)(2,1)S(1)}, bf16[256,128]{1,0:T(8,128)(2,1)S(1)}, bf16[32,256]{1,0:T(8,128)(2,1)S(1)}) custom-call(s32[1]{0:T(128)} %bitcast.1.place_ref.refs_0_, bf16[256,896]{1,0:T(8,128)(2,1)} %get-tuple-element.87.x0, bf16[256,896]{1,0:T(8,128)(2,1)} %collective-permute-done.3.x1, ...), custom_call_target="tpu_custom_call" | custom-call | flops 2348810240 | bytes 11010048 | tf_op jit(solution)/shard_map/project_span_rows/pallas_call | solution.py:589
  66.7 2.9 %collective-permute-start.15 = (bf16[272,128]{1,0:T(8,128)(2,1)S(1)}, bf16[272,128]{1,0:T(8,128)(2,1)S(1)}, u32[]{:S(2)}, u32[]{:S(2)}) collective-permute-start(bf16[272,128]{1,0:T(8,128)(2,1)S(1)} %get-tuple-element.56), channel_id=1, source_target_pairs={{0,16},{4,20},{8,24},{12,28},{16,0},{20,4},{24,8},{28,12},{1,17},{... | collective-permute-start | bytes 208904 | tf_op jit(solution)/shard_map/ppermute | solution.py:478
  69.6 1.3 collective-permute-start.16
  70.9 3.6 %collective-permute-start.17 = (bf16[272,128]{1,0:T(8,128)(2,1)S(1)}, bf16[272,128]{1,0:T(8,128)(2,1)S(1)}, u32[]{:S(2)}, u32[]{:S(2)}) collective-permute-start(bf16[272,128]{1,0:T(8,128)(2,1)S(1)} %get-tuple-element.58), channel_id=1, source_target_pairs={{0,24},{4,28},{8,16},{12,20},{16,8},{20,12},{24,0},{28,4},{1,25},{... | collective-permute-start | bytes 208904 | tf_op jit(solution)/shard_map/ppermute | solution.py:478
  74.6 8.3 %project_span_rows.2 = (bf16[256,896]{1,0:T(8,128)(2,1)S(1)}, bf16[256,128]{1,0:T(8,128)(2,1)S(1)}, bf16[256,128]{1,0:T(8,128)(2,1)S(1)}, bf16[32,256]{1,0:T(8,128)(2,1)S(1)}) custom-call(s32[1]{0:T(128)} %bitcast.1.place_ref.refs_0_, bf16[256,896]{1,0:T(8,128)(2,1)} %get-tuple-element.88.x0, bf16[256,896]{1,0:T(8,128)(2,1)} %collective-permute-done.x1, ...), custom_call_target="tpu_custom_call" | custom-call | flops 2348810240 | bytes 11010048 | tf_op jit(solution)/shard_map/project_span_rows/pallas_call | solution.py:589
  83.0 21.8 %span_attention.1 = (f32[40,512]{1,0:T(8,128)S(1)}, f32[16,1024]{1,0:T(8,128)S(1)}, f32[16,128]{1,0:T(8,128)S(1)}, f32[16,128]{1,0:T(8,128)S(1)}, f32[16,128]{1,...) custom-call(s32[4]{0:T(128)S(1)} %copy-done.16, ...), custom_call_target="tpu_custom_call" | custom-call | flops 10569646080 | bytes 1835008 | tf_op jit(solution)/shard_map/span_attention/pallas_call | solution.py:613
  104.8 1.6 collective-permute-start.46
  106.8 2.2 %collective-permute-done.46 = f32[16,1024]{1,0:T(8,128)S(1)} collective-permute-done((f32[16,1024]{1,0:T(8,128)S(1)}, f32[16,1024]{1,0:T(8,128)S(1)}, u32[]{:S(2)}, u32[]{:S(2)}) %collective-permute-start.46) | collective-permute-done | bytes 65568 | tf_op jit(solution)/shard_map/ppermute | solution.py:478
  109.1 0.5 collective-permute-start.47
  109.6 1.6 collective-permute-start.23
  111.2 1.1 collective-permute-start.24
  112.2 4.1 %collective-permute-start.25 = (f32[16,128]{1,0:T(8,128)S(1)}, f32[16,128]{1,0:T(8,128)S(1)}, u32[]{:S(2)}, u32[]{:S(2)}) collective-permute-start(f32[16,128]{1,0:T(8,128)S(1)} %get-tuple-element.65), channel_id=1, source_target_pairs={{0,16},{4,20},{8,24},{12,28},{16,0},{20,4},{24,8},{28,12},{1,17},{... | collective-permute-start | bytes 24584 | tf_op jit(solution)/shard_map/ppermute | solution.py:478
  116.3 2.4 %collective-permute-start.27 = (f32[16,128]{1,0:T(8,128)S(1)}, f32[16,128]{1,0:T(8,128)S(1)}, u32[]{:S(2)}, u32[]{:S(2)}) collective-permute-start(f32[16,128]{1,0:T(8,128)S(1)} %get-tuple-element.67), channel_id=1, source_target_pairs={{0,24},{4,28},{8,16},{12,20},{16,8},{20,12},{24,0},{28,4},{1,25},{... | collective-permute-start | bytes 24584 | tf_op jit(solution)/shard_map/ppermute | solution.py:478
  118.7 2.3 %collective-permute-start.28 = (f32[16,128]{1,0:T(8,128)S(1)}, f32[16,128]{1,0:T(8,128)S(1)}, u32[]{:S(2)}, u32[]{:S(2)}) collective-permute-start(f32[16,128]{1,0:T(8,128)S(1)} %get-tuple-element.68), channel_id=1, source_target_pairs={{0,28},{4,24},{8,20},{12,16},{16,12},{20,8},{24,4},{28,0},{1,29},{... | collective-permute-start | bytes 24584 | tf_op jit(solution)/shard_map/ppermute | solution.py:478
  121.1 0.7 collective-permute-done.26.refs_7_
  121.8 1.5 collective-permute-start.20
  123.3 1.8 %collective-permute-done.28.refs_9_ = f32[16,128]{1,0:T(8,128)S(1)} collective-permute-done((f32[16,128]{1,0:T(8,128)S(1)}, f32[16,128]{1,0:T(8,128)S(1)}, u32[]{:S(2)}, u32[]{:S(2)}) %collective-permute-start.28) | collective-permute-done | bytes 8224 | tf_op jit(solution)/shard_map/ppermute | solution.py:478
  125.1 0.6 owned_cotangent.1.refs_5_
  125.7 1.2 collective-permute-done.29.refs_6_
  126.9 1.6 collective-permute-start.30
  128.5 2.3 %collective-permute-done.30.refs_7_ = f32[16,512]{1,0:T(8,128)S(1)} collective-permute-done((f32[16,512]{1,0:T(8,128)S(1)}, f32[16,512]{1,0:T(8,128)S(1)}, u32[]{:S(2)}, u32[]{:S(2)}) %collective-permute-start.30) | collective-permute-done | bytes 32800 | tf_op jit(solution)/shard_map/ppermute | solution.py:478
  130.9 1.3 collective-permute-done.31.refs_8_
  132.2 0.9 down_gradients.1
  133.1 1.5 collective-permute-start.32
  134.6 0.7 collective-permute-start.33
  135.3 1.3 collective-permute-start.34
  136.6 1.6 collective-permute-start.35
  138.2 2.2 %collective-permute-start.36 = (f32[2,16,128]{2,1,0:T(8,128)S(1)}, f32[2,16,128]{2,1,0:T(8,128)S(1)}, u32[]{:S(2)}, u32[]{:S(2)}) collective-permute-start(f32[2,16,128]{2,1,0:T(8,128)S(1)} %get-tuple-element.75), channel_id=1, source_target_pairs={{0,20},{4,16},{8,28},{12,24},{16,4},{20,0},{24,12},{28,8},{1,21},{... | collective-permute-start | bytes 49160 | tf_op jit(solution)/shard_map/ppermute | solution.py:478
  140.5 1.4 collective-permute-start.37
  141.8 2.4 %collective-permute-start.38 = (f32[2,16,128]{2,1,0:T(8,128)S(1)}, f32[2,16,128]{2,1,0:T(8,128)S(1)}, u32[]{:S(2)}, u32[]{:S(2)}) collective-permute-start(f32[2,16,128]{2,1,0:T(8,128)S(1)} %get-tuple-element.77), channel_id=1, source_target_pairs={{0,28},{4,24},{8,20},{12,16},{16,12},{20,8},{24,4},{28,0},{1,29},{... | collective-permute-start | bytes 49160 | tf_op jit(solution)/shard_map/ppermute | solution.py:478
  144.3 1.7 %collective-permute-done.37.refs_6_ = f32[2,16,128]{2,1,0:T(8,128)S(1)} collective-permute-done((f32[2,16,128]{2,1,0:T(8,128)S(1)}, f32[2,16,128]{2,1,0:T(8,128)S(1)}, u32[]{:S(2)}, u32[]{:S(2)}) %collective-permute-start.37) | collective-permute-done | bytes 16416 | tf_op jit(solution)/shard_map/ppermute | solution.py:478
  146.0 2.3 %collective-permute-done.38.refs_7_ = f32[2,16,128]{2,1,0:T(8,128)S(1)} collective-permute-done((f32[2,16,128]{2,1,0:T(8,128)S(1)}, f32[2,16,128]{2,1,0:T(8,128)S(1)}, u32[]{:S(2)}, u32[]{:S(2)}) %collective-permute-start.38) | collective-permute-done | bytes 16416 | tf_op jit(solution)/shard_map/ppermute | solution.py:478
  148.3 0.7 collective-permute-start.39
  149.0 2.9 %collective-permute-start.41 = (f32[2,16,128]{2,1,0:T(8,128)S(1)}, f32[2,16,128]{2,1,0:T(8,128)S(1)}, u32[]{:S(2)}, u32[]{:S(2)}) collective-permute-start(f32[2,16,128]{2,1,0:T(8,128)S(1)} %share_sum.1.refs_1_), channel_id=1, source_target_pairs={{0,12},{4,8},{8,4},{12,0},{16,28},{20,24},{24,20},{28,16},{1,13},{... | collective-permute-start | bytes 49160 | tf_op jit(solution)/shard_map/ppermute | solution.py:478
  151.9 1.0 collective-permute-start.42
  152.8 2.0 %collective-permute-start.43 = (f32[2,16,128]{2,1,0:T(8,128)S(1)}, f32[2,16,128]{2,1,0:T(8,128)S(1)}, u32[]{:S(2)}, u32[]{:S(2)}) collective-permute-start(f32[2,16,128]{2,1,0:T(8,128)S(1)} %share_sum.1.refs_1_), channel_id=1, source_target_pairs={{0,20},{4,16},{8,28},{12,24},{16,4},{20,0},{24,12},{28,8},{1,21},{... | collective-permute-start | bytes 49160 | tf_op jit(solution)/shard_map/ppermute | solution.py:478
  154.9 2.3 %collective-permute-start.44 = (f32[2,16,128]{2,1,0:T(8,128)S(1)}, f32[2,16,128]{2,1,0:T(8,128)S(1)}, u32[]{:S(2)}, u32[]{:S(2)}) collective-permute-start(f32[2,16,128]{2,1,0:T(8,128)S(1)} %share_sum.1.refs_1_), channel_id=1, source_target_pairs={{0,24},{4,28},{8,16},{12,20},{16,8},{20,12},{24,0},{28,4},{1,25},{... | collective-permute-start | bytes 49160 | tf_op jit(solution)/shard_map/ppermute | solution.py:478
  157.2 2.3 %collective-permute-start.45 = (f32[2,16,128]{2,1,0:T(8,128)S(1)}, f32[2,16,128]{2,1,0:T(8,128)S(1)}, u32[]{:S(2)}, u32[]{:S(2)}) collective-permute-start(f32[2,16,128]{2,1,0:T(8,128)S(1)} %share_sum.1.refs_1_), channel_id=1, source_target_pairs={{0,28},{4,24},{8,20},{12,16},{16,12},{20,8},{24,4},{28,0},{1,29},{... | collective-permute-start | bytes 49160 | tf_op jit(solution)/shard_map/ppermute | solution.py:478
  159.6 0.8 collective-permute-done.44.refs_7_
  160.4 3.2 %collective-permute-done.45.refs_8_ = f32[2,16,128]{2,1,0:T(8,128)S(1)} collective-permute-done((f32[2,16,128]{2,1,0:T(8,128)S(1)}, f32[2,16,128]{2,1,0:T(8,128)S(1)}, u32[]{:S(2)}, u32[]{:S(2)}) %collective-permute-start.45) | collective-permute-done | bytes 16416 | tf_op jit(solution)/shard_map/ppermute | solution.py:478
  163.6 0.7 finish_outputs.1
  (91 shorter events, 2.4 us)
Async XLA Ops:
  0.6 35.5 %copy-start = (f32[512,8]{0,1:T(8,128)S(1)}, f32[512,8]{0,1:T(8,128)}, u32[]{:S(2)}) copy-start(f32[512,8]{0,1:T(8,128)} %param.25) | copy-start | bytes 49156
  0.6 5.8 %copy-start.3 = (bf16[512,896]{1,0:T(8,128)(2,1)S(1)}, bf16[512,896]{1,0:T(8,128)(2,1)}, u32[]{:S(2)}) copy-start(bf16[512,896]{1,0:T(8,128)(2,1)} %refs_9_.5) | copy-start | bytes 2752516
  0.7 35.5 %copy-start.15 = (bf16[896,8]{0,1:T(8,128)(2,1)S(1)}, bf16[896,8]{0,1:T(8,128)(2,1)}, u32[]{:S(2)}) copy-start(bf16[896,8]{0,1:T(8,128)(2,1)} %param.22) | copy-start | bytes 43012
  2.0 14.5 %collective-permute-start.10 = (bf16[256,896]{1,0:T(8,128)(2,1)S(1)}, bf16[256,896]{1,0:T(8,128)(2,1)}, u32[]{:S(2)}, u32[]{:S(2)}) collective-permute-start(bf16[256,896]{1,0:T(8,128)(2,1)S(1)} %get-tuple-element.85.refs_3_), channel_id=1, source_target_pairs={{0,2},{1,3},{2,0},{3,1},{4,6},{5,7},{6,4},{7,5},{8,10},{9,11},{10,... | collective-permute-start | bytes 1376264 | tf_op jit(solution)/shard_map/ppermute | solution.py:478
  5.0 13.5 %collective-permute-start.9 = (bf16[256,896]{1,0:T(8,128)(2,1)S(1)}, bf16[256,896]{1,0:T(8,128)(2,1)S(1)}, u32[]{:S(2)}, u32[]{:S(2)}) collective-permute-start(bf16[256,896]{1,0:T(8,128)(2,1)S(1)} %get-tuple-element.85.refs_3_), channel_id=1, source_target_pairs={{0,1},{1,0},{2,3},{3,2},{4,5},{5,4},{6,7},{7,6},{8,9},{9,8},{10,11... | collective-permute-start | bytes 1376264 | tf_op jit(solution)/shard_map/ppermute | solution.py:478
  5.8 42.0 %copy-start.1 = (bf16[3584,128]{1,0:T(8,128)(2,1)S(1)}, bf16[3584,128]{1,0:T(8,128)(2,1)}, u32[]{:S(2)}) copy-start(bf16[3584,128]{1,0:T(8,128)(2,1)} %refs_7_.3) | copy-start | bytes 2752516
  5.8 42.0 %copy-start.2 = (bf16[3584,128]{1,0:T(8,128)(2,1)S(1)}, bf16[3584,128]{1,0:T(8,128)(2,1)}, u32[]{:S(2)}) copy-start(bf16[3584,128]{1,0:T(8,128)(2,1)} %refs_8_.3) | copy-start | bytes 2752516
  5.8 42.0 %copy-start.7 = (bf16[16,3584]{1,0:T(8,128)(2,1)S(1)}, bf16[16,3584]{1,0:T(8,128)(2,1)}, u32[]{:S(2)}) copy-start(bf16[16,3584]{1,0:T(8,128)(2,1)} %refs_9_.4) | copy-start | bytes 344068
  5.8 42.0 %copy-start.14 = (bf16[16,128]{1,0:T(8,128)(2,1)S(1)}, bf16[16,128]{1,0:T(8,128)(2,1)}, u32[]{:S(2)}) copy-start(bf16[16,128]{1,0:T(8,128)(2,1)} %refs_18_.1) | copy-start | bytes 12292
  5.8 20.5 %collective-permute-start.7 = (bf16[256,896]{1,0:T(8,128)(2,1)S(1)}, bf16[256,896]{1,0:T(8,128)(2,1)}, u32[]{:S(2)}, u32[]{:S(2)}) collective-permute-start(bf16[256,896]{1,0:T(8,128)(2,1)S(1)} %get-tuple-element.86.refs_3_), channel_id=1, source_target_pairs={{0,2},{1,3},{2,0},{3,1},{4,6},{5,7},{6,4},{7,5},{8,10},{9,11},{10,... | collective-permute-start | bytes 1376264 | tf_op jit(solution)/shard_map/ppermute | solution.py:478
  6.0 20.3 %collective-permute-start.6 = (bf16[256,896]{1,0:T(8,128)(2,1)S(1)}, bf16[256,896]{1,0:T(8,128)(2,1)}, u32[]{:S(2)}, u32[]{:S(2)}) collective-permute-start(bf16[256,896]{1,0:T(8,128)(2,1)S(1)} %get-tuple-element.86.refs_3_), channel_id=1, source_target_pairs={{0,1},{1,0},{2,3},{3,2},{4,5},{5,4},{6,7},{7,6},{8,9},{9,8},{10,11... | collective-permute-start | bytes 1376264 | tf_op jit(solution)/shard_map/ppermute | solution.py:478
  7.5 28.7 %collective-permute-start.4 = (bf16[256,896]{1,0:T(8,128)(2,1)}, bf16[256,896]{1,0:T(8,128)(2,1)}, u32[]{:S(2)}, u32[]{:S(2)}) collective-permute-start(bf16[256,896]{1,0:T(8,128)(2,1)} %get-tuple-element.87.x0), channel_id=1, source_target_pairs={{0,2},{1,3},{2,0},{3,1},{4,6},{5,7},{6,4},{7,5},{8,10},{9,11},{10,... | collective-permute-start | bytes 1376264 | tf_op jit(solution)/shard_map/ppermute | solution.py:478
  16.5 28.7 %collective-permute-start.1 = (bf16[256,896]{1,0:T(8,128)(2,1)}, bf16[256,896]{1,0:T(8,128)(2,1)}, u32[]{:S(2)}, u32[]{:S(2)}) collective-permute-start(bf16[256,896]{1,0:T(8,128)(2,1)} %get-tuple-element.88.x0), channel_id=1, source_target_pairs={{0,2},{1,3},{2,0},{3,1},{4,6},{5,7},{6,4},{7,5},{8,10},{9,11},{10,... | collective-permute-start | bytes 1376264 | tf_op jit(solution)/shard_map/ppermute | solution.py:478
  19.3 25.8 %collective-permute-start.11 = (bf16[256,896]{1,0:T(8,128)(2,1)}, bf16[256,896]{1,0:T(8,128)(2,1)}, u32[]{:S(2)}, u32[]{:S(2)}) collective-permute-start(bf16[256,896]{1,0:T(8,128)(2,1)} %collective-permute-done.10.refs_5_), channel_id=1, source_target_pairs={{0,1},{1,0},{2,3},{3,2},{4,5},{5,4},{6,7},{7,6},{8,9},{9,8},{10,11... | collective-permute-start | bytes 1376264 | tf_op jit(solution)/shard_map/ppermute | solution.py:478
  20.1 27.4 %all-to-all-start = ((s32[8,1,1]{2,1,0:T(1,128)}), s32[8,1,1]{2,1,0:T(1,128)S(1)}, u32[]{:S(2)}, u32[]{:S(2)}) async-start(s32[8,1,1]{2,1,0:T(1,128)} %copy.20), calls=%async_computation | async-start | bytes 8192 | tf_op jit(solution)/shard_map/all_to_all | solution.py:547
  26.3 30.5 %collective-permute-start.3 = (bf16[256,896]{1,0:T(8,128)(2,1)}, bf16[256,896]{1,0:T(8,128)(2,1)}, u32[]{:S(2)}, u32[]{:S(2)}) collective-permute-start(bf16[256,896]{1,0:T(8,128)(2,1)} %get-tuple-element.87.x0), channel_id=1, source_target_pairs={{0,1},{1,0},{2,3},{3,2},{4,5},{5,4},{6,7},{7,6},{8,9},{9,8},{10,11... | collective-permute-start | bytes 1376264 | tf_op jit(solution)/shard_map/ppermute | solution.py:478
  26.3 26.0 %collective-permute-start.8 = (bf16[256,896]{1,0:T(8,128)(2,1)}, bf16[256,896]{1,0:T(8,128)(2,1)}, u32[]{:S(2)}, u32[]{:S(2)}) collective-permute-start(bf16[256,896]{1,0:T(8,128)(2,1)} %collective-permute-done.7.refs_5_), channel_id=1, source_target_pairs={{0,1},{1,0},{2,3},{3,2},{4,5},{5,4},{6,7},{7,6},{8,9},{9,8},{10,11... | collective-permute-start | bytes 1376264 | tf_op jit(solution)/shard_map/ppermute | solution.py:478
  36.1 22.2 %collective-permute-start.5 = (bf16[256,896]{1,0:T(8,128)(2,1)}, bf16[256,896]{1,0:T(8,128)(2,1)}, u32[]{:S(2)}, u32[]{:S(2)}) collective-permute-start(bf16[256,896]{1,0:T(8,128)(2,1)} %collective-permute-done.4.x2), channel_id=1, source_target_pairs={{0,1},{1,0},{2,3},{3,2},{4,5},{5,4},{6,7},{7,6},{8,9},{9,8},{10,11... | collective-permute-start | bytes 1376264 | tf_op jit(solution)/shard_map/ppermute | solution.py:478
  45.1 21.6 %collective-permute-start = (bf16[256,896]{1,0:T(8,128)(2,1)}, bf16[256,896]{1,0:T(8,128)(2,1)}, u32[]{:S(2)}, u32[]{:S(2)}) collective-permute-start(bf16[256,896]{1,0:T(8,128)(2,1)} %get-tuple-element.88.x0), channel_id=1, source_target_pairs={{0,1},{1,0},{2,3},{3,2},{4,5},{5,4},{6,7},{7,6},{8,9},{9,8},{10,11... | collective-permute-start | bytes 1376264 | tf_op jit(solution)/shard_map/ppermute | solution.py:478
  45.1 24.5 %collective-permute-start.2 = (bf16[256,896]{1,0:T(8,128)(2,1)}, bf16[256,896]{1,0:T(8,128)(2,1)}, u32[]{:S(2)}, u32[]{:S(2)}) collective-permute-start(bf16[256,896]{1,0:T(8,128)(2,1)} %collective-permute-done.1.x2), channel_id=1, source_target_pairs={{0,1},{1,0},{2,3},{3,2},{4,5},{5,4},{6,7},{7,6},{8,9},{9,8},{10,11... | collective-permute-start | bytes 1376264 | tf_op jit(solution)/shard_map/ppermute | solution.py:478
  47.8 1.0 copy-start.6
  52.3 6.3 %copy-start.12 = (bf16[16,3584]{1,0:T(8,128)(2,1)S(1)}, bf16[16,3584]{1,0:T(8,128)(2,1)}, u32[]{:S(2)}) copy-start(bf16[16,3584]{1,0:T(8,128)(2,1)} %qd_hbm.3) | copy-start | bytes 344068
  52.3 6.3 %copy-start.13 = (bf16[16,896]{1,0:T(8,128)(2,1)S(1)}, bf16[16,896]{1,0:T(8,128)(2,1)}, u32[]{:S(2)}) copy-start(bf16[16,896]{1,0:T(8,128)(2,1)} %refs_17_.1) | copy-start | bytes 86020
  55.0 15.9 %collective-permute-start.12 = (bf16[272,128]{1,0:T(8,128)(2,1)S(1)}, bf16[272,128]{1,0:T(8,128)(2,1)S(1)}, u32[]{:S(2)}, u32[]{:S(2)}) collective-permute-start(bf16[272,128]{1,0:T(8,128)(2,1)S(1)} %get-tuple-element.53), channel_id=1, source_target_pairs={{0,4},{4,0},{8,12},{12,8},{16,20},{20,16},{24,28},{28,24},{1,5},{5... | collective-permute-start | bytes 208904 | tf_op jit(solution)/shard_map/ppermute | solution.py:478
  56.8 17.7 %collective-permute-start.13 = (bf16[272,128]{1,0:T(8,128)(2,1)S(1)}, bf16[272,128]{1,0:T(8,128)(2,1)S(1)}, u32[]{:S(2)}, u32[]{:S(2)}) collective-permute-start(bf16[272,128]{1,0:T(8,128)(2,1)S(1)} %get-tuple-element.54), channel_id=1, source_target_pairs={{0,8},{4,12},{8,0},{12,4},{16,24},{20,28},{24,16},{28,20},{1,9},{5... | collective-permute-start | bytes 208904 | tf_op jit(solution)/shard_map/ppermute | solution.py:478
  58.3 24.5 %collective-permute-start.14 = (bf16[272,128]{1,0:T(8,128)(2,1)S(1)}, bf16[272,128]{1,0:T(8,128)(2,1)S(1)}, u32[]{:S(2)}, u32[]{:S(2)}) collective-permute-start(bf16[272,128]{1,0:T(8,128)(2,1)S(1)} %get-tuple-element.55), channel_id=1, source_target_pairs={{0,12},{4,8},{8,4},{12,0},{16,28},{20,24},{24,20},{28,16},{1,13},{... | collective-permute-start | bytes 208904 | tf_op jit(solution)/shard_map/ppermute | solution.py:478
  66.7 16.1 %collective-permute-start.15 = (bf16[272,128]{1,0:T(8,128)(2,1)S(1)}, bf16[272,128]{1,0:T(8,128)(2,1)S(1)}, u32[]{:S(2)}, u32[]{:S(2)}) collective-permute-start(bf16[272,128]{1,0:T(8,128)(2,1)S(1)} %get-tuple-element.56), channel_id=1, source_target_pairs={{0,16},{4,20},{8,24},{12,28},{16,0},{20,4},{24,8},{28,12},{1,17},{... | collective-permute-start | bytes 208904 | tf_op jit(solution)/shard_map/ppermute | solution.py:478
  69.6 13.3 %collective-permute-start.16 = (bf16[272,128]{1,0:T(8,128)(2,1)S(1)}, bf16[272,128]{1,0:T(8,128)(2,1)S(1)}, u32[]{:S(2)}, u32[]{:S(2)}) collective-permute-start(bf16[272,128]{1,0:T(8,128)(2,1)S(1)} %get-tuple-element.57), channel_id=1, source_target_pairs={{0,20},{4,16},{8,28},{12,24},{16,4},{20,0},{24,12},{28,8},{1,21},{... | collective-permute-start | bytes 208904 | tf_op jit(solution)/shard_map/ppermute | solution.py:478
  70.9 12.0 %collective-permute-start.17 = (bf16[272,128]{1,0:T(8,128)(2,1)S(1)}, bf16[272,128]{1,0:T(8,128)(2,1)S(1)}, u32[]{:S(2)}, u32[]{:S(2)}) collective-permute-start(bf16[272,128]{1,0:T(8,128)(2,1)S(1)} %get-tuple-element.58), channel_id=1, source_target_pairs={{0,24},{4,28},{8,16},{12,20},{16,8},{20,12},{24,0},{28,4},{1,25},{... | collective-permute-start | bytes 208904 | tf_op jit(solution)/shard_map/ppermute | solution.py:478
  74.5 8.4 %copy-start.8 = (bf16[896,512]{1,0:T(8,128)(2,1)S(1)}, bf16[896,512]{1,0:T(8,128)(2,1)}, u32[]{:S(2)}) copy-start(bf16[896,512]{1,0:T(8,128)(2,1)} %convolution_convert_fusion.refs_21_) | copy-start | bytes 2752516
  74.5 8.4 %copy-start.9 = (bf16[512,896]{1,0:T(8,128)(2,1)S(1)}, bf16[512,896]{1,0:T(8,128)(2,1)}, u32[]{:S(2)}) copy-start(bf16[512,896]{1,0:T(8,128)(2,1)} %convolution_convert_fusion.1.refs_20_) | copy-start | bytes 2752516
  74.5 8.5 %copy-start.16 = (s32[4]{0:T(128)S(1)}, s32[4]{0:T(128)}, u32[]{:S(2)}) copy-start(s32[4]{0:T(128)} %refs_0_.1) | copy-start | bytes 52
  74.5 8.4 %collective-permute-start.18 = (bf16[272,128]{1,0:T(8,128)(2,1)S(1)}, bf16[272,128]{1,0:T(8,128)(2,1)S(1)}, u32[]{:S(2)}, u32[]{:S(2)}) collective-permute-start(bf16[272,128]{1,0:T(8,128)(2,1)S(1)} %get-tuple-element.59), channel_id=1, source_target_pairs={{0,28},{4,24},{8,20},{12,16},{16,12},{20,8},{24,4},{28,0},{1,29},{... | collective-permute-start | bytes 208904 | tf_op jit(solution)/shard_map/ppermute | solution.py:478
  82.9 49.2 %copy-start.4 = (bf16[512,896]{1,0:T(8,128)(2,1)S(1)}, bf16[512,896]{1,0:T(8,128)(2,1)}, u32[]{:S(2)}) copy-start(bf16[512,896]{1,0:T(8,128)(2,1)} %refs_10_.5) | copy-start | bytes 2752516
  104.8 4.3 %collective-permute-start.46 = (f32[16,1024]{1,0:T(8,128)S(1)}, f32[16,1024]{1,0:T(8,128)S(1)}, u32[]{:S(2)}, u32[]{:S(2)}) collective-permute-start(f32[16,1024]{1,0:T(8,128)S(1)} %get-tuple-element.78), channel_id=1, source_target_pairs={{0,4},{4,0},{8,12},{12,8},{16,20},{20,16},{24,28},{28,24},{1,5},{5... | collective-permute-start | bytes 196616 | tf_op jit(solution)/shard_map/ppermute | solution.py:478
  106.3 10.0 %collective-permute-start.22 = (f32[16,128]{1,0:T(8,128)S(1)}, f32[16,128]{1,0:T(8,128)S(1)}, u32[]{:S(2)}, u32[]{:S(2)}) collective-permute-start(f32[16,128]{1,0:T(8,128)S(1)} %get-tuple-element.62), channel_id=1, source_target_pairs={{0,4},{4,0},{8,12},{12,8},{16,20},{20,16},{24,28},{28,24},{1,5},{5... | collective-permute-start | bytes 24584 | tf_op jit(solution)/shard_map/ppermute | solution.py:478
  109.1 19.4 %collective-permute-start.47 = (f32[16,1024]{1,0:T(8,128)S(1)}, f32[16,1024]{1,0:T(8,128)S(1)}, u32[]{:S(2)}, u32[]{:S(2)}) collective-permute-start(f32[16,1024]{1,0:T(8,128)S(1)} %add.17), channel_id=1, source_target_pairs={{0,8},{4,12},{8,0},{12,4},{16,24},{20,28},{24,16},{28,20},{1,9},{5... | collective-permute-start | bytes 196616 | tf_op jit(solution)/shard_map/ppermute | solution.py:478
  109.6 6.7 %collective-permute-start.23 = (f32[16,128]{1,0:T(8,128)S(1)}, f32[16,128]{1,0:T(8,128)S(1)}, u32[]{:S(2)}, u32[]{:S(2)}) collective-permute-start(f32[16,128]{1,0:T(8,128)S(1)} %get-tuple-element.63), channel_id=1, source_target_pairs={{0,8},{4,12},{8,0},{12,4},{16,24},{20,28},{24,16},{28,20},{1,9},{5... | collective-permute-start | bytes 24584 | tf_op jit(solution)/shard_map/ppermute | solution.py:478
  111.2 7.6 %collective-permute-start.24 = (f32[16,128]{1,0:T(8,128)S(1)}, f32[16,128]{1,0:T(8,128)S(1)}, u32[]{:S(2)}, u32[]{:S(2)}) collective-permute-start(f32[16,128]{1,0:T(8,128)S(1)} %get-tuple-element.64), channel_id=1, source_target_pairs={{0,12},{4,8},{8,4},{12,0},{16,28},{20,24},{24,20},{28,16},{1,13},{... | collective-permute-start | bytes 24584 | tf_op jit(solution)/shard_map/ppermute | solution.py:478
  112.2 8.8 %collective-permute-start.25 = (f32[16,128]{1,0:T(8,128)S(1)}, f32[16,128]{1,0:T(8,128)S(1)}, u32[]{:S(2)}, u32[]{:S(2)}) collective-permute-start(f32[16,128]{1,0:T(8,128)S(1)} %get-tuple-element.65), channel_id=1, source_target_pairs={{0,16},{4,20},{8,24},{12,28},{16,0},{20,4},{24,8},{28,12},{1,17},{... | collective-permute-start | bytes 24584 | tf_op jit(solution)/shard_map/ppermute | solution.py:478
  116.3 5.4 %collective-permute-start.26 = (f32[16,128]{1,0:T(8,128)S(1)}, f32[16,128]{1,0:T(8,128)S(1)}, u32[]{:S(2)}, u32[]{:S(2)}) collective-permute-start(f32[16,128]{1,0:T(8,128)S(1)} %get-tuple-element.66), channel_id=1, source_target_pairs={{0,20},{4,16},{8,28},{12,24},{16,4},{20,0},{24,12},{28,8},{1,21},{... | collective-permute-start | bytes 24584 | tf_op jit(solution)/shard_map/ppermute | solution.py:478
  116.3 7.0 %collective-permute-start.27 = (f32[16,128]{1,0:T(8,128)S(1)}, f32[16,128]{1,0:T(8,128)S(1)}, u32[]{:S(2)}, u32[]{:S(2)}) collective-permute-start(f32[16,128]{1,0:T(8,128)S(1)} %get-tuple-element.67), channel_id=1, source_target_pairs={{0,24},{4,28},{8,16},{12,20},{16,8},{20,12},{24,0},{28,4},{1,25},{... | collective-permute-start | bytes 24584 | tf_op jit(solution)/shard_map/ppermute | solution.py:478
  118.7 6.3 %collective-permute-start.28 = (f32[16,128]{1,0:T(8,128)S(1)}, f32[16,128]{1,0:T(8,128)S(1)}, u32[]{:S(2)}, u32[]{:S(2)}) collective-permute-start(f32[16,128]{1,0:T(8,128)S(1)} %get-tuple-element.68), channel_id=1, source_target_pairs={{0,28},{4,24},{8,20},{12,16},{16,12},{20,8},{24,4},{28,0},{1,29},{... | collective-permute-start | bytes 24584 | tf_op jit(solution)/shard_map/ppermute | solution.py:478
  121.1 11.1 %collective-permute-start.19 = (f32[40,512]{1,0:T(8,128)S(1)}, f32[40,512]{1,0:T(8,128)S(1)}, u32[]{:S(2)}, u32[]{:S(2)}) collective-permute-start(f32[40,512]{1,0:T(8,128)S(1)} %get-tuple-element.60.refs_1_), channel_id=1, source_target_pairs={{0,1},{1,0},{2,3},{3,2},{4,5},{5,4},{6,7},{7,6},{8,9},{9,8},{10,11... | collective-permute-start | bytes 245768 | tf_op jit(solution)/shard_map/ppermute | solution.py:478
  121.8 10.4 %collective-permute-start.20 = (f32[40,512]{1,0:T(8,128)S(1)}, f32[40,512]{1,0:T(8,128)S(1)}, u32[]{:S(2)}, u32[]{:S(2)}) collective-permute-start(f32[40,512]{1,0:T(8,128)S(1)} %get-tuple-element.60.refs_1_), channel_id=1, source_target_pairs={{0,2},{1,3},{2,0},{3,1},{4,6},{5,7},{6,4},{7,5},{8,10},{9,11},{10,... | collective-permute-start | bytes 245768 | tf_op jit(solution)/shard_map/ppermute | solution.py:478
  123.3 8.9 %collective-permute-start.21 = (f32[40,512]{1,0:T(8,128)S(1)}, f32[40,512]{1,0:T(8,128)S(1)}, u32[]{:S(2)}, u32[]{:S(2)}) collective-permute-start(f32[40,512]{1,0:T(8,128)S(1)} %get-tuple-element.60.refs_1_), channel_id=1, source_target_pairs={{0,3},{1,2},{2,1},{3,0},{4,7},{5,6},{6,5},{7,4},{8,11},{9,10},{10,... | collective-permute-start | bytes 245768 | tf_op jit(solution)/shard_map/ppermute | solution.py:478
  125.7 1.3 collective-permute-start.29
  126.9 3.9 %collective-permute-start.30 = (f32[16,512]{1,0:T(8,128)S(1)}, f32[16,512]{1,0:T(8,128)S(1)}, u32[]{:S(2)}, u32[]{:S(2)}) collective-permute-start(f32[16,512]{1,0:T(8,128)S(1)} %owned_cotangent.1.refs_5_), channel_id=1, source_target_pairs={{0,2},{1,3},{2,0},{3,1},{4,6},{5,7},{6,4},{7,5},{8,10},{9,11},{10,... | collective-permute-start | bytes 98312 | tf_op jit(solution)/shard_map/ppermute | solution.py:478
  128.5 3.7 %collective-permute-start.31 = (f32[16,512]{1,0:T(8,128)S(1)}, f32[16,512]{1,0:T(8,128)S(1)}, u32[]{:S(2)}, u32[]{:S(2)}) collective-permute-start(f32[16,512]{1,0:T(8,128)S(1)} %owned_cotangent.1.refs_5_), channel_id=1, source_target_pairs={{0,3},{1,2},{2,1},{3,0},{4,7},{5,6},{6,5},{7,4},{8,11},{9,10},{10,... | collective-permute-start | bytes 98312 | tf_op jit(solution)/shard_map/ppermute | solution.py:478
  130.9 26.3 %collective-permute-start.48 = (f32[16,1024]{1,0:T(8,128)S(1)}, f32[16,1024]{1,0:T(8,128)S(1)}, u32[]{:S(2)}, u32[]{:S(2)}) collective-permute-start(f32[16,1024]{1,0:T(8,128)S(1)} %add.18), channel_id=1, source_target_pairs={{0,16},{4,20},{8,24},{12,28},{16,0},{20,4},{24,8},{28,12},{1,17},{... | collective-permute-start | bytes 196616 | tf_op jit(solution)/shard_map/ppermute | solution.py:478
  133.1 5.1 %collective-permute-start.32 = (f32[2,16,128]{2,1,0:T(8,128)S(1)}, f32[2,16,128]{2,1,0:T(8,128)S(1)}, u32[]{:S(2)}, u32[]{:S(2)}) collective-permute-start(f32[2,16,128]{2,1,0:T(8,128)S(1)} %get-tuple-element.71), channel_id=1, source_target_pairs={{0,4},{4,0},{8,12},{12,8},{16,20},{20,16},{24,28},{28,24},{1,5},{5... | collective-permute-start | bytes 49160 | tf_op jit(solution)/shard_map/ppermute | solution.py:478
  134.6 5.9 %collective-permute-start.33 = (f32[2,16,128]{2,1,0:T(8,128)S(1)}, f32[2,16,128]{2,1,0:T(8,128)S(1)}, u32[]{:S(2)}, u32[]{:S(2)}) collective-permute-start(f32[2,16,128]{2,1,0:T(8,128)S(1)} %get-tuple-element.72), channel_id=1, source_target_pairs={{0,8},{4,12},{8,0},{12,4},{16,24},{20,28},{24,16},{28,20},{1,9},{5... | collective-permute-start | bytes 49160 | tf_op jit(solution)/shard_map/ppermute | solution.py:478
  135.3 6.6 %collective-permute-start.34 = (f32[2,16,128]{2,1,0:T(8,128)S(1)}, f32[2,16,128]{2,1,0:T(8,128)S(1)}, u32[]{:S(2)}, u32[]{:S(2)}) collective-permute-start(f32[2,16,128]{2,1,0:T(8,128)S(1)} %get-tuple-element.73), channel_id=1, source_target_pairs={{0,12},{4,8},{8,4},{12,0},{16,28},{20,24},{24,20},{28,16},{1,13},{... | collective-permute-start | bytes 49160 | tf_op jit(solution)/shard_map/ppermute | solution.py:478
  136.6 7.7 %collective-permute-start.35 = (f32[2,16,128]{2,1,0:T(8,128)S(1)}, f32[2,16,128]{2,1,0:T(8,128)S(1)}, u32[]{:S(2)}, u32[]{:S(2)}) collective-permute-start(f32[2,16,128]{2,1,0:T(8,128)S(1)} %get-tuple-element.74), channel_id=1, source_target_pairs={{0,16},{4,20},{8,24},{12,28},{16,0},{20,4},{24,8},{28,12},{1,17},{... | collective-permute-start | bytes 49160 | tf_op jit(solution)/shard_map/ppermute | solution.py:478
  138.2 6.0 %collective-permute-start.36 = (f32[2,16,128]{2,1,0:T(8,128)S(1)}, f32[2,16,128]{2,1,0:T(8,128)S(1)}, u32[]{:S(2)}, u32[]{:S(2)}) collective-permute-start(f32[2,16,128]{2,1,0:T(8,128)S(1)} %get-tuple-element.75), channel_id=1, source_target_pairs={{0,20},{4,16},{8,28},{12,24},{16,4},{20,0},{24,12},{28,8},{1,21},{... | collective-permute-start | bytes 49160 | tf_op jit(solution)/shard_map/ppermute | solution.py:478
  140.5 5.5 %collective-permute-start.37 = (f32[2,16,128]{2,1,0:T(8,128)S(1)}, f32[2,16,128]{2,1,0:T(8,128)S(1)}, u32[]{:S(2)}, u32[]{:S(2)}) collective-permute-start(f32[2,16,128]{2,1,0:T(8,128)S(1)} %get-tuple-element.76), channel_id=1, source_target_pairs={{0,24},{4,28},{8,16},{12,20},{16,8},{20,12},{24,0},{28,4},{1,25},{... | collective-permute-start | bytes 49160 | tf_op jit(solution)/shard_map/ppermute | solution.py:478
  141.8 6.4 %collective-permute-start.38 = (f32[2,16,128]{2,1,0:T(8,128)S(1)}, f32[2,16,128]{2,1,0:T(8,128)S(1)}, u32[]{:S(2)}, u32[]{:S(2)}) collective-permute-start(f32[2,16,128]{2,1,0:T(8,128)S(1)} %get-tuple-element.77), channel_id=1, source_target_pairs={{0,28},{4,24},{8,20},{12,16},{16,12},{20,8},{24,4},{28,0},{1,29},{... | collective-permute-start | bytes 49160 | tf_op jit(solution)/shard_map/ppermute | solution.py:478
  148.3 4.5 %collective-permute-start.39 = (f32[2,16,128]{2,1,0:T(8,128)S(1)}, f32[2,16,128]{2,1,0:T(8,128)S(1)}, u32[]{:S(2)}, u32[]{:S(2)}) collective-permute-start(f32[2,16,128]{2,1,0:T(8,128)S(1)} %share_sum.1.refs_1_), channel_id=1, source_target_pairs={{0,4},{4,0},{8,12},{12,8},{16,20},{20,16},{24,28},{28,24},{1,5},{5... | collective-permute-start | bytes 49160 | tf_op jit(solution)/shard_map/ppermute | solution.py:478
  149.0 5.9 %collective-permute-start.40 = (f32[2,16,128]{2,1,0:T(8,128)S(1)}, f32[2,16,128]{2,1,0:T(8,128)S(1)}, u32[]{:S(2)}, u32[]{:S(2)}) collective-permute-start(f32[2,16,128]{2,1,0:T(8,128)S(1)} %share_sum.1.refs_1_), channel_id=1, source_target_pairs={{0,8},{4,12},{8,0},{12,4},{16,24},{20,28},{24,16},{28,20},{1,9},{5... | collective-permute-start | bytes 49160 | tf_op jit(solution)/shard_map/ppermute | solution.py:478
  149.0 10.5 %collective-permute-start.41 = (f32[2,16,128]{2,1,0:T(8,128)S(1)}, f32[2,16,128]{2,1,0:T(8,128)S(1)}, u32[]{:S(2)}, u32[]{:S(2)}) collective-permute-start(f32[2,16,128]{2,1,0:T(8,128)S(1)} %share_sum.1.refs_1_), channel_id=1, source_target_pairs={{0,12},{4,8},{8,4},{12,0},{16,28},{20,24},{24,20},{28,16},{1,13},{... | collective-permute-start | bytes 49160 | tf_op jit(solution)/shard_map/ppermute | solution.py:478
  151.9 7.7 %collective-permute-start.42 = (f32[2,16,128]{2,1,0:T(8,128)S(1)}, f32[2,16,128]{2,1,0:T(8,128)S(1)}, u32[]{:S(2)}, u32[]{:S(2)}) collective-permute-start(f32[2,16,128]{2,1,0:T(8,128)S(1)} %share_sum.1.refs_1_), channel_id=1, source_target_pairs={{0,16},{4,20},{8,24},{12,28},{16,0},{20,4},{24,8},{28,12},{1,17},{... | collective-permute-start | bytes 49160 | tf_op jit(solution)/shard_map/ppermute | solution.py:478
  152.8 6.7 %collective-permute-start.43 = (f32[2,16,128]{2,1,0:T(8,128)S(1)}, f32[2,16,128]{2,1,0:T(8,128)S(1)}, u32[]{:S(2)}, u32[]{:S(2)}) collective-permute-start(f32[2,16,128]{2,1,0:T(8,128)S(1)} %share_sum.1.refs_1_), channel_id=1, source_target_pairs={{0,20},{4,16},{8,28},{12,24},{16,4},{20,0},{24,12},{28,8},{1,21},{... | collective-permute-start | bytes 49160 | tf_op jit(solution)/shard_map/ppermute | solution.py:478
  154.9 5.5 %collective-permute-start.44 = (f32[2,16,128]{2,1,0:T(8,128)S(1)}, f32[2,16,128]{2,1,0:T(8,128)S(1)}, u32[]{:S(2)}, u32[]{:S(2)}) collective-permute-start(f32[2,16,128]{2,1,0:T(8,128)S(1)} %share_sum.1.refs_1_), channel_id=1, source_target_pairs={{0,24},{4,28},{8,16},{12,20},{16,8},{20,12},{24,0},{28,4},{1,25},{... | collective-permute-start | bytes 49160 | tf_op jit(solution)/shard_map/ppermute | solution.py:478
  157.2 6.4 %collective-permute-start.45 = (f32[2,16,128]{2,1,0:T(8,128)S(1)}, f32[2,16,128]{2,1,0:T(8,128)S(1)}, u32[]{:S(2)}, u32[]{:S(2)}) collective-permute-start(f32[2,16,128]{2,1,0:T(8,128)S(1)} %share_sum.1.refs_1_), channel_id=1, source_target_pairs={{0,28},{4,24},{8,20},{12,16},{16,12},{20,8},{24,4},{28,0},{1,29},{... | collective-permute-start | bytes 49160 | tf_op jit(solution)/shard_map/ppermute | solution.py:478
  (3 other events, 2.6 us)

commit v3 on v2

--- a/solution.py
+++ b/solution.py
@@ -243,28 +243,39 @@
     return pl.ds(pl.multiple_of(lax.bitwise_xor(place_ref[0], j) * width, width), width)
 
 
-def memory_kernel(peers, last, place_ref, me_ref, asked_ref, x0, x1, x2, x3, wk_ref, wv_ref, down_ref, up_ref, *refs):
-    tokens = (x0, x1, x2, x3)
-    rows, width = x0.shape
-    blocks = rows // BLK
-    acc = None
-    low = None
-    for j in range(4):
+def memory_early_kernel(place_ref, x0, x1, wk_ref, wv_ref, down_ref, acc_ref, low_ref):
+    width = x0.shape[1]
+    acc = low = None
+    for j, x_ref in enumerate((x0, x1)):
         here = piece_rows(place_ref, j, width)
-        x = tokens[j][...]
+        x = x_ref[...]
         term = dot_nn(x, jnp.concatenate([wk_ref[here, :], wv_ref[here, :]], 1))
         low_term = dot_nt(x, down_ref[:, here])
         acc = term if acc is None else acc + term
         low = low_term if low is None else low + low_term
+    acc_ref[...] = acc
+    low_ref[...] = low
+
+
+def memory_kernel(first, peers, last, place_ref, asked_ref, x2, x3, acc_ref, low_in, wk_ref, wv_ref, down_ref, up_ref, *refs):
+    rows, width = x2.shape
+    blocks = rows // BLK
+    acc = acc_ref[first : first + rows, :]
+    low = low_in[first : first + rows, :]
+    for j, x_ref in ((2, x2), (3, x3)):
+        here = piece_rows(place_ref, j, width)
+        x = x_ref[...]
+        acc = acc + dot_nn(x, jnp.concatenate([wk_ref[here, :], wv_ref[here, :]], 1))
+        low = low + dot_nt(x, down_ref[:, here])
     values = (acc[:, HD:] + dot_nn(low.astype(jnp.bfloat16), up_ref[...])).astype(jnp.bfloat16)
     keys = acc[:, :HD].astype(jnp.bfloat16)
     low_t = jnp.transpose(low).astype(jnp.bfloat16)
     if last:
-        before, outs, pair_ref = refs[0], refs[1 : 1 + peers], refs[1 + peers]
+        before, out_ref, pair_ref = refs
         offset = before.shape[0]
         pair_ref[:offset] = before[...]
     else:
-        pair_ref = refs[0]
+        pair_ref = refs[1]
         offset = 0
     for b in range(blocks):
         at = slice(b * BLK, (b + 1) * BLK)
@@ -272,39 +283,62 @@
         pair_ref[offset + b, BLK : 2 * BLK, :] = values[at]
         pair_ref[offset + b, 2 * BLK : PACK, :] = low_t[:, at]
     if last:
-        for d in range(peers):
-            outs[d][...] = pair_ref[asked_ref[lax.bitwise_xor(me_ref[0], d)]]
-
-
-def project_kernel(place_ref, x0, x1, x2, x3, wq_hbm, wk_hbm, wv_hbm, qd_hbm, vd_hbm, qup_ref, vup_ref,
-                   q_ref, k_ref, v_ref, low_ref, wq_s, wk_s, wv_s, qd_s, vd_s, sems):
-    tokens = (x0, x1, x2, x3)
-    width = x0.shape[1]
-    copies = []
-    for j in range(4):
-        here = piece_rows(place_ref, j, width)
-        group = [
-            pltpu.make_async_copy(wq_hbm.at[here, :], wq_s.at[j], sems.at[j, 0]),
-            pltpu.make_async_copy(wk_hbm.at[here, :], wk_s.at[j], sems.at[j, 1]),
-            pltpu.make_async_copy(wv_hbm.at[here, :], wv_s.at[j], sems.at[j, 2]),
-            pltpu.make_async_copy(qd_hbm.at[:, here], qd_s.at[j], sems.at[j, 3]),
-            pltpu.make_async_copy(vd_hbm.at[:, here], vd_s.at[j], sems.at[j, 4]),
-        ]
-        for c in group:
-            c.start()
-        copies.append(group)
-    q_acc = kv_acc = low_acc = None
-    for j in range(4):
+        for r in range(peers):
+            out_ref[r] = pair_ref[asked_ref[r]]
+
+
+def weight_copies(place_ref, j, slot, width, hbm, scratch, sems):
+    wq_hbm, wk_hbm, wv_hbm, qd_hbm, vd_hbm = hbm
+    wq_s, wk_s, wv_s, qd_s, vd_s = scratch
+    here = piece_rows(place_ref, j, width)
+    group = [
+        pltpu.make_async_copy(wq_hbm.at[here, :], wq_s.at[slot], sems.at[slot, 0]),
+        pltpu.make_async_copy(wk_hbm.at[here, :], wk_s.at[slot], sems.at[slot, 1]),
+        pltpu.make_async_copy(wv_hbm.at[here, :], wv_s.at[slot], sems.at[slot, 2]),
+        pltpu.make_async_copy(qd_hbm.at[:, here], qd_s.at[slot], sems.at[slot, 3]),
+        pltpu.make_async_copy(vd_hbm.at[:, here], vd_s.at[slot], sems.at[slot, 4]),
+    ]
+    for c in group:
+        c.start()
+    return group
+
+
+def project_terms(x, slot, scratch):
+    wq_s, wk_s, wv_s, qd_s, vd_s = scratch
+    return (
+        dot_nn(x, wq_s[slot]),
+        dot_nn(x, jnp.concatenate([wk_s[slot], wv_s[slot]], 1)),
+        dot_nt(x, jnp.concatenate([qd_s[slot], vd_s[slot]], 0)),
+    )
+
+
+def project_early_kernel(place_ref, x0, x1, *refs):
+    hbm, (q_ref, kv_ref, low_ref), scratch, sems = refs[:5], refs[5:8], refs[8:13], refs[13]
+    copies = [weight_copies(place_ref, j, j, x0.shape[1], hbm, scratch, sems) for j in range(2)]
+    for j, x_ref in enumerate((x0, x1)):
         for c in copies[j]:
             c.wait()
-        x = tokens[j][...]
-        q_term = dot_nn(x, wq_s[j])
-        kv_term = dot_nn(x, jnp.concatenate([wk_s[j], wv_s[j]], 1))
-        low_term = dot_nt(x, jnp.concatenate([qd_s[j], vd_s[j]], 0))
-        if q_acc is None:
-            q_acc, kv_acc, low_acc = q_term, kv_term, low_term
-        else:
-            q_acc, kv_acc, low_acc = q_acc + q_term, kv_acc + kv_term, low_acc + low_term
+        terms = project_terms(x_ref[...], j, scratch)
+        for ref, term in zip((q_ref, kv_ref, low_ref), terms):
+            if j == 0:
+                ref[...] = term
+            else:
+                ref[...] += term
+
+
+def project_kernel(first, place_ref, x2, x3, *refs):
+    hbm, (q_in, kv_in, low_in), (qup_ref, vup_ref) = refs[:5], refs[5:8], refs[8:10]
+    q_ref, k_ref, v_ref, low_ref = refs[10:14]
+    scratch, sems = refs[14:19], refs[19]
+    rows, width = x2.shape
+    at = slice(first, first + rows)
+    copies = [weight_copies(place_ref, 2 + s, s, width, hbm, scratch, sems) for s in range(2)]
+    sums = [q_in[at, :], kv_in[at, :], low_in[at, :]]
+    for s, x_ref in enumerate((x2, x3)):
+        for c in copies[s]:
+            c.wait()
+        sums = [a + b for a, b in zip(sums, project_terms(x_ref[...], s, scratch))]
+    q_acc, kv_acc, low_acc = sums
     low = low_acc.astype(jnp.bfloat16)
     q_ref[...] = (q_acc + dot_nn(low[:, :RANK], qup_ref[...])).astype(jnp.bfloat16)
     k_ref[...] = kv_acc[:, :HD].astype(jnp.bfloat16)
@@ -314,12 +348,8 @@
 
 def attention_kernel(cuts, peers, heads, bound_ref, *refs):
     parts = refs[: 4 * cuts]
-    got = refs[4 * cuts : 4 * cuts + peers]
-    qup_ref, vup_ref, tag_ref, grad_ref, grad_t_ref = refs[4 * cuts + peers : 4 * cuts + peers + 5]
-    outs = refs[4 * cuts + peers + 5 :]
-    cot_ref, up_ref = outs[0], outs[1]
-    mcot_refs = outs[2 : 2 + peers]
-    (q_s, k_own, v_own, low_s, k_all, v_all, kt_all, vt_all, bias_s, s_s, e_s, dp_s, p_s, ds_s, att_s, dq_s, dv_s) = outs[2 + peers :]
+    got, qup_ref, vup_ref, tag_ref, grad_ref, grad_t_ref, cot_ref, up_ref, mcot_ref = refs[4 * cuts : 4 * cuts + 9]
+    (q_s, k_own, v_own, low_s, k_all, v_all, kt_all, vt_all, bias_s, s_s, e_s, dp_s, p_s, ds_s, att_s, dq_s, dv_s) = refs[4 * cuts + 9 :]
     seen = peers * BLK
     for t in range(cuts):
         q_c, k_c, v_c, low_c = parts[4 * t : 4 * t + 4]
@@ -331,8 +361,8 @@
         low_s[:, at] = low_c[...]
     for b in range(peers):
         at = slice(b * BLK, (b + 1) * BLK)
-        k = got[b][0:BLK, :]
-        v = got[b][BLK : 2 * BLK, :]
+        k = got[b, 0:BLK, :]
+        v = got[b, BLK : 2 * BLK, :]
         k_all[at, :] = k
         v_all[at, :] = v
         kt_all[:, at] = jnp.transpose(k)
@@ -416,72 +446,70 @@
     lax.fori_loop(0, q_s.shape[0] // BLK, span_step, 0)
     dv = dv_s[...]
     mcot = dot_nn(up_wide, dv, HIGHEST)
-    low_m = jnp.concatenate([got[b][2 * BLK : PACK, :] for b in range(peers)], 1).astype(jnp.float32)
+    low_m = jnp.concatenate([got[b, 2 * BLK : PACK, :] for b in range(peers)], 1).astype(jnp.float32)
     up_ref[:, query_width:] += dot_nt(low_m, dv, HIGHEST)
     for b in range(peers):
-        mcot_refs[b][...] = mcot[:, b * BLK : (b + 1) * BLK]
-
-
-def own_kernel(peers, me_ref, asked_ref, *refs):
-    pieces, out_ref, sum_s = refs[:peers], refs[peers], refs[peers + 1]
+        mcot_ref[b] = mcot[:, b * BLK : (b + 1) * BLK]
+
+
+def own_kernel(peers, asked_ref, back_ref, cot_ref, dep_ref, out_ref, sum_s):
     sum_s[...] = jnp.zeros_like(sum_s)
-    for d in range(peers):
-        block = asked_ref[lax.bitwise_xor(me_ref[0], d)]
-        sum_s[block] = sum_s[block] + pieces[d][...]
-    out_ref[...] = jnp.concatenate([sum_s[m] for m in range(sum_s.shape[0])], 1)
-
-
-def down_kernel(peers, me_ref, *refs):
-    cots, owns = refs[0:4], refs[4:8]
-    slab_ref, memory_ref, logit_ref = refs[8:11]
-    outs, part_s = refs[11 : 11 + peers], refs[11 + peers]
-    cot = (cots[0][...] + cots[1][...]) + (cots[2][...] + cots[3][...])
-    own = (owns[0][...] + owns[1][...]) + (owns[2][...] + owns[3][...])
-    logit_ref[...] = cot[2 * RANK :]
-    both = dot_nn(cot[: 2 * RANK].astype(jnp.bfloat16), slab_ref[...])
-    value = both[RANK:] + dot_nn(own.astype(jnp.bfloat16), memory_ref[...])
-    tiles = []
-    for whole in (both[:RANK], value):
-        for n in range(whole.shape[1] // HD):
-            tiles.append(whole[:, n * HD : (n + 1) * HD])
-    each = part_s.shape[1]
-    for n in range(each * peers):
-        part_s[n // each, n % each] = tiles[n] if n < len(tiles) else jnp.zeros((RANK, HD), jnp.float32)
-    for d in range(peers):
-        outs[d][...] = part_s[lax.bitwise_xor(me_ref[0], d)]
-
-
-def share_kernel(peers, *refs):
-    total = refs[0][...]
-    for d in range(1, peers):
-        total = total + refs[d][...]
-    refs[peers][...] = total
-
-
-def finish_kernel(peers, me_ref, *refs):
-    shares, up_ref = refs[:peers], refs[peers]
-    query_down_ref, query_up_ref, value_down_ref, value_up_ref, all_s = refs[peers + 1 :]
-    for d in range(peers):
-        all_s[lax.bitwise_xor(me_ref[0], d)] = shares[d][...]
-    each = all_s.shape[1]
-    n = 0
-    for out_ref in (query_down_ref, value_down_ref):
-        for m in range(out_ref.shape[1] // HD):
-            out_ref[:, m * HD : (m + 1) * HD] = all_s[n // each, n % each]
-            n += 1
+    for r in range(peers):
+        block = asked_ref[r]
+        sum_s[block] = sum_s[block] + back_ref[r]
+    rows = cot_ref.shape[0]
+    out_ref[:rows, :] = cot_ref[...]
+    out_ref[rows:, :] = jnp.concatenate([sum_s[m] for m in range(sum_s.shape[0])], 1)
+
+
+def down_kernel(c0, c1, c2, c3, slab_ref, memory_ref, dep_ref, logit_ref, out_ref):
+    cot = (c0[...] + c1[...]) + (c2[...] + c3[...])
+    tags = logit_ref.shape[0]
+    logit_ref[...] = cot[2 * RANK : 2 * RANK + tags]
+    low = cot.astype(jnp.bfloat16)
+    both = dot_nn(low[: 2 * RANK], slab_ref[...])
+    out_ref[:RANK, :] = both[:RANK]
+    out_ref[RANK:, :] = both[RANK:] + dot_nn(low[2 * RANK + tags :], memory_ref[...])
+
+
+def finish_kernel(d0, d1, u0, u1, query_down_ref, query_up_ref, value_down_ref, value_up_ref):
+    down = d0[...] + d1[...]
+    up = u0[...] + u1[...]
     query_width = query_up_ref.shape[1]
-    query_up_ref[...] = up_ref[:, :query_width]
-    value_up_ref[...] = up_ref[:, query_width:]
+    query_down_ref[...] = down[:RANK]
+    value_down_ref[...] = down[RANK:]
+    query_up_ref[...] = up[:, :query_width]
+    value_up_ref[...] = up[:, query_width:]
 
 
 def swap(x, bit, axis="heads"):
     return lax.ppermute(x, axis, [(i, i ^ bit) for i in range(lax.axis_size(axis))])
 
 
-def gather_parts(x):
-    far = swap(x, 2)
-    near = swap(x, 1)
-    return x, near, far, swap(far, 1)
+def split_after(x, cuts, dep):
+    rows = x.shape[0] // cuts
+
+    def body(x_ref, dep_ref, *outs):
+        for n in range(cuts):
+            outs[n][...] = x_ref[n * rows : (n + 1) * rows, :]
+
+    out_shape = [jax.ShapeDtypeStruct((rows, x.shape[1]), x.dtype)] * cuts
+    return run(body, "split_rows", out_shape, [vmem(), anywhere()], moved=4 * x.size)(x, dep)
+
+
+def after(x, dep):
+    return pl.pallas_call(
+        lambda x_ref, dep_ref, out_ref: None,
+        out_shape=jax.ShapeDtypeStruct(x.shape, x.dtype),
+        in_specs=[anywhere(), anywhere()],
+        out_specs=anywhere(),
+        input_output_aliases={0: 0},
+        name="in_order",
+    )(x, dep)
+
+
+def anywhere():
+    return pl.BlockSpec(memory_space=pl.ANY)
 
 
 def smem():
@@ -536,8 +564,10 @@
     bf16 = jnp.bfloat16
     mem_cuts, tok_cuts = 2, 2
 
-    mem_parts = [gather_parts(m) for m in jnp.split(memory, mem_cuts, 0)]
-    tok_parts = [gather_parts(x) for x in jnp.split(slab_tokens, tok_cuts, 0)]
+    mem_far = [swap(m, 2) for m in jnp.split(memory, mem_cuts, 0)]
+    mem_near = swap(memory, 1)
+    tok_near = swap(slab_tokens, 1)
+    tok_far = [swap(x, 2) for x in split_after(slab_tokens, tok_cuts, mem_far[0])]
 
     named = retrieval[0]
     owner_ids = jnp.arange(peers, dtype=jnp.int32)
@@ -546,7 +576,6 @@
     ).astype(jnp.int32)
     asked = lax.all_to_all(wanted, "tm", split_axis=0, concat_axis=0, tiled=True)
     place = lax.axis_index("heads").astype(jnp.int32).reshape(1)
-    me = lax.axis_index("tm").astype(jnp.int32).reshape(1)
 
     tag_t = tag_weight.T
     tags = tag_t.shape[0]
@@ -556,65 +585,86 @@
     ).astype(bf16)
     grad = lax.dot_general(grad_tags, wide_tag, (((1,), (0,)), ((), ())), precision=HIGHEST).astype(bf16)
 
+    mem_acc, mem_low = run(
+        memory_early_kernel,
+        "memory_near_half",
+        (shaped(mem_rows, 2 * HD), shaped(mem_rows, RANK)),
+        [smem()] + [vmem()] * 5,
+        flops=2 * mem_rows * 2 * width * 3 * HD,
+        moved=4 * mem_rows * width,
+    )(place, memory, mem_near, key_weight, value_weight, value_down)
+    rows = tok_rows // tok_cuts
+    weights = (query_weight, key_weight, value_weight, query_down, value_down)
+    weight_scratch = [
+        pltpu.VMEM((2, width, query_width), bf16),
+        pltpu.VMEM((2, width, HD), bf16),
+        pltpu.VMEM((2, width, HD), bf16),
+        pltpu.VMEM((2, RANK, width), bf16),
+        pltpu.VMEM((2, RANK, width), bf16),
+        pltpu.SemaphoreType.DMA((2, 5)),
+    ]
+    early = run(
+        project_early_kernel,
+        "project_near_half",
+        (shaped(tok_rows, query_width), shaped(tok_rows, 2 * HD), shaped(tok_rows, 2 * RANK)),
+        [smem()] + [vmem()] * 2 + [anywhere()] * 5,
+        weight_scratch,
+        flops=2 * tok_rows * 2 * width * (query_width + 3 * HD),
+        moved=4 * width * (tok_rows + query_width + 3 * HD),
+    )(place, slab_tokens, tok_near, *weights)
+    mem_far = [mem_far[0]] + [after(m, early[2]) for m in mem_far[1:]]
+    mem_cross = [swap(m, 1) for m in mem_far]
     cut_rows = mem_rows // mem_cuts
-    cut_blocks = blocks // mem_cuts
     before = []
     for t in range(mem_cuts):
         last = t == mem_cuts - 1
-        args = [place, me, asked, *mem_parts[t], key_weight, value_weight, value_down, value_up]
+        args = [place, asked, mem_far[t], mem_cross[t], mem_acc, mem_low, key_weight, value_weight, value_down, value_up]
         if last:
             args.append(jnp.concatenate(before, 0) if len(before) > 1 else before[0])
-            out_shape = [shaped(PACK, HD, dtype=bf16)] * peers
+            out_shape = shaped(peers, PACK, HD, dtype=bf16)
             scratch = [pltpu.VMEM((blocks, PACK, HD), bf16)]
         else:
-            out_shape = shaped(cut_blocks, PACK, HD, dtype=bf16)
+            args.append(early[2])
+            out_shape = shaped(cut_rows // BLK, PACK, HD, dtype=bf16)
             scratch = []
         result = run(
-            lambda *refs, last=last: memory_kernel(peers, last, *refs),
+            lambda *refs, t=t, last=last: memory_kernel(t * cut_rows, peers, last, *refs),
             "memory_pairs",
             out_shape,
-            [smem()] * 3 + [vmem()] * (len(args) - 3),
+            [smem()] * 2 + [vmem()] * (len(args) - 3) + [vmem() if last else anywhere()],
             scratch,
-            flops=2 * cut_rows * 4 * width * 3 * HD,
-            moved=8 * cut_rows * width + 16 * width * HD,
+            flops=2 * cut_rows * 2 * width * 3 * HD,
+            moved=4 * cut_rows * width,
         )(*args)
         before.append(result)
-    outgoing = before[-1]
-    got = [outgoing[0]] + [swap(outgoing[d], d, "tm") for d in range(1, peers)]
-
-    rows = tok_rows // tok_cuts
-    anywhere = pl.BlockSpec(memory_space=pl.ANY)
+    got = lax.all_to_all(before[-1], "tm", split_axis=0, concat_axis=0, tiled=True)
+
+    tok_far = [after(x, before[-1]) for x in tok_far]
+    tok_cross = [swap(x, 1) for x in tok_far]
     parts = []
     for t in range(tok_cuts):
         parts += run(
-            project_kernel,
-            "project_span_rows",
+            lambda *refs, t=t: project_kernel(t * rows, *refs),
+            "project_far_half",
             (
                 shaped(rows, query_width, dtype=bf16),
                 shaped(rows, HD, dtype=bf16),
                 shaped(rows, HD, dtype=bf16),
                 shaped(2 * RANK, rows, dtype=bf16),
             ),
-            [smem()] + [vmem()] * 4 + [anywhere] * 5 + [vmem()] * 2,
-            [
-                pltpu.VMEM((4, width, query_width), bf16),
-                pltpu.VMEM((4, width, HD), bf16),
-                pltpu.VMEM((4, width, HD), bf16),
-                pltpu.VMEM((4, RANK, width), bf16),
-                pltpu.VMEM((4, RANK, width), bf16),
-                pltpu.SemaphoreType.DMA((4, 5)),
-            ],
-            flops=2 * rows * 4 * width * (query_width + 3 * HD),
-            moved=8 * width * (rows + query_width + 3 * HD),
-        )(place, *tok_parts[t], query_weight, key_weight, value_weight, query_down, value_down, query_up, value_up)
+            [smem()] + [vmem()] * 2 + [anywhere()] * 5 + [vmem()] * 5,
+            weight_scratch,
+            flops=2 * rows * 2 * width * (query_width + 3 * HD),
+            moved=4 * width * (rows + query_width + 3 * HD),
+        )(place, tok_far[t], tok_cross[t], *weights, *early, query_up, value_up)
 
     seen = peers * BLK
     total = seen + BLK
-    cot, ups, *mcot = run(
+    cot, ups, mcot = run(
         lambda *refs: attention_kernel(tok_cuts, peers, heads, *refs),
         "span_attention",
-        [shaped(2 * RANK + tags, tok_rows), shaped(RANK, query_width + HD)] + [shaped(RANK, BLK)] * peers,
-        [smem()] + [vmem()] * (4 * tok_cuts + peers + 5),
+        (shaped(2 * RANK + tags, tok_rows), shaped(RANK, query_width + HD), shaped(peers, RANK, BLK)),
+        [smem()] + [vmem()] * (4 * tok_cuts + 6),
         [
             pltpu.VMEM((tok_rows, query_width), bf16),
             pltpu.VMEM((tok_rows, HD), bf16),
@@ -636,44 +686,35 @@
         ],
         flops=20 * tok_rows * query_width * total,
         moved=4 * tok_rows * query_width,
-    )(boundary, *parts, *got, query_up, value_up, tag_t, grad, grad_t)
-
-    back = [mcot[0]] + [swap(mcot[d], d, "tm") for d in range(1, peers)]
-    cots = [cot] + [swap(cot, d) for d in range(1, 4)]
-    bit = 1
-    while bit < peers:
-        ups = ups + swap(ups, bit, "tm")
-        bit *= 2
-    own = run(
+    )(boundary, *parts, got, query_up, value_up, tag_t, grad, grad_t)
+
+    back = lax.all_to_all(mcot, "tm", split_axis=0, concat_axis=0, tiled=True)
+    ups = ups + swap(ups, 1, "tm")
+    cots = run(
         lambda *refs: own_kernel(peers, *refs),
         "owned_cotangent",
-        shaped(RANK, mem_rows),
-        [smem()] * 2 + [vmem()] * peers,
+        shaped(cot.shape[0] + RANK, mem_rows),
+        [smem()] + [vmem()] * 2 + [anywhere()],
         [pltpu.VMEM((blocks, RANK, BLK), f32)],
-    )(me, asked, *back)
-    owns = [own] + [swap(own, d) for d in range(1, 4)]
-    each = -(-2 * (width // HD) // peers)
-    logits, *pieces = run(
-        lambda *refs: down_kernel(peers, *refs),
+    )(asked, back, cot, ups)
+    ups = ups + swap(ups, 2, "tm")
+    cots = [cots] + [swap(cots, d) for d in range(1, 4)]
+    logits, downs = run(
+        down_kernel,
         "down_gradients",
-        [shaped(tags, tok_rows)] + [shaped(each, RANK, HD)] * peers,
-        [smem()] + [vmem()] * 10,
-        [pltpu.VMEM((peers, each, RANK, HD), f32)],
+        (shaped(tags, tok_rows), shaped(2 * RANK, width)),
+        [vmem()] * 6 + [anywhere()],
         flops=6 * RANK * tok_rows * width,
         moved=4 * tok_rows * width,
-    )(me, *cots, *owns, slab_tokens, memory)
-    pieces = [pieces[0]] + [swap(pieces[d], d, "tm") for d in range(1, peers)]
-    share = run(
-        lambda *refs: share_kernel(peers, *refs), "share_sum", shaped(each, RANK, HD), [vmem()] * peers
-    )(*pieces)
-    shares = [share] + [swap(share, d, "tm") for d in range(1, peers)]
+    )(*cots, slab_tokens, memory, ups)
+    for bit in (1, 2):
+        downs = downs + swap(downs, bit, "tm")
     query_down_grad, query_up_grad, value_down_grad, value_up_grad = run(
-        lambda *refs: finish_kernel(peers, *refs),
+        finish_kernel,
         "finish_outputs",
         (shaped(RANK, width), shaped(RANK, query_width), shaped(RANK, width), shaped(RANK, HD)),
-        [smem()] + [vmem()] * (peers + 1),
-        [pltpu.VMEM((peers, each, RANK, HD), f32)],
-    )(me, *shares, ups)
+        [vmem()] * 4,
+    )(downs, swap(downs, 4, "tm"), ups, swap(ups, 4, "tm"))
     return (logits.T, query_down_grad, query_up_grad, value_down_grad, value_up_grad)
 
 
@@ -700,6 +741,6 @@
         P(None, "heads"),
         P(None, "heads"),
     )
-    fits = mesh.shape["heads"] == 4 and mesh.shape["tm"] * CAP == TOP
+    fits = mesh.shape["heads"] == 4 and mesh.shape["tm"] == 8 == TOP * CAP
     local = fast if fits else general
     return jax.shard_map(local, mesh=mesh, in_specs=in_specs, out_specs=out_specs, check_vma=False)

time: 165 us -> 146 us (0.88)
  starting transfers between devices: 65.1 us -> 24.4 us
  blocking collectives: 0 us -> 12.5 us
  local copies, waits for them, and re-layouts: 6.65 us -> 15.3 us
  Pallas kernels: 45.5 us -> 49.5 us
  waiting for transfers between devices: 41.2 us -> 37.6 us
    ppermute x49 -> x19, starting transfers between devices: 59.3 us -> 14.2 us  [swap(): lax.ppermute(x, axis, [(i, i ^ bit) for i in range(lax.axis_size(axis))])]
    all_to_all x0 -> x1, blocking collectives: none -> 12.5 us  [fast(): lax.all_to_all(wanted, 'tm', split_axis=0, concat_axis=0, tiled=True)]
    unnamed x34 -> x54, local copies, waits for them, and re-layouts: 3.64 us -> 13.1 us
    ppermute x49 -> x19, waiting for transfers between devices: 41.2 us -> 35.3 us  [swap(): lax.ppermute(x, axis, [(i, i ^ bit) for i in range(lax.axis_size(axis))])]
    all_to_all x1 -> x2, starting transfers between devices: 5.81 us -> 10.2 us  [the longest x1 5.7 us: fast(): back = lax.all_to_all(mcot, 'tm', split_axis=0, concat_axis=0, tiled=True)]
    pallas_call x8 -> x13, Pallas kernels: 23.7 us -> 27.2 us  [the longest x2 10.8 us: fast(): run(lambda *refs, t=t: project_kernel(t * rows, *refs), 'project_far_half...]
    all_to_all x1 -> x2, waiting for transfers between devices: 0.01 us -> 2.25 us  [the longest x1 2.25 us: fast(): back = lax.all_to_all(mcot, 'tm', split_axis=0, concat_axis=0, tiled=True)]
  transfers between devices with their start and end apart: 50 -> 21, of which waited for: 14 -> 8; matrix products, arithmetic and copies ran while one was open for 4% -> 5% of each run, Pallas kernels for 14% -> 17%
where the time goes in v3:
time: 146 us; the launch traced here: 145 us
  Pallas kernels  49.5 us (34%)
  waiting for transfers between devices  37.6 us (26%)
  starting transfers between devices  24.4 us (17%)
  local copies, waits for them, and re-layouts  15.3 us (10%)
  blocking collectives  12.5 us (9%)
  matrix products  3.74 us (3%)
    ppermute x19, waiting for transfers between devices, swap(): lax.ppermute(x, axis, [(i, i ^ bit) for i in range(lax.axis_size(axis))])  35.3 us
    pallas_call x1, Pallas kernels, fast(): run(lambda *refs: attention_kernel(tok_cuts, peers, heads, *refs), 'span_...  22.3 us
    ppermute x19, starting transfers between devices, swap(): lax.ppermute(x, axis, [(i, i ^ bit) for i in range(lax.axis_size(axis))])  14.2 us
    unnamed x54, local copies, waits for them, and re-layouts  13.1 us
    all_to_all x1, blocking collectives, fast(): lax.all_to_all(wanted, 'tm', split_axis=0, concat_axis=0, tiled=True)  12.5 us
    pallas_call x2, Pallas kernels, fast(): run(lambda *refs, t=t: project_kernel(t * rows, *refs), 'project_far_half...  10.8 us
    pallas_call x1, Pallas kernels, fast(): run(project_early_kernel, 'project_near_half', (shaped(tok_rows, query_wi...  6.13 us
    all_to_all x1, starting transfers between devices, fast(): back = lax.all_to_all(mcot, 'tm', split_axis=0, concat_axis=0, tiled=True)  5.7 us
  transfers between devices with their start and end apart: 21, of which 8 were waited for; matrix products, arithmetic and copies ran while one was open for 5% of the time, Pallas kernels for 17%

profile of v3, /device:TPU:0, one launch (start us, length us, event | category | flops | bytes accessed | tf_op | source)
XLA Modules:
  0.0 145.1 jit_solution(10055825490481492762)
XLA Ops:
  0.6 0.0 copy-start
  0.7 0.5 collective-permute-start.3
  1.2 2.1 %fusion.2 = (bf16[256,896]{1,0:T(8,128)(2,1)}, bf16[256,896]{1,0:T(8,128)(2,1)S(1)}) fusion(bf16[512,896]{1,0:T(8,128)(2,1)} %memory_ref.1), kind=kLoop, calls=%fused_computation.11 | loop fusion | bytes 1835008 | tf_op jit(solution)/shard_map/split | solution.py:567
  3.2 2.6 %collective-permute-start = (bf16[256,896]{1,0:T(8,128)(2,1)S(1)}, bf16[256,896]{1,0:T(8,128)(2,1)}, u32[]{:S(2)}, u32[]{:S(2)}) collective-permute-start(bf16[256,896]{1,0:T(8,128)(2,1)S(1)} %get-tuple-element.56), channel_id=1, source_target_pairs={{0,2},{1,3},{2,0},{3,1},{4,6},{5,7},{6,4},{7,5},{8,10},{9,11},{10,... | collective-permute-start | bytes 1376264 | tf_op jit(solution)/shard_map/ppermute | solution.py:486
  5.9 0.0 collective-permute-start.2
  5.9 0.1 collective-permute-start.5
  6.0 11.3 %collective-permute-done.dep_ref.refs_2_ = bf16[256,896]{1,0:T(8,128)(2,1)} collective-permute-done((bf16[256,896]{1,0:T(8,128)(2,1)S(1)}, bf16[256,896]{1,0:T(8,128)(2,1)}, u32[]{:S(2)}, u32[]{:S(2)}) %collective-permute-start) | collective-permute-done | bytes 458784 | tf_op jit(solution)/shard_map/ppermute | solution.py:486
  17.4 0.0 copy-start.4
  17.4 1.2 copy-done.4
  18.5 0.9 copy-done.9
  19.4 0.9 copy-done.13
  20.3 6.1 %project_near_half.1 = (f32[512,896]{1,0:T(8,128)}, f32[512,256]{1,0:T(8,128)S(1)}, f32[512,32]{1,0:T(8,128)S(1)}) custom-call(s32[1]{0:T(128)} %bitcast.3.place_ref.refs_0_, bf16[512,896]{1,0:T(8,128)(2,1)S(1)} %copy-done.4, bf16[512,896]{1,0:T(8,128)(2,1)S(1)} %collective-permute-done.3.x1, bf16[3584,896]{1,0:T(8,128)(2,1)} %refs_3_.5, ...), custom_call_target="tpu_custom_call" | custom-call | flops 2348810240 | bytes 6422528 | tf_op jit(solution)/shard_map/project_near_half/pallas_call | solution.py:606
  26.5 0.7 copy-done.7
  27.2 0.8 copy-done.11
  28.0 0.6 collective-permute-start.4
  28.6 0.7 fusion.1
  29.3 1.2 copy-done.5
  30.4 1.1 split_rows.1
  31.5 2.0 %collective-permute-start.8 = (bf16[256,896]{1,0:T(8,128)(2,1)}, bf16[256,896]{1,0:T(8,128)(2,1)}, u32[]{:S(2)}, u32[]{:S(2)}) collective-permute-start(bf16[256,896]{1,0:T(8,128)(2,1)} %get-tuple-element.39), channel_id=1, source_target_pairs={{0,2},{1,3},{2,0},{3,1},{4,6},{5,7},{6,4},{7,5},{8,10},{9,11},{10,... | collective-permute-start | bytes 1376264 | tf_op jit(solution)/shard_map/ppermute | solution.py:486
  33.5 0.0 collective-permute-start.1
  33.5 0.1 select_reduce_fusion
  33.7 0.1 copy.23
  33.7 12.5 %all_to_all.21 = s32[8,1,1]{2,1,0:T(1,128)S(1)} all-to-all(s32[8,1,1]{2,1,0:T(1,128)S(1)} %copy.23), channel_id=1, replica_groups=mesh['tm'=8,'heads'=4] {'tm'}, dimensions={0} | all-to-all | bytes 64 | tf_op jit(solution)/shard_map/all_to_all | solution.py:577
  46.2 0.2 reduce.refs_1_.refs_0_
  46.5 0.0 copy-start.18
  46.5 2.4 %memory_near_half.1 = (f32[512,256]{1,0:T(8,128)S(1)}, f32[512,16]{1,0:T(8,128)S(1)}) custom-call(s32[1]{0:T(128)} %bitcast.3.place_ref.refs_0_, bf16[512,896]{1,0:T(8,128)(2,1)S(1)} %copy-done.3, bf16[512,896]{1,0:T(8,128)(2,1)} %collective-permute-done.5.x1, bf16[3584,128]{1,0:T(8,128)(2,1)S(1)} %copy-done.1, bf16[3584,128]{1,0:T(8,128)(2,1)S(1)} %copy-done.2, ...), custom_call_target="tpu_custom_call" | custom-call | flops 704643072 | bytes 1835008 | tf_op jit(solution)/shard_map/memory_near_half/pallas_call | solution.py:588
  49.0 1.9 %memory_pairs.2.refs_10_ = bf16[2,272,128]{2,1,0:T(8,128)(2,1)S(1)} custom-call(s32[1]{0:T(128)} %bitcast.3.place_ref.refs_0_, s32[8]{0:T(128)S(1)} %reduce.refs_1_.refs_0_, bf16[256,896]{1,0:T(8,128)(2,1)} %collective-permute-done.dep_ref.refs_2_, bf16[256,896]{1,0:T(8,128)(2,1)} %collective-permute-done.6.refs_3_, ...), custom_call_target="tpu_custom_call" | custom-call | flops 352321536 | bytes 917504 | tf_op jit(solution)/shard_map/memory_pairs/pallas_call | solution.py:630
  50.9 2.8 %memory_pairs.3.dep_ref = bf16[8,272,128]{2,1,0:T(8,128)(2,1)} custom-call(s32[1]{0:T(128)} %bitcast.3.place_ref.refs_0_, s32[8]{0:T(128)S(1)} %reduce.refs_1_.refs_0_, bf16[256,896]{1,0:T(8,128)(2,1)} %in_order.3.refs_2_, bf16[256,896]{1,0:T(8,128)(2,1)} %collective-permute-done.4.refs_3_, f32[512,256]{1,0:T(8,128)S(1)} %get-tuple-element.31.refs_4_, ...), custom_call_target="tpu_custom_call" | custom-call | flops 352321536 | bytes 917504 | tf_op jit(solution)/shard_map/memory_pairs/pallas_call | solution.py:630
  53.7 4.5 %all-to-all-start.1 = ((bf16[8,272,128]{2,1,0:T(8,128)(2,1)}), bf16[8,272,128]{2,1,0:T(8,128)(2,1)}, u32[]{:S(2)}, u32[]{:S(2)}) async-start(bf16[8,272,128]{2,1,0:T(8,128)(2,1)} %memory_pairs.3.dep_ref), calls=%async_computation.1 | async-start | bytes 1114112 | tf_op jit(solution)/shard_map/all_to_all | solution.py:640
  58.3 0.1 collective-permute-start.9
  58.4 0.5 collective-permute-start.7
  58.9 1.8 %convolution_convert_fusion.refs_14_ = bf16[896,512]{1,0:T(8,128)(2,1)} fusion(bf16[896,8]{0,1:T(8,128)(2,1)S(1)} %copy-done.19, f32[512,8]{0,1:T(8,128)S(1)} %copy-done), kind=kOutput, calls=%fused_computation | convolution fusion | flops 44498944 | bytes 948224 | tf_op jit(solution)/shard_map/dot_general | solution.py:583
  60.7 1.9 %convolution_convert_fusion.1.refs_13_ = bf16[512,896]{1,0:T(8,128)(2,1)} fusion(f32[512,8]{0,1:T(8,128)S(1)} %copy-done, bf16[896,8]{0,1:T(8,128)(2,1)S(1)} %copy-done.19), kind=kOutput, calls=%fused_computation.1 | convolution fusion | flops 44498944 | bytes 948224 | tf_op jit(solution)/shard_map/dot_general | solution.py:586
  62.6 5.5 %project_far_half.3 = (bf16[256,896]{1,0:T(8,128)(2,1)S(1)}, bf16[256,128]{1,0:T(8,128)(2,1)S(1)}, bf16[256,128]{1,0:T(8,128)(2,1)S(1)}, bf16[32,256]{1,0:T(8,128)(2,1)S(1)}) custom-call(s32[1]{0:T(128)} %bitcast.3.place_ref.refs_0_, bf16[256,896]{1,0:T(8,128)(2,1)} %in_order.5.refs_1_, bf16[256,896]{1,0:T(8,128)(2,1)} %collective-permute-done.9.refs_2_, ...), custom_call_target="tpu_custom_call" | custom-call | flops 1174405120 | bytes 5505024 | tf_op jit(solution)/shard_map/project_far_half/pallas_call | solution.py:646
  68.1 0.8 copy-done.20
  68.9 5.3 %project_far_half.2 = (bf16[256,896]{1,0:T(8,128)(2,1)S(1)}, bf16[256,128]{1,0:T(8,128)(2,1)S(1)}, bf16[256,128]{1,0:T(8,128)(2,1)S(1)}, bf16[32,256]{1,0:T(8,128)(2,1)S(1)}) custom-call(s32[1]{0:T(128)} %bitcast.3.place_ref.refs_0_, bf16[256,896]{1,0:T(8,128)(2,1)} %in_order.4.refs_1_, bf16[256,896]{1,0:T(8,128)(2,1)S(1)} %collective-permute-done.7.refs_2_, ...), custom_call_target="tpu_custom_call" | custom-call | flops 1174405120 | bytes 5505024 | tf_op jit(solution)/shard_map/project_far_half/pallas_call | solution.py:646
  74.2 0.8 copy-done.22
  75.0 0.6 copy-done.24
  75.6 1.2 copy-done.15
  76.8 1.2 copy-done.16
  78.0 1.0 copy-done.21
  79.0 1.0 copy-done.23
  80.0 0.8 copy-done.25
  80.9 22.3 %span_attention.1 = (f32[40,512]{1,0:T(8,128)S(1)}, f32[16,1024]{1,0:T(8,128)S(1)}, f32[8,16,128]{2,1,0:T(8,128)}) custom-call(s32[4]{0:T(128)S(1)} %copy-done.26, bf16[256,896]{1,0:T(8,128)(2,1)S(1)} %copy-done.23, bf16[256,128]{1,0:T(8,128)(2,1)S(1)} %get-tuple-element.36.refs_2_, bf16[256,128]{1,0:T(8,128)(2,1)S(1)} %copy-done.25, ...), custom_call_target="tpu_custom_call" | custom-call | flops 10569646080 | bytes 1835008 | tf_op jit(solution)/shard_map/span_attention/pallas_call | solution.py:663
  103.2 5.7 %all-to-all-start.2 = ((f32[8,16,128]{2,1,0:T(8,128)}), f32[8,16,128]{2,1,0:T(8,128)S(1)}, u32[]{:S(2)}, u32[]{:S(2)}) async-start(f32[8,16,128]{2,1,0:T(8,128)} %get-tuple-element.44), calls=%async_computation.2 | async-start | bytes 131072 | tf_op jit(solution)/shard_map/all_to_all | solution.py:691
  108.9 2.0 %collective-permute-start.10 = (f32[16,1024]{1,0:T(8,128)S(1)}, f32[16,1024]{1,0:T(8,128)S(1)}, u32[]{:S(2)}, u32[]{:S(2)}) collective-permute-start(f32[16,1024]{1,0:T(8,128)S(1)} %get-tuple-element.46), channel_id=1, source_target_pairs={{0,4},{4,0},{8,12},{12,8},{16,20},{20,16},{24,28},{28,24},{1,5},{5... | collective-permute-start | bytes 196616 | tf_op jit(solution)/shard_map/ppermute | solution.py:486
  110.9 2.6 %collective-permute-done.10 = f32[16,1024]{1,0:T(8,128)S(1)} collective-permute-done((f32[16,1024]{1,0:T(8,128)S(1)}, f32[16,1024]{1,0:T(8,128)S(1)}, u32[]{:S(2)}, u32[]{:S(2)}) %collective-permute-start.10) | collective-permute-done | bytes 65568 | tf_op jit(solution)/shard_map/ppermute | solution.py:486
  113.6 2.2 %all-to-all-done.2.refs_1_ = f32[8,16,128]{2,1,0:T(8,128)S(1)} async-done(((f32[8,16,128]{2,1,0:T(8,128)}), f32[8,16,128]{2,1,0:T(8,128)S(1)}, u32[]{:S(2)}, u32[]{:S(2)}) %all-to-all-start.2) | async-done | bytes 65568 | tf_op jit(solution)/shard_map/all_to_all | solution.py:691
  115.8 0.6 owned_cotangent.1.c0
  116.4 0.1 collective-permute-start.11
  116.5 1.6 %collective-permute-start.12 = (f32[56,512]{1,0:T(8,128)S(1)}, f32[56,512]{1,0:T(8,128)S(1)}, u32[]{:S(2)}, u32[]{:S(2)}) collective-permute-start(f32[56,512]{1,0:T(8,128)S(1)} %owned_cotangent.1.c0), channel_id=1, source_target_pairs={{0,2},{1,3},{2,0},{3,1},{4,6},{5,7},{6,4},{7,5},{8,10},{9,11},{10,... | collective-permute-start | bytes 344072 | tf_op jit(solution)/shard_map/ppermute | solution.py:486
  118.1 0.3 collective-permute-start.13
  118.3 0.2 collective-permute-start.14
  118.5 4.1 %collective-permute-done.14 = f32[16,1024]{1,0:T(8,128)S(1)} collective-permute-done((f32[16,1024]{1,0:T(8,128)S(1)}, f32[16,1024]{1,0:T(8,128)S(1)}, u32[]{:S(2)}, u32[]{:S(2)}) %collective-permute-start.14) | collective-permute-done | bytes 65568 | tf_op jit(solution)/shard_map/ppermute | solution.py:486
  122.7 1.3 collective-permute-done.13.c3
  124.0 0.8 down_gradients.1
  124.8 0.4 collective-permute-start.15
  125.2 4.9 %collective-permute-done.15 = f32[32,896]{1,0:T(8,128)S(1)} collective-permute-done((f32[32,896]{1,0:T(8,128)S(1)}, f32[32,896]{1,0:T(8,128)S(1)}, u32[]{:S(2)}, u32[]{:S(2)}) %collective-permute-start.15) | collective-permute-done | bytes 114720 | tf_op jit(solution)/shard_map/ppermute | solution.py:486
  130.2 0.3 collective-permute-start.16
  130.5 4.6 %collective-permute-done.16 = f32[32,896]{1,0:T(8,128)S(1)} collective-permute-done((f32[32,896]{1,0:T(8,128)S(1)}, f32[32,896]{1,0:T(8,128)S(1)}, u32[]{:S(2)}, u32[]{:S(2)}) %collective-permute-start.16) | collective-permute-done | bytes 114720 | tf_op jit(solution)/shard_map/ppermute | solution.py:486
  135.1 0.5 collective-permute-start.17
  135.6 2.5 %collective-permute-start.18 = (f32[16,1024]{1,0:T(8,128)S(1)}, f32[16,1024]{1,0:T(8,128)S(1)}, u32[]{:S(2)}, u32[]{:S(2)}) collective-permute-start(f32[16,1024]{1,0:T(8,128)S(1)} %add.21.dep_ref.u0), channel_id=1, source_target_pairs={{0,16},{4,20},{8,24},{12,28},{16,0},{20,4},{24,8},{28,12},{1,17},{... | collective-permute-start | bytes 196616 | tf_op jit(solution)/shard_map/ppermute | solution.py:486
  138.1 6.3 %collective-permute-done.18.u1 = f32[16,1024]{1,0:T(8,128)S(1)} collective-permute-done((f32[16,1024]{1,0:T(8,128)S(1)}, f32[16,1024]{1,0:T(8,128)S(1)}, u32[]{:S(2)}, u32[]{:S(2)}) %collective-permute-start.18) | collective-permute-done | bytes 65568 | tf_op jit(solution)/shard_map/ppermute | solution.py:486
  144.4 0.7 finish_outputs.1
  (59 shorter events, 0.2 us)
Async XLA Ops:
  0.6 58.2 %copy-start = (f32[512,8]{0,1:T(8,128)S(1)}, f32[512,8]{0,1:T(8,128)}, u32[]{:S(2)}) copy-start(f32[512,8]{0,1:T(8,128)} %param.25) | copy-start | bytes 49156
  0.6 16.7 %copy-start.1 = (bf16[3584,128]{1,0:T(8,128)(2,1)S(1)}, bf16[3584,128]{1,0:T(8,128)(2,1)}, u32[]{:S(2)}) copy-start(bf16[3584,128]{1,0:T(8,128)(2,1)} %refs_4_.5) | copy-start | bytes 2752516
  0.7 16.7 %copy-start.2 = (bf16[3584,128]{1,0:T(8,128)(2,1)S(1)}, bf16[3584,128]{1,0:T(8,128)(2,1)}, u32[]{:S(2)}) copy-start(bf16[3584,128]{1,0:T(8,128)(2,1)} %refs_5_.3) | copy-start | bytes 2752516
  0.7 16.7 %collective-permute-start.3 = (bf16[512,896]{1,0:T(8,128)(2,1)}, bf16[512,896]{1,0:T(8,128)(2,1)S(1)}, u32[]{:S(2)}, u32[]{:S(2)}) collective-permute-start(bf16[512,896]{1,0:T(8,128)(2,1)} %slab_ref.1), channel_id=1, source_target_pairs={{0,1},{1,0},{2,3},{3,2},{4,5},{5,4},{6,7},{7,6},{8,9},{9,8},{10,11... | collective-permute-start | bytes 2752520 | tf_op jit(solution)/shard_map/ppermute | solution.py:486
  3.2 14.1 %collective-permute-start = (bf16[256,896]{1,0:T(8,128)(2,1)S(1)}, bf16[256,896]{1,0:T(8,128)(2,1)}, u32[]{:S(2)}, u32[]{:S(2)}) collective-permute-start(bf16[256,896]{1,0:T(8,128)(2,1)S(1)} %get-tuple-element.56), channel_id=1, source_target_pairs={{0,2},{1,3},{2,0},{3,1},{4,6},{5,7},{6,4},{7,5},{8,10},{9,11},{10,... | collective-permute-start | bytes 1376264 | tf_op jit(solution)/shard_map/ppermute | solution.py:486
  5.9 22.1 %collective-permute-start.2 = (bf16[256,896]{1,0:T(8,128)(2,1)}, bf16[256,896]{1,0:T(8,128)(2,1)}, u32[]{:S(2)}, u32[]{:S(2)}) collective-permute-start(bf16[256,896]{1,0:T(8,128)(2,1)} %get-tuple-element.55), channel_id=1, source_target_pairs={{0,2},{1,3},{2,0},{3,1},{4,6},{5,7},{6,4},{7,5},{8,10},{9,11},{10,... | collective-permute-start | bytes 1376264 | tf_op jit(solution)/shard_map/ppermute | solution.py:486
  5.9 40.6 %collective-permute-start.5 = (bf16[512,896]{1,0:T(8,128)(2,1)}, bf16[512,896]{1,0:T(8,128)(2,1)}, u32[]{:S(2)}, u32[]{:S(2)}) collective-permute-start(bf16[512,896]{1,0:T(8,128)(2,1)} %memory_ref.1), channel_id=1, source_target_pairs={{0,1},{1,0},{2,3},{3,2},{4,5},{5,4},{6,7},{7,6},{8,9},{9,8},{10,11... | collective-permute-start | bytes 2752520 | tf_op jit(solution)/shard_map/ppermute | solution.py:486
  17.3 31.6 %collective-permute-start.6 = (bf16[256,896]{1,0:T(8,128)(2,1)}, bf16[256,896]{1,0:T(8,128)(2,1)}, u32[]{:S(2)}, u32[]{:S(2)}) collective-permute-start(bf16[256,896]{1,0:T(8,128)(2,1)} %collective-permute-done.dep_ref.refs_2_), channel_id=1, source_target_pairs={{0,1},{1,0},{2,3},{3,2},{4,5},{5,4},{6,7},{7,6},{8,9},{9,8},{10,11... | collective-permute-start | bytes 1376264 | tf_op jit(solution)/shard_map/ppermute | solution.py:486
  17.4 1.2 copy-start.4
  18.5 0.9 copy-start.9
  19.4 0.9 copy-start.13
  26.5 0.7 copy-start.7
  27.2 0.8 copy-start.11
  28.0 18.5 %copy-start.3 = (bf16[512,896]{1,0:T(8,128)(2,1)S(1)}, bf16[512,896]{1,0:T(8,128)(2,1)}, u32[]{:S(2)}) copy-start(bf16[512,896]{1,0:T(8,128)(2,1)} %memory_ref.1) | copy-start | bytes 2752516
  28.0 18.5 %copy-start.10 = (bf16[16,3584]{1,0:T(8,128)(2,1)S(1)}, bf16[16,3584]{1,0:T(8,128)(2,1)}, u32[]{:S(2)}) copy-start(bf16[16,3584]{1,0:T(8,128)(2,1)} %refs_7_.7) | copy-start | bytes 344068
  28.0 22.9 %collective-permute-start.4 = (bf16[256,896]{1,0:T(8,128)(2,1)}, bf16[256,896]{1,0:T(8,128)(2,1)}, u32[]{:S(2)}, u32[]{:S(2)}) collective-permute-start(bf16[256,896]{1,0:T(8,128)(2,1)} %in_order.3.refs_2_), channel_id=1, source_target_pairs={{0,1},{1,0},{2,3},{3,2},{4,5},{5,4},{6,7},{7,6},{8,9},{9,8},{10,11... | collective-permute-start | bytes 1376264 | tf_op jit(solution)/shard_map/ppermute | solution.py:486
  29.3 1.2 copy-start.5
  31.5 26.7 %collective-permute-start.8 = (bf16[256,896]{1,0:T(8,128)(2,1)}, bf16[256,896]{1,0:T(8,128)(2,1)}, u32[]{:S(2)}, u32[]{:S(2)}) collective-permute-start(bf16[256,896]{1,0:T(8,128)(2,1)} %get-tuple-element.39), channel_id=1, source_target_pairs={{0,2},{1,3},{2,0},{3,1},{4,6},{5,7},{6,4},{7,5},{8,10},{9,11},{10,... | collective-permute-start | bytes 1376264 | tf_op jit(solution)/shard_map/ppermute | solution.py:486
  33.5 24.8 %collective-permute-start.1 = (bf16[256,896]{1,0:T(8,128)(2,1)}, bf16[256,896]{1,0:T(8,128)(2,1)}, u32[]{:S(2)}, u32[]{:S(2)}) collective-permute-start(bf16[256,896]{1,0:T(8,128)(2,1)} %get-tuple-element.29), channel_id=1, source_target_pairs={{0,2},{1,3},{2,0},{3,1},{4,6},{5,7},{6,4},{7,5},{8,10},{9,11},{10,... | collective-permute-start | bytes 1376264 | tf_op jit(solution)/shard_map/ppermute | solution.py:486
  46.5 2.5 %copy-start.8 = (f32[512,32]{1,0:T(8,128)S(1)}, f32[512,32]{1,0:T(8,128)}, u32[]{:S(2)}) copy-start(f32[512,32]{1,0:T(8,128)} %copy-done.7) | copy-start | bytes 196612
  46.5 2.5 %copy-start.18 = (bf16[16,128]{1,0:T(8,128)(2,1)S(1)}, bf16[16,128]{1,0:T(8,128)(2,1)}, u32[]{:S(2)}) copy-start(bf16[16,128]{1,0:T(8,128)(2,1)} %refs_11_.5) | copy-start | bytes 12292
  53.7 5.1 %copy-start.19 = (bf16[896,8]{0,1:T(8,128)(2,1)S(1)}, bf16[896,8]{0,1:T(8,128)(2,1)}, u32[]{:S(2)}) copy-start(bf16[896,8]{0,1:T(8,128)(2,1)} %param.22) | copy-start | bytes 43012
  53.7 21.9 %all-to-all-start.1 = ((bf16[8,272,128]{2,1,0:T(8,128)(2,1)}), bf16[8,272,128]{2,1,0:T(8,128)(2,1)}, u32[]{:S(2)}, u32[]{:S(2)}) async-start(bf16[8,272,128]{2,1,0:T(8,128)(2,1)} %memory_pairs.3.dep_ref), calls=%async_computation.1 | async-start | bytes 1114112 | tf_op jit(solution)/shard_map/all_to_all | solution.py:640
  58.2 4.4 %copy-start.14 = (bf16[16,3584]{1,0:T(8,128)(2,1)S(1)}, bf16[16,3584]{1,0:T(8,128)(2,1)}, u32[]{:S(2)}) copy-start(bf16[16,3584]{1,0:T(8,128)(2,1)} %refs_6_.7) | copy-start | bytes 344068
  58.2 4.3 %copy-start.17 = (bf16[16,896]{1,0:T(8,128)(2,1)S(1)}, bf16[16,896]{1,0:T(8,128)(2,1)}, u32[]{:S(2)}) copy-start(bf16[16,896]{1,0:T(8,128)(2,1)} %refs_10_.1) | copy-start | bytes 86020
  58.3 4.3 %collective-permute-start.9 = (bf16[256,896]{1,0:T(8,128)(2,1)}, bf16[256,896]{1,0:T(8,128)(2,1)}, u32[]{:S(2)}, u32[]{:S(2)}) collective-permute-start(bf16[256,896]{1,0:T(8,128)(2,1)} %in_order.5.refs_1_), channel_id=1, source_target_pairs={{0,1},{1,0},{2,3},{3,2},{4,5},{5,4},{6,7},{7,6},{8,9},{9,8},{10,11... | collective-permute-start | bytes 1376264 | tf_op jit(solution)/shard_map/ppermute | solution.py:486
  58.4 4.2 %copy-start.12 = (f32[512,256]{1,0:T(8,128)S(1)}, f32[512,256]{1,0:T(8,128)}, u32[]{:S(2)}) copy-start(f32[512,256]{1,0:T(8,128)} %copy-done.11) | copy-start | bytes 1572868
  58.4 10.5 %collective-permute-start.7 = (bf16[256,896]{1,0:T(8,128)(2,1)}, bf16[256,896]{1,0:T(8,128)(2,1)S(1)}, u32[]{:S(2)}, u32[]{:S(2)}) collective-permute-start(bf16[256,896]{1,0:T(8,128)(2,1)} %in_order.4.refs_1_), channel_id=1, source_target_pairs={{0,1},{1,0},{2,3},{3,2},{4,5},{5,4},{6,7},{7,6},{8,9},{9,8},{10,11... | collective-permute-start | bytes 1376264 | tf_op jit(solution)/shard_map/ppermute | solution.py:486
  68.1 0.8 copy-start.20
  68.9 6.7 %copy-start.26 = (s32[4]{0:T(128)S(1)}, s32[4]{0:T(128)}, u32[]{:S(2)}) copy-start(s32[4]{0:T(128)} %refs_0_.3) | copy-start | bytes 52
  74.2 0.8 copy-start.22
  75.0 0.6 copy-start.24
  75.6 1.2 copy-start.15
  76.8 1.2 copy-start.16
  78.0 1.0 copy-start.21
  79.0 1.0 copy-start.23
  80.0 0.8 copy-start.25
  80.9 43.2 %copy-start.6 = (bf16[512,896]{1,0:T(8,128)(2,1)S(1)}, bf16[512,896]{1,0:T(8,128)(2,1)}, u32[]{:S(2)}) copy-start(bf16[512,896]{1,0:T(8,128)(2,1)} %slab_ref.1) | copy-start | bytes 2752516
  103.2 12.6 %all-to-all-start.2 = ((f32[8,16,128]{2,1,0:T(8,128)}), f32[8,16,128]{2,1,0:T(8,128)S(1)}, u32[]{:S(2)}, u32[]{:S(2)}) async-start(f32[8,16,128]{2,1,0:T(8,128)} %get-tuple-element.44), calls=%async_computation.2 | async-start | bytes 131072 | tf_op jit(solution)/shard_map/all_to_all | solution.py:691
  108.9 4.6 %collective-permute-start.10 = (f32[16,1024]{1,0:T(8,128)S(1)}, f32[16,1024]{1,0:T(8,128)S(1)}, u32[]{:S(2)}, u32[]{:S(2)}) collective-permute-start(f32[16,1024]{1,0:T(8,128)S(1)} %get-tuple-element.46), channel_id=1, source_target_pairs={{0,4},{4,0},{8,12},{12,8},{16,20},{20,16},{24,28},{28,24},{1,5},{5... | collective-permute-start | bytes 196616 | tf_op jit(solution)/shard_map/ppermute | solution.py:486
  116.4 6.3 %collective-permute-start.11 = (f32[56,512]{1,0:T(8,128)S(1)}, f32[56,512]{1,0:T(8,128)S(1)}, u32[]{:S(2)}, u32[]{:S(2)}) collective-permute-start(f32[56,512]{1,0:T(8,128)S(1)} %owned_cotangent.1.c0), channel_id=1, source_target_pairs={{0,1},{1,0},{2,3},{3,2},{4,5},{5,4},{6,7},{7,6},{8,9},{9,8},{10,11... | collective-permute-start | bytes 344072 | tf_op jit(solution)/shard_map/ppermute | solution.py:486
  116.5 6.2 %collective-permute-start.12 = (f32[56,512]{1,0:T(8,128)S(1)}, f32[56,512]{1,0:T(8,128)S(1)}, u32[]{:S(2)}, u32[]{:S(2)}) collective-permute-start(f32[56,512]{1,0:T(8,128)S(1)} %owned_cotangent.1.c0), channel_id=1, source_target_pairs={{0,2},{1,3},{2,0},{3,1},{4,6},{5,7},{6,4},{7,5},{8,10},{9,11},{10,... | collective-permute-start | bytes 344072 | tf_op jit(solution)/shard_map/ppermute | solution.py:486
  118.1 6.0 %collective-permute-start.13 = (f32[56,512]{1,0:T(8,128)S(1)}, f32[56,512]{1,0:T(8,128)S(1)}, u32[]{:S(2)}, u32[]{:S(2)}) collective-permute-start(f32[56,512]{1,0:T(8,128)S(1)} %owned_cotangent.1.c0), channel_id=1, source_target_pairs={{0,3},{1,2},{2,1},{3,0},{4,7},{5,6},{6,5},{7,4},{8,11},{9,10},{10,... | collective-permute-start | bytes 344072 | tf_op jit(solution)/shard_map/ppermute | solution.py:486
  118.3 4.3 %collective-permute-start.14 = (f32[16,1024]{1,0:T(8,128)S(1)}, f32[16,1024]{1,0:T(8,128)S(1)}, u32[]{:S(2)}, u32[]{:S(2)}) collective-permute-start(f32[16,1024]{1,0:T(8,128)S(1)} %add.20.refs_3_), channel_id=1, source_target_pairs={{0,8},{4,12},{8,0},{12,4},{16,24},{20,28},{24,16},{28,20},{1,9},{5... | collective-permute-start | bytes 196616 | tf_op jit(solution)/shard_map/ppermute | solution.py:486
  124.8 5.3 %collective-permute-start.15 = (f32[32,896]{1,0:T(8,128)S(1)}, f32[32,896]{1,0:T(8,128)S(1)}, u32[]{:S(2)}, u32[]{:S(2)}) collective-permute-start(f32[32,896]{1,0:T(8,128)S(1)} %get-tuple-element.48), channel_id=1, source_target_pairs={{0,4},{4,0},{8,12},{12,8},{16,20},{20,16},{24,28},{28,24},{1,5},{5... | collective-permute-start | bytes 344072 | tf_op jit(solution)/shard_map/ppermute | solution.py:486
  130.2 4.9 %collective-permute-start.16 = (f32[32,896]{1,0:T(8,128)S(1)}, f32[32,896]{1,0:T(8,128)S(1)}, u32[]{:S(2)}, u32[]{:S(2)}) collective-permute-start(f32[32,896]{1,0:T(8,128)S(1)} %add.22), channel_id=1, source_target_pairs={{0,8},{4,12},{8,0},{12,4},{16,24},{20,28},{24,16},{28,20},{1,9},{5... | collective-permute-start | bytes 344072 | tf_op jit(solution)/shard_map/ppermute | solution.py:486
  135.1 9.3 %collective-permute-start.17 = (f32[32,896]{1,0:T(8,128)S(1)}, f32[32,896]{1,0:T(8,128)S(1)}, u32[]{:S(2)}, u32[]{:S(2)}) collective-permute-start(f32[32,896]{1,0:T(8,128)S(1)} %add.23.d0), channel_id=1, source_target_pairs={{0,16},{4,20},{8,24},{12,28},{16,0},{20,4},{24,8},{28,12},{1,17},{... | collective-permute-start | bytes 344072 | tf_op jit(solution)/shard_map/ppermute | solution.py:486
  135.6 8.8 %collective-permute-start.18 = (f32[16,1024]{1,0:T(8,128)S(1)}, f32[16,1024]{1,0:T(8,128)S(1)}, u32[]{:S(2)}, u32[]{:S(2)}) collective-permute-start(f32[16,1024]{1,0:T(8,128)S(1)} %add.21.dep_ref.u0), channel_id=1, source_target_pairs={{0,16},{4,20},{8,24},{12,28},{16,0},{20,4},{24,8},{28,12},{1,17},{... | collective-permute-start | bytes 196616 | tf_op jit(solution)/shard_map/ppermute | solution.py:486
